TPU v7x, 32 devices: a whole 2x2x4 slice. The times are simulated.
32 devices in a mesh: expert: 16 (over z, y, x), dp: 2 (over core).
Axes of the slice: x: 2, y: 2, z: 4, core: 2. Of those that a mesh axis runs over, the one named last changes fastest.
Arguments:
- tokens: bfloat16 [4096, 2048], P(('dp', 'expert')), parts along dimension 0, may hold values from -6 to 6
- route_ids: int32 [4096, 8], P(('dp', 'expert')), parts along dimension 0, may hold values from 0 to 15, all different within a row; in each aligned block of 128 rows (0 to 127, 128 to 255, ...) at most 80 rows name the same one
- route_weights: float32 [4096, 8], P(('dp', 'expert')), parts along dimension 0, may hold values from 0.05 to 0.3
- w_gate: bfloat16 [16, 2048, 768], P(None, 'expert'), may hold values from -0.125 to 0.125
- w_up: bfloat16 [16, 2048, 768], P(None, 'expert'), may hold values from -0.125 to 0.125
- w_down: bfloat16 [16, 768, 2048], P(None, 'expert'), may hold values from -0.21875 to 0.21875
Outputs:
- moe_output: bfloat16 [4096, 2048], P(('dp', 'expert')), parts along dimension 0
There are 2 independent parts, one for each index of `dp`. A program takes and returns all parts, laid end to end along the dimension named above; an argument that names none is the same for every part. Nothing has to cross between parts.
Inputs may be any that keep to these rules, and one draw needn't show every extreme that they name: `route_ids`: each token names 8 different experts. Within each aligned block of 128 tokens no expert is named by more than 80 routes, and in some block some expert is named by exactly 80 routes.
All inputs are finite; a program needn't handle non-finite values.
Results may differ from a plain program's by a relative error of at most 0.0057.
Values may be sent and summed in bfloat16 or wider, within the bound.
No kernel may reach another device: no remote copies, remote signals or barrier semaphores. Data moves between devices by JAX's collectives and lax.ppermute only.
A program may use at most 128 MiB of HBM per device.

v0:
```python
import jax
import jax.numpy as jnp
from jax import lax
from jax.sharding import PartitionSpec as P


def apply_expert(received, gates, uppers, downs):
    gate_proj = jnp.einsum("necd,edf->necf", received, gates, preferred_element_type=jnp.float32)
    up_proj = jnp.einsum("necd,edf->necf", received, uppers, preferred_element_type=jnp.float32)
    hidden = (jax.nn.silu(gate_proj) * up_proj).astype(jnp.bfloat16)
    return jnp.einsum("necf,efd->necd", hidden, downs, preferred_element_type=jnp.float32).astype(
        jnp.bfloat16
    )


def local(tokens, route_ids, route_weights, w_gate, w_up, w_down):
    devices = lax.axis_size("expert")
    experts = w_gate.shape[0]
    local_experts = experts // devices
    tok_rows = tokens.shape[0]
    model_width = tokens.shape[1]
    top_count = route_ids.shape[1]
    capacity = min(tok_rows, 5 * tok_rows * top_count // (4 * experts))
    route_flat = route_ids.reshape(-1)
    one_hot = (route_flat[:, None] == jnp.arange(experts, dtype=jnp.int32)[None, :]).astype(
        jnp.int32
    )
    earlier = jnp.cumsum(one_hot, axis=0) - one_hot
    position = jnp.sum(earlier * one_hot, axis=1)
    slots = (route_flat * capacity + position).reshape(tok_rows, top_count)
    slot_index = jnp.arange(experts * capacity, dtype=jnp.int32)
    matches = slots[:, :, None] == slot_index[None, None, :]
    dispatch_mask = jnp.any(matches, axis=1).astype(jnp.bfloat16)
    outgoing = lax.dot_general(
        dispatch_mask, tokens, (((0,), (0,)), ((), ())), preferred_element_type=jnp.float32
    )
    outgoing = outgoing.astype(jnp.bfloat16).reshape(experts, capacity, model_width)
    gates, uppers, downs = (
        lax.all_to_all(w_gate, "expert", split_axis=0, concat_axis=1, tiled=True),
        lax.all_to_all(w_up, "expert", split_axis=0, concat_axis=1, tiled=True),
        lax.all_to_all(w_down, "expert", split_axis=0, concat_axis=1, tiled=True),
    )
    received = lax.all_to_all(outgoing, "expert", split_axis=0, concat_axis=0, tiled=True)
    results = apply_expert(
        received.reshape(devices, local_experts, capacity, model_width), gates, uppers, downs
    )
    returned = lax.all_to_all(
        results.reshape(experts, capacity, model_width),
        "expert",
        split_axis=0,
        concat_axis=0,
        tiled=True,
    )
    returned_rows = returned.reshape(experts * capacity, model_width)
    picked = returned_rows[slots]
    combined = jnp.sum(route_weights[:, :, None] * picked.astype(jnp.float32), axis=1)
    return combined.astype(jnp.bfloat16)


def solution(mesh):
    placed = (
        P(("dp", "expert"), None),
        P(("dp", "expert"), None),
        P(("dp", "expert"), None),
        P(None, "expert", None),
        P(None, "expert", None),
        P(None, "expert", None),
    )
    return jax.shard_map(
        local, mesh=mesh, in_specs=placed, out_specs=P(("dp", "expert"), None), check_vma=False
    )
```

profile of v0, /device:TPU:12, one launch (start us, length us, event | category | flops | bytes accessed | tf_op | source)
XLA Modules:
  0.0 503.2 jit_solution(7583653174146825391)
XLA Ops:
  0.0 0.0 copy-start
  0.0 77.5 %all_to_all.37 = bf16[16,128,768]{2,1,0:T(8,128)(2,1)} all-to-all(bf16[16,128,768]{2,1,0:T(8,128)(2,1)} %param.10), channel_id=1, replica_groups=mesh['expert'=16,'dp'=2] {'expert'}, dimensions={0} | all-to-all | bytes 6291456 | tf_op jit(solution)/shard_map/all_to_all | solution.py:40
  77.5 0.0 copy-start.1
  77.5 5.7 %all-to-all-start.3 = ((bf16[16,48,2048]{2,1,0:T(8,128)(2,1)}), bf16[16,48,2048]{2,1,0:T(8,128)(2,1)}, u32[]{:S(2)}, u32[]{:S(2)}) async-start(bf16[16,48,2048]{2,1,0:T(8,128)(2,1)} %param.11), calls=%async_computation.3 | async-start | bytes 6291456 | tf_op jit(solution)/shard_map/all_to_all | solution.py:41
  83.2 0.0 copy-done.1
  83.2 0.1 copy.26
  83.3 0.1 eq.42
  83.4 0.1 eq.38
  83.5 4.5 reduce-window.6
  88.0 0.1 slice.10
  88.1 0.1 copy.28
  88.3 0.1 copy.29
  88.3 0.1 broadcast_add_fusion
  88.5 0.1 reduce_sum.21
  88.6 0.1 copy.31
  88.7 1.6 fusion.1
  90.4 0.0 copy-done
  90.4 3.8 convolution_convert_fusion
  94.2 58.5 %all-to-all-done.3 = bf16[16,48,2048]{2,1,0:T(8,128)(2,1)} async-done(((bf16[16,48,2048]{2,1,0:T(8,128)(2,1)}), bf16[16,48,2048]{2,1,0:T(8,128)(2,1)}, u32[]{:S(2)}, u32[]{:S(2)}) %all-to-all-start.3) | async-done | bytes 3145760 | tf_op jit(solution)/shard_map/all_to_all | solution.py:41
  152.7 119.5 %all_to_all.38 = bf16[16,80,2048]{2,1,0:T(8,128)(2,1)} all-to-all(bf16[16,80,2048]{2,1,0:T(8,128)(2,1)} %bitcast.75), channel_id=1, replica_groups=mesh['expert'=16,'dp'=2] {'expert'}, dimensions={0} | all-to-all | bytes 10485760 | tf_op jit(solution)/shard_map/all_to_all | solution.py:43
  272.2 5.6 %all-to-all-start.1 = ((bf16[16,128,768]{2,1,0:T(8,128)(2,1)}), bf16[16,128,768]{2,1,0:T(8,128)(2,1)}, u32[]{:S(2)}, u32[]{:S(2)}) async-start(bf16[16,128,768]{2,1,0:T(8,128)(2,1)} %param.9), calls=%async_computation.1 | async-start | bytes 6291456 | tf_op jit(solution)/shard_map/all_to_all | solution.py:39
  277.8 9.6 %fusion.12 = f32[16,80,768]{2,1,0:T(8,128)} fusion(bf16[16,80,2048]{2,1,0:T(8,128)(2,1)} %all_to_all.38, bf16[2048,768,1]{1,0,2:T(8,128)(2,1)} %bitcast.76), kind=kOutput, calls=%fused_computation.27 | convolution fusion | flops 4026531840 | bytes 12320768 | tf_op jit(solution)/shard_map/necd,edf->necf/dot_general | solution.py:9
  287.3 60.0 %all-to-all-done.1 = bf16[16,128,768]{2,1,0:T(8,128)(2,1)} async-done(((bf16[16,128,768]{2,1,0:T(8,128)(2,1)}), bf16[16,128,768]{2,1,0:T(8,128)(2,1)}, u32[]{:S(2)}, u32[]{:S(2)}) %all-to-all-start.1) | async-done | bytes 3145760 | tf_op jit(solution)/shard_map/all_to_all | solution.py:39
  347.3 15.6 %convolution_convert_fusion.1 = bf16[16,80,2048]{2,1,0:T(8,128)(2,1)} fusion(bf16[768,2048,1]{1,0,2:T(8,128)(2,1)} %bitcast.17, f32[16,80,768]{2,1,0:T(8,128)} %fusion.12, bf16[16,80,2048]{2,1,0:T(8,128)(2,1)} %all_to_all.38, bf16[2048,768,1]{1,0,2:T(8,128)(2,1)} %bitcast.4), kind=kOutput, calls=%fused_computation.6 | convolution fusion | flops 8061583360 | bytes 20709376 | tf_op jit(solution)/shard_map/necf,efd->necd/dot_general | solution.py:11
  362.9 5.1 %all-to-all-start.4 = ((bf16[16,80,2048]{2,1,0:T(8,128)(2,1)}), bf16[16,80,2048]{2,1,0:T(8,128)(2,1)}, u32[]{:S(2)}, u32[]{:S(2)}) async-start(bf16[16,80,2048]{2,1,0:T(8,128)(2,1)} %convolution_convert_fusion.1), calls=%async_computation.4 | async-start | bytes 10485760 | tf_op jit(solution)/shard_map/all_to_all | solution.py:47
  368.0 0.1 copy.32
  368.1 0.1 reshape.76
  368.2 0.0 copy-done.2
  368.2 0.1 copy.25
  368.4 115.5 %all-to-all-done.4 = bf16[16,80,2048]{2,1,0:T(8,128)(2,1)} async-done(((bf16[16,80,2048]{2,1,0:T(8,128)(2,1)}), bf16[16,80,2048]{2,1,0:T(8,128)(2,1)}, u32[]{:S(2)}, u32[]{:S(2)}) %all-to-all-start.4) | async-done | bytes 5242912 | tf_op jit(solution)/shard_map/all_to_all | solution.py:47
  483.8 12.0 %gather_fusion = bf16[1024,2048]{1,0:T(8,128)(2,1)} fusion(bf16[1280,2048]{1,0:T(8,128)(2,1)} %bitcast.18, s32[1024]{0:T(1024)S(1)} %broadcast_clamp_fusion), kind=kCustom, calls=%fused_computation | custom fusion | bytes 8392704 | tf_op jit(solution)/shard_map/gather | solution.py:55
  495.9 7.3 %fusion = bf16[128,2048]{1,0:T(8,128)(2,1)} fusion(bf16[1024,2048]{1,0:T(8,128)(2,1)} %gather_fusion, f32[128,8]{1,0:T(8,128)S(1)} %copy.25), kind=kLoop, calls=%fused_computation.2 | loop fusion | flops 6029312 | bytes 4722688 | tf_op jit(solution)/shard_map/reduce_sum | solution.py:56
  (8 shorter events, 0.1 us)
Async XLA Ops:
  0.0 90.4 %copy-start = (bf16[128,2048]{1,0:T(8,128)(2,1)S(1)}, bf16[128,2048]{1,0:T(8,128)(2,1)}, u32[]{:S(2)}) copy-start(bf16[128,2048]{1,0:T(8,128)(2,1)} %param.6) | copy-start | bytes 1572868
  77.5 5.7 %copy-start.1 = (s32[128,8]{0,1:T(8,128)S(1)}, s32[128,8]{0,1:T(8,128)}, u32[]{:S(2)}) copy-start(s32[128,8]{0,1:T(8,128)} %param.7) | copy-start | bytes 12292
  77.5 75.2 %all-to-all-start.3 = ((bf16[16,48,2048]{2,1,0:T(8,128)(2,1)}), bf16[16,48,2048]{2,1,0:T(8,128)(2,1)}, u32[]{:S(2)}, u32[]{:S(2)}) async-start(bf16[16,48,2048]{2,1,0:T(8,128)(2,1)} %param.11), calls=%async_computation.3 | async-start | bytes 6291456 | tf_op jit(solution)/shard_map/all_to_all | solution.py:41
  272.2 75.1 %all-to-all-start.1 = ((bf16[16,128,768]{2,1,0:T(8,128)(2,1)}), bf16[16,128,768]{2,1,0:T(8,128)(2,1)}, u32[]{:S(2)}, u32[]{:S(2)}) async-start(bf16[16,128,768]{2,1,0:T(8,128)(2,1)} %param.9), calls=%async_computation.1 | async-start | bytes 6291456 | tf_op jit(solution)/shard_map/all_to_all | solution.py:39
  362.9 5.3 %copy-start.2 = (f32[128,8]{0,1:T(8,128)S(1)}, f32[128,8]{0,1:T(8,128)}, u32[]{:S(2)}) copy-start(f32[128,8]{0,1:T(8,128)} %param.8) | copy-start | bytes 12292
  362.9 120.9 %all-to-all-start.4 = ((bf16[16,80,2048]{2,1,0:T(8,128)(2,1)}), bf16[16,80,2048]{2,1,0:T(8,128)(2,1)}, u32[]{:S(2)}, u32[]{:S(2)}) async-start(bf16[16,80,2048]{2,1,0:T(8,128)(2,1)} %convolution_convert_fusion.1), calls=%async_computation.4 | async-start | bytes 10485760 | tf_op jit(solution)/shard_map/all_to_all | solution.py:47
where the time goes:
time: 504 us; the launch traced here: 503 us
  waiting for transfers between devices  234 us (46%)
  blocking collectives  197 us (39%)
  matrix products  29 us (6%)
  starting transfers between devices  16.4 us (3%)
  other arithmetic  13.7 us (3%)
  local copies, waits for them, and re-layouts  13.2 us (3%)
    all_to_all x1, blocking collectives, local(): lax.all_to_all(outgoing, 'expert', split_axis=0, concat_axis=0, tiled=True)  119 us
    all_to_all x1, waiting for transfers between devices, local(): lax.all_to_all(results.reshape(experts, capacity, model_width), 'expert',...  115 us
    all_to_all x1, blocking collectives, local(): lax.all_to_all(w_up, 'expert', split_axis=0, concat_axis=1, tiled=True)  77.5 us
    all_to_all x1, waiting for transfers between devices, local(): lax.all_to_all(w_gate, 'expert', split_axis=0, concat_axis=1, tiled=True)  60 us
    all_to_all x1, waiting for transfers between devices, local(): lax.all_to_all(w_down, 'expert', split_axis=0, concat_axis=1, tiled=True)  58.5 us
    dot_general x1, matrix products, apply_expert(): jnp.einsum('necf,efd->necd', hidden, downs, preferred_element_type=jnp.fl...  15.6 us
    gather x1, local copies, waits for them, and re-layouts, local(): picked = returned_rows[slots]  12 us
  transfers between devices with their start and end apart: 3, of which 3 were waited for; matrix products, arithmetic and copies ran while one was open for 4% of the time, Pallas kernels for 0%

commit v1 on v0

v1 whole, which is shorter than its diff:
```python
import jax
import jax.numpy as jnp
from jax import lax
from jax.sharding import PartitionSpec as P


def swap_cores(x):
    size = lax.axis_size("dp")
    return lax.ppermute(x, "dp", [(i, i ^ 1) for i in range(size)])


def flip(x, bit):
    size = lax.axis_size("expert")
    return lax.ppermute(x, "expert", [(i, i ^ bit) for i in range(size)])


def turn(x, by):
    size = lax.axis_size("expert")
    return lax.ppermute(x, "expert", [(i, (i + 4 * by) % size) for i in range(size)])


def local(tokens, route_ids, route_weights, w_gate, w_up, w_down):
    devices = lax.axis_size("expert")
    experts, depth, width = w_gate.shape
    rows, model = tokens.shape
    line = devices // 4
    me = lax.axis_index("expert")
    core = lax.axis_index("dp") % 2
    half, part = width // 2, model // 2

    def sliced(w, size):
        return lax.dynamic_slice_in_dim(w, core * size, size, axis=2)

    wide = jnp.concatenate([sliced(w_gate, half), sliced(w_up, half)], axis=2)
    wide = lax.all_to_all(wide, "expert", split_axis=0, concat_axis=0, tiled=True)
    wide = wide.reshape(devices * depth, width)
    wide_other = swap_cores(wide)
    down = lax.all_to_all(sliced(w_down, part), "expert", split_axis=0, concat_axis=0, tiled=True)
    down = down.reshape(width, part)
    down_other = swap_cores(down)

    share = jnp.sum(
        jnp.where(
            route_ids[None, :, :] == jnp.arange(experts, dtype=jnp.int32)[:, None, None],
            route_weights[None, :, :],
            0.0,
        ),
        axis=2,
    )
    shares = lax.all_gather(share, "expert", axis=0)
    mine = lax.dynamic_index_in_dim(shares, me, axis=1, keepdims=False)
    order = jnp.array(
        [[((me // 4 - s) % line) * 4 + ((me % 4) ^ q) for q in range(4)] for s in range(line)]
    )
    mine = mine[order.reshape(-1)].reshape(line, 4 * rows)

    held = [tokens]
    for _ in range(line - 1):
        held.append(turn(held[-1], 1))
    blocks = []
    for s in range(line):
        by_x, by_y = flip(held[s], 1), flip(held[s], 2)
        across = jnp.concatenate([flip(by_x[:, :part], 2), flip(by_y[:, part:], 1)], axis=1)
        blocks.append(jnp.concatenate([held[s], by_x, by_y, across], axis=0))

    def hidden_of(x, w):
        both = jnp.dot(x, w, preferred_element_type=jnp.float32)
        return (jax.nn.silu(both[:, :half]) * both[:, half:]).astype(jnp.bfloat16)

    arriving = None
    for s in reversed(range(line)):
        own, other = hidden_of(blocks[s], wide), hidden_of(blocks[s], wide_other)
        hidden = jnp.where(
            core == 0, jnp.concatenate([own, other], axis=1), jnp.concatenate([other, own], axis=1)
        )
        scale = mine[s][:, None]
        outs = [
            (jnp.dot(hidden, w, preferred_element_type=jnp.float32) * scale).astype(jnp.bfloat16)
            for w in (down, down_other)
        ]
        near, by_x, by_y, across = zip(*[[o[q * rows : (q + 1) * rows] for q in range(4)] for o in outs])
        f32 = jnp.float32
        x0 = (by_x[0].astype(f32) + flip(across[0], 2).astype(f32)).astype(jnp.bfloat16)
        y1 = (by_y[1].astype(f32) + flip(across[1], 1).astype(f32)).astype(jnp.bfloat16)
        from_x = flip(jnp.concatenate([x0, by_x[1]], axis=1), 1)
        from_y = flip(jnp.concatenate([by_y[0], y1], axis=1), 2)
        total = jnp.concatenate(near, axis=1).astype(f32) + from_x.astype(f32) + from_y.astype(f32)
        if arriving is not None:
            total = total + arriving.astype(f32)
        if s > 0:
            arriving = turn(total.astype(jnp.bfloat16), -1)
    left, right = total[:, :part], total[:, part:]
    result = jnp.where(
        core == 0, jnp.concatenate([left, right], axis=1), jnp.concatenate([right, left], axis=1)
    )
    return result.astype(jnp.bfloat16)


def solution(mesh):
    placed = (
        P(("dp", "expert"), None),
        P(("dp", "expert"), None),
        P(("dp", "expert"), None),
        P(None, "expert", None),
        P(None, "expert", None),
        P(None, "expert", None),
    )
    return jax.shard_map(
        local, mesh=mesh, in_specs=placed, out_specs=P(("dp", "expert"), None), check_vma=False
    )
```

time: 504 us -> 349 us (0.69)
  blocking collectives: 197 us -> 35.2 us
  waiting for transfers between devices: 234 us -> 183 us
  starting transfers between devices: 16.4 us -> 60.1 us
  matrix products: 29 us -> 43.3 us
  other arithmetic: 13.7 us -> 7.04 us
    all_to_all x3 -> x2, waiting for transfers between devices: 234 us -> 9.56 us  [the longest x1 9.56 us: local(): lax.all_to_all(wide, 'expert', split_axis=0, concat_axis=0, tiled=True)]
    all_to_all x2 -> x0, blocking collectives: 197 us -> none  [the longest x1 119 us: local(): lax.all_to_all(outgoing, 'expert', split_axis=0, concat_axis=0, tiled=True)]
    ppermute x0 -> x40, waiting for transfers between devices: none -> 174 us  [the longest x6 123 us: turn(): lax.ppermute(x, 'expert', [(i, (i + 4 * by) % size) for i in range(size)])]
    ppermute x0 -> x40, starting transfers between devices: none -> 47.6 us  [the longest x32 34.8 us: flip(): return lax.ppermute(x, 'expert', [(i, i ^ bit) for i in range(size)])]
    all_gather x0 -> x1, blocking collectives: none -> 35.2 us  [local(): shares = lax.all_gather(share, 'expert', axis=0)]
    dot_general x3 -> x16, matrix products: 29 us -> 43.3 us  [the longest x8 35.3 us: hidden_of(): both = jnp.dot(x, w, preferred_element_type=jnp.float32)]
    gather x1, local copies, waits for them, and re-layouts: 12 us -> 0.56 us  [local(): mine = mine[order.reshape(-1)].reshape(line, 4 * rows)]
    slice x2 -> x17, local copies, waits for them, and re-layouts: 0.21 us -> 8.66 us  [the longest x4 4.59 us: local(): by_x[:, :part]]
  transfers between devices with their start and end apart: 3 -> 42, of which waited for: 3 -> 16; matrix products, arithmetic and copies ran while one was open for 4% -> 16% of each run, Pallas kernels for 0% -> 0%
where the time goes in v1:
time: 349 us; the launch traced here: 345 us
  waiting for transfers between devices  183 us (52%)
  starting transfers between devices  60.1 us (17%)
  matrix products  43.3 us (12%)
  blocking collectives  35.2 us (10%)
  local copies, waits for them, and re-layouts  15.6 us (4%)
  other arithmetic  7.04 us (2%)
    ppermute x6, waiting for transfers between devices, turn(): lax.ppermute(x, 'expert', [(i, (i + 4 * by) % size) for i in range(size)])  123 us
    ppermute x32, waiting for transfers between devices, flip(): return lax.ppermute(x, 'expert', [(i, i ^ bit) for i in range(size)])  50.9 us
    dot_general x8, matrix products, hidden_of(): both = jnp.dot(x, w, preferred_element_type=jnp.float32)  35.3 us
    all_gather x1, blocking collectives, local(): shares = lax.all_gather(share, 'expert', axis=0)  35.2 us
    ppermute x32, starting transfers between devices, flip(): return lax.ppermute(x, 'expert', [(i, i ^ bit) for i in range(size)])  34.8 us
    ppermute x6, starting transfers between devices, turn(): lax.ppermute(x, 'expert', [(i, (i + 4 * by) % size) for i in range(size)])  12.7 us
    all_to_all x1, waiting for transfers between devices, local(): lax.all_to_all(wide, 'expert', split_axis=0, concat_axis=0, tiled=True)  9.56 us
    dot_general x8, matrix products, local(): jnp.dot(hidden, w, preferred_element_type=jnp.float32) * scale  8.05 us
  transfers between devices with their start and end apart: 42, of which 16 were waited for; matrix products, arithmetic and copies ran while one was open for 16% of the time, Pallas kernels for 0%

profile of v1, /device:TPU:12, one launch (start us, length us, event | category | flops | bytes accessed | tf_op | source)
XLA Modules:
  0.0 345.1 jit_solution(16193502639954714315)
XLA Ops:
  0.0 2.4 constant_dynamic-slice_fusion.2
  2.4 2.0 pad_maximum_fusion
  4.5 7.2 %all-to-all-start = ((bf16[16,128,768]{2,1,0:T(8,128)(2,1)}), bf16[16,128,768]{2,1,0:T(8,128)(2,1)}, u32[]{:S(2)}, u32[]{:S(2)}) async-start(bf16[16,128,768]{2,1,0:T(8,128)(2,1)} %pad_maximum_fusion), calls=%async_computation | async-start | bytes 6291456 | tf_op jit(solution)/shard_map/all_to_all | solution.py:35
  13.1 78.1 %collective-permute-done.10 = bf16[128,2048]{1,0:T(8,128)(2,1)} collective-permute-done((bf16[128,2048]{1,0:T(8,128)(2,1)}, bf16[128,2048]{1,0:T(8,128)(2,1)}, u32[]{:S(2)}, u32[]{:S(2)}) %collective-permute-start.10) | collective-permute-done | bytes 524320 | tf_op jit(solution)/shard_map/ppermute | solution.py:19
  91.2 2.5 collective-permute-start.19
  95.1 9.6 %all-to-all-done = bf16[16,128,768]{2,1,0:T(8,128)(2,1)} async-done(((bf16[16,128,768]{2,1,0:T(8,128)(2,1)}), bf16[16,128,768]{2,1,0:T(8,128)(2,1)}, u32[]{:S(2)}, u32[]{:S(2)}) %all-to-all-start) | async-done | bytes 3145760 | tf_op jit(solution)/shard_map/all_to_all | solution.py:35
  104.7 5.4 %all-to-all-start.1 = ((bf16[16,48,1024]{2,1,0:T(8,128)(2,1)}), bf16[16,48,1024]{2,1,0:T(8,128)(2,1)S(1)}, u32[]{:S(2)}, u32[]{:S(2)}) async-start(bf16[16,48,1024]{2,1,0:T(8,128)(2,1)} %constant_dynamic-slice_fusion.1), calls=%async_computation.1 | async-start | bytes 3145728 | tf_op jit(solution)/shard_map/all_to_all | solution.py:38
  113.6 40.7 %collective-permute-done.28 = bf16[128,2048]{1,0:T(8,128)(2,1)} collective-permute-done((bf16[128,2048]{1,0:T(8,128)(2,1)}, bf16[128,2048]{1,0:T(8,128)(2,1)}, u32[]{:S(2)}, u32[]{:S(2)}) %collective-permute-start.28) | collective-permute-done | bytes 524320 | tf_op jit(solution)/shard_map/ppermute | solution.py:19
  158.1 35.2 %all-gather = f32[256,128]{1,0:T(8,128)S(1)} all-gather(f32[16,128]{1,0:T(8,128)S(1)} %select_reduce_fusion), channel_id=2, replica_groups=mesh['expert'=16,'dp'=2] {'expert'}, dimensions={0}, use_global_device_ids=true | all-gather | bytes 139264 | tf_op jit(solution)/shard_map/all_gather | solution.py:50
  195.0 1.9 collective-permute-start.20
  203.7 4.8 %collective-permute-done.11 = bf16[128,2048]{1,0:T(8,128)(2,1)} collective-permute-done((bf16[128,2048]{1,0:T(8,128)(2,1)}, bf16[128,2048]{1,0:T(8,128)(2,1)}, u32[]{:S(2)}, u32[]{:S(2)}) %collective-permute-start.11) | collective-permute-done | bytes 524320 | tf_op jit(solution)/shard_map/ppermute | solution.py:14
  212.7 6.8 %collective-permute-done.20 = bf16[128,2048]{1,0:T(8,128)(2,1)} collective-permute-done((bf16[128,2048]{1,0:T(8,128)(2,1)}, bf16[128,2048]{1,0:T(8,128)(2,1)}, u32[]{:S(2)}, u32[]{:S(2)}) %collective-permute-start.20) | collective-permute-done | bytes 524320 | tf_op jit(solution)/shard_map/ppermute | solution.py:14
  222.2 1.8 collective-permute-start.22
  224.0 4.3 %fusion.19 = f32[512,768]{1,0:T(8,128)S(1)} fusion(bf16[2048,768]{1,0:T(8,128)(2,1)} %bitcast, bf16[128,1024]{1,0:T(8,128)(2,1)} %copy-done.7, bf16[128,1024]{1,0:T(8,128)(2,1)} %collective-permute-done.31, bf16[128,2048]{1,0:T(8,128)(2,1)} %collective-permute-done.30, bf16[128,2048]{1,0:T(8,128)(2,1)} %collective-permute-done.29, ...), kind=kOutput, calls=%fused_computation.83 | convolution fusion | flops 1621098496 | bytes 6815744 | tf_op jit(solution)/shard_map/dot_general | solution.py:67
  231.0 5.3 %fusion.21 = f32[512,768]{1,0:T(8,128)} fusion(bf16[2048,768]{1,0:T(8,128)(2,1)} %bitcast, bf16[128,1024]{1,0:T(8,128)(2,1)S(1)} %collective-permute-done.23, bf16[128,1024]{1,0:T(8,128)(2,1)S(1)} %collective-permute-done.22, bf16[128,2048]{1,0:T(8,128)(2,1)} %collective-permute-done.21, bf16[128,2048]{1,0:T(8,128)(2,1)} %collective-permute-done.20, ...), kind=kOutput, calls=%fused_computation.85 | convolution fusion | flops 1621098496 | bytes 6815744 | tf_op jit(solution)/shard_map/dot_general | solution.py:67
  238.6 4.3 %fusion.23 = f32[512,768]{1,0:T(8,128)S(1)} fusion(bf16[2048,768]{1,0:T(8,128)(2,1)} %bitcast, bf16[128,1024]{1,0:T(8,128)(2,1)} %collective-permute-done.14, bf16[128,1024]{1,0:T(8,128)(2,1)} %collective-permute-done.13, bf16[128,2048]{1,0:T(8,128)(2,1)} %collective-permute-done.12, bf16[128,2048]{1,0:T(8,128)(2,1)} %collective-permute-done.11, ...), kind=kOutput, calls=%fused_computation.87 | convolution fusion | flops 1621098496 | bytes 6815744 | tf_op jit(solution)/shard_map/dot_general | solution.py:67
  244.6 4.2 %fusion.25 = f32[512,768]{1,0:T(8,128)S(1)} fusion(bf16[2048,768]{1,0:T(8,128)(2,1)} %bitcast, bf16[128,1024]{1,0:T(8,128)(2,1)} %collective-permute-done.3, bf16[128,1024]{1,0:T(8,128)(2,1)} %collective-permute-done.2, bf16[128,2048]{1,0:T(8,128)(2,1)S(1)} %copy-done.4, bf16[128,2048]{1,0:T(8,128)(2,1)} %collective-permute-done, bf16[128,2048]{1,0:T(8,128)(2,1)} %param.6), kind=kOutput, calls=%fused_computation.89 | convolution fusion | flops 1621098496 | bytes 6815744 | tf_op jit(solution)/shard_map/dot_general | solution.py:67
  249.7 4.2 %fusion.18 = f32[512,768]{1,0:T(8,128)S(1)} fusion(bf16[2048,768]{1,0:T(8,128)(2,1)} %collective-permute-done.4, bf16[128,1024]{1,0:T(8,128)(2,1)S(1)} %copy-done.8, bf16[128,1024]{1,0:T(8,128)(2,1)} %collective-permute-done.31, bf16[128,2048]{1,0:T(8,128)(2,1)} %collective-permute-done.30, bf16[128,2048]{1,0:T(8,128)(2,1)} %collective-permute-done.29, ...), kind=kOutput, calls=%fused_computation.82 | convolution fusion | flops 1621098496 | bytes 6815744 | tf_op jit(solution)/shard_map/dot_general | solution.py:67
  257.8 4.4 %fusion.20 = f32[512,768]{1,0:T(8,128)S(1)} fusion(bf16[2048,768]{1,0:T(8,128)(2,1)} %collective-permute-done.4, bf16[128,1024]{1,0:T(8,128)(2,1)S(1)} %copy-done.10, bf16[128,1024]{1,0:T(8,128)(2,1)S(1)} %copy-done.12, bf16[128,2048]{1,0:T(8,128)(2,1)} %collective-permute-done.21, bf16[128,2048]{1,0:T(8,128)(2,1)} %collective-permute-done.20, ...), kind=kOutput, calls=%fused_computation.84 | convolution fusion | flops 1621098496 | bytes 6815744 | tf_op jit(solution)/shard_map/dot_general | solution.py:67
  267.4 4.3 %fusion.22 = f32[512,768]{1,0:T(8,128)S(1)} fusion(bf16[2048,768]{1,0:T(8,128)(2,1)} %collective-permute-done.4, bf16[128,1024]{1,0:T(8,128)(2,1)} %collective-permute-done.14, bf16[128,1024]{1,0:T(8,128)(2,1)} %collective-permute-done.13, bf16[128,2048]{1,0:T(8,128)(2,1)} %collective-permute-done.12, bf16[128,2048]{1,0:T(8,128)(2,1)} %collective-permute-done.11, ...), kind=kOutput, calls=%fused_computation.86 | convolution fusion | flops 1621098496 | bytes 6815744 | tf_op jit(solution)/shard_map/dot_general | solution.py:67
  274.9 4.2 %fusion.24 = f32[512,768]{1,0:T(8,128)S(1)} fusion(bf16[2048,768]{1,0:T(8,128)(2,1)} %collective-permute-done.4, bf16[128,1024]{1,0:T(8,128)(2,1)} %collective-permute-done.3, bf16[128,1024]{1,0:T(8,128)(2,1)} %collective-permute-done.2, bf16[128,2048]{1,0:T(8,128)(2,1)S(1)} %copy-done.4, bf16[128,2048]{1,0:T(8,128)(2,1)} %collective-permute-done, ...), kind=kOutput, calls=%fused_computation.88 | convolution fusion | flops 1621098496 | bytes 6815744 | tf_op jit(solution)/shard_map/dot_general | solution.py:67
  287.1 3.7 %collective-permute-done.15 = bf16[128,1024]{1,0:T(8,128)(2,1)S(1)} collective-permute-done((bf16[128,1024]{1,0:T(8,128)(2,1)S(1)}, bf16[128,1024]{1,0:T(8,128)(2,1)S(1)}, u32[]{:S(2)}, u32[]{:S(2)}) %collective-permute-start.15) | collective-permute-done | bytes 262176 | tf_op jit(solution)/shard_map/ppermute | solution.py:14
  291.5 10.5 %collective-permute-done.36 = bf16[128,2048]{1,0:T(8,128)(2,1)S(1)} collective-permute-done((bf16[128,2048]{1,0:T(8,128)(2,1)S(1)}, bf16[128,2048]{1,0:T(8,128)(2,1)S(1)}, u32[]{:S(2)}, u32[]{:S(2)}) %collective-permute-start.36) | collective-permute-done | bytes 524320 | tf_op jit(solution)/shard_map/ppermute | solution.py:14
  303.6 2.4 collective-permute-start.37
  306.9 12.0 %collective-permute-done.27 = bf16[128,2048]{1,0:T(8,128)(2,1)S(1)} collective-permute-done((bf16[128,2048]{1,0:T(8,128)(2,1)S(1)}, bf16[128,2048]{1,0:T(8,128)(2,1)S(1)}, u32[]{:S(2)}, u32[]{:S(2)}) %collective-permute-start.27) | collective-permute-done | bytes 524320 | tf_op jit(solution)/shard_map/ppermute | solution.py:14
  320.6 2.4 collective-permute-start.38
  323.8 1.7 collective-permute-start.7
  325.5 4.5 %collective-permute-done.18 = bf16[128,2048]{1,0:T(8,128)(2,1)S(1)} collective-permute-done((bf16[128,2048]{1,0:T(8,128)(2,1)S(1)}, bf16[128,2048]{1,0:T(8,128)(2,1)S(1)}, u32[]{:S(2)}, u32[]{:S(2)}) %collective-permute-start.18) | collective-permute-done | bytes 524320 | tf_op jit(solution)/shard_map/ppermute | solution.py:14
  330.1 3.3 collective-permute-done.16
  333.7 2.5 collective-permute-start.39
  336.3 2.5 collective-permute-done.9
  339.0 4.0 %collective-permute-done.39 = bf16[128,2048]{1,0:T(8,128)(2,1)S(1)} collective-permute-done((bf16[128,2048]{1,0:T(8,128)(2,1)S(1)}, bf16[128,2048]{1,0:T(8,128)(2,1)S(1)}, u32[]{:S(2)}, u32[]{:S(2)}) %collective-permute-start.39) | collective-permute-done | bytes 524320 | tf_op jit(solution)/shard_map/ppermute | solution.py:19
  (154 shorter events, 61.5 us)
Async XLA Ops:
  4.5 100.2 %all-to-all-start = ((bf16[16,128,768]{2,1,0:T(8,128)(2,1)}), bf16[16,128,768]{2,1,0:T(8,128)(2,1)}, u32[]{:S(2)}, u32[]{:S(2)}) async-start(bf16[16,128,768]{2,1,0:T(8,128)(2,1)} %pad_maximum_fusion), calls=%async_computation | async-start | bytes 6291456 | tf_op jit(solution)/shard_map/all_to_all | solution.py:35
  11.6 79.6 %collective-permute-start.10 = (bf16[128,2048]{1,0:T(8,128)(2,1)}, bf16[128,2048]{1,0:T(8,128)(2,1)}, u32[]{:S(2)}, u32[]{:S(2)}) collective-permute-start(bf16[128,2048]{1,0:T(8,128)(2,1)} %param.6), channel_id=1, source_target_pairs={{0,8},{2,10},{4,12},{6,14},{8,16},{10,18},{12,20},{14,22},{16,24},... | collective-permute-start | bytes 1572872 | tf_op jit(solution)/shard_map/ppermute | solution.py:19
  91.2 18.9 %collective-permute-start.19 = (bf16[128,2048]{1,0:T(8,128)(2,1)}, bf16[128,2048]{1,0:T(8,128)(2,1)}, u32[]{:S(2)}, u32[]{:S(2)}) collective-permute-start(bf16[128,2048]{1,0:T(8,128)(2,1)} %collective-permute-done.10), channel_id=1, source_target_pairs={{0,8},{2,10},{4,12},{6,14},{8,16},{10,18},{12,20},{14,22},{16,24},... | collective-permute-start | bytes 1572872 | tf_op jit(solution)/shard_map/ppermute | solution.py:19
  104.7 132.6 %all-to-all-start.1 = ((bf16[16,48,1024]{2,1,0:T(8,128)(2,1)}), bf16[16,48,1024]{2,1,0:T(8,128)(2,1)S(1)}, u32[]{:S(2)}, u32[]{:S(2)}) async-start(bf16[16,48,1024]{2,1,0:T(8,128)(2,1)} %constant_dynamic-slice_fusion.1), calls=%async_computation.1 | async-start | bytes 3145728 | tf_op jit(solution)/shard_map/all_to_all | solution.py:38
  110.1 44.2 %collective-permute-start.28 = (bf16[128,2048]{1,0:T(8,128)(2,1)}, bf16[128,2048]{1,0:T(8,128)(2,1)}, u32[]{:S(2)}, u32[]{:S(2)}) collective-permute-start(bf16[128,2048]{1,0:T(8,128)(2,1)} %collective-permute-done.19), channel_id=1, source_target_pairs={{0,8},{2,10},{4,12},{6,14},{8,16},{10,18},{12,20},{14,22},{16,24},... | collective-permute-start | bytes 1572872 | tf_op jit(solution)/shard_map/ppermute | solution.py:19
  111.6 81.7 %collective-permute-start.1 = (bf16[128,2048]{1,0:T(8,128)(2,1)}, bf16[128,2048]{1,0:T(8,128)(2,1)S(1)}, u32[]{:S(2)}, u32[]{:S(2)}) collective-permute-start(bf16[128,2048]{1,0:T(8,128)(2,1)} %param.6), channel_id=1, source_target_pairs={{0,4},{2,6},{4,0},{6,2},{8,12},{10,14},{12,8},{14,10},{16,20},{18,... | collective-permute-start | bytes 1572872 | tf_op jit(solution)/shard_map/ppermute | solution.py:14
  112.1 86.7 %collective-permute-start = (bf16[128,2048]{1,0:T(8,128)(2,1)}, bf16[128,2048]{1,0:T(8,128)(2,1)}, u32[]{:S(2)}, u32[]{:S(2)}) collective-permute-start(bf16[128,2048]{1,0:T(8,128)(2,1)} %param.6), channel_id=1, source_target_pairs={{0,2},{2,0},{4,6},{6,4},{8,10},{10,8},{12,14},{14,12},{16,18},{18,... | collective-permute-start | bytes 1572872 | tf_op jit(solution)/shard_map/ppermute | solution.py:14
  154.3 40.1 %collective-permute-start.30 = (bf16[128,2048]{1,0:T(8,128)(2,1)}, bf16[128,2048]{1,0:T(8,128)(2,1)}, u32[]{:S(2)}, u32[]{:S(2)}) collective-permute-start(bf16[128,2048]{1,0:T(8,128)(2,1)} %collective-permute-done.28), channel_id=1, source_target_pairs={{0,4},{2,6},{4,0},{6,2},{8,12},{10,14},{12,8},{14,10},{16,20},{18,... | collective-permute-start | bytes 1572872 | tf_op jit(solution)/shard_map/ppermute | solution.py:14
  154.9 40.1 %collective-permute-start.29 = (bf16[128,2048]{1,0:T(8,128)(2,1)}, bf16[128,2048]{1,0:T(8,128)(2,1)}, u32[]{:S(2)}, u32[]{:S(2)}) collective-permute-start(bf16[128,2048]{1,0:T(8,128)(2,1)} %collective-permute-done.28), channel_id=1, source_target_pairs={{0,2},{2,0},{4,6},{6,4},{8,10},{10,8},{12,14},{14,12},{16,18},{18,... | collective-permute-start | bytes 1572872 | tf_op jit(solution)/shard_map/ppermute | solution.py:14
  156.4 42.6 %collective-permute-start.12 = (bf16[128,2048]{1,0:T(8,128)(2,1)}, bf16[128,2048]{1,0:T(8,128)(2,1)}, u32[]{:S(2)}, u32[]{:S(2)}) collective-permute-start(bf16[128,2048]{1,0:T(8,128)(2,1)} %collective-permute-done.10), channel_id=1, source_target_pairs={{0,4},{2,6},{4,0},{6,2},{8,12},{10,14},{12,8},{14,10},{16,20},{18,... | collective-permute-start | bytes 1572872 | tf_op jit(solution)/shard_map/ppermute | solution.py:14
  193.3 15.2 %collective-permute-start.11 = (bf16[128,2048]{1,0:T(8,128)(2,1)}, bf16[128,2048]{1,0:T(8,128)(2,1)}, u32[]{:S(2)}, u32[]{:S(2)}) collective-permute-start(bf16[128,2048]{1,0:T(8,128)(2,1)} %collective-permute-done.10), channel_id=1, source_target_pairs={{0,2},{2,0},{4,6},{6,4},{8,10},{10,8},{12,14},{14,12},{16,18},{18,... | collective-permute-start | bytes 1572872 | tf_op jit(solution)/shard_map/ppermute | solution.py:14
  194.4 16.9 %collective-permute-start.21 = (bf16[128,2048]{1,0:T(8,128)(2,1)}, bf16[128,2048]{1,0:T(8,128)(2,1)}, u32[]{:S(2)}, u32[]{:S(2)}) collective-permute-start(bf16[128,2048]{1,0:T(8,128)(2,1)} %collective-permute-done.19), channel_id=1, source_target_pairs={{0,4},{2,6},{4,0},{6,2},{8,12},{10,14},{12,8},{14,10},{16,20},{18,... | collective-permute-start | bytes 1572872 | tf_op jit(solution)/shard_map/ppermute | solution.py:14
  195.0 24.5 %collective-permute-start.20 = (bf16[128,2048]{1,0:T(8,128)(2,1)}, bf16[128,2048]{1,0:T(8,128)(2,1)}, u32[]{:S(2)}, u32[]{:S(2)}) collective-permute-start(bf16[128,2048]{1,0:T(8,128)(2,1)} %collective-permute-done.19), channel_id=1, source_target_pairs={{0,2},{2,0},{4,6},{6,4},{8,10},{10,8},{12,14},{14,12},{16,18},{18,... | collective-permute-start | bytes 1572872 | tf_op jit(solution)/shard_map/ppermute | solution.py:14
  198.9 23.3 %collective-permute-start.32 = (bf16[128,1024]{1,0:T(8,128)(2,1)S(1)}, bf16[128,1024]{1,0:T(8,128)(2,1)S(1)}, u32[]{:S(2)}, u32[]{:S(2)}) collective-permute-start(bf16[128,1024]{1,0:T(8,128)(2,1)S(1)} %slice.301), channel_id=1, source_target_pairs={{0,2},{2,0},{4,6},{6,4},{8,10},{10,8},{12,14},{14,12},{16,18},{18,... | collective-permute-start | bytes 786440 | tf_op jit(solution)/shard_map/ppermute | solution.py:14
  199.0 25.0 %collective-permute-start.31 = (bf16[128,1024]{1,0:T(8,128)(2,1)S(1)}, bf16[128,1024]{1,0:T(8,128)(2,1)}, u32[]{:S(2)}, u32[]{:S(2)}) collective-permute-start(bf16[128,1024]{1,0:T(8,128)(2,1)S(1)} %slice.300), channel_id=1, source_target_pairs={{0,4},{2,6},{4,0},{6,2},{8,12},{10,14},{12,8},{14,10},{16,20},{18,... | collective-permute-start | bytes 786440 | tf_op jit(solution)/shard_map/ppermute | solution.py:14
  208.5 36.0 %collective-permute-start.3 = (bf16[128,1024]{1,0:T(8,128)(2,1)}, bf16[128,1024]{1,0:T(8,128)(2,1)}, u32[]{:S(2)}, u32[]{:S(2)}) collective-permute-start(bf16[128,1024]{1,0:T(8,128)(2,1)} %slice.256), channel_id=1, source_target_pairs={{0,2},{2,0},{4,6},{6,4},{8,10},{10,8},{12,14},{14,12},{16,18},{18,... | collective-permute-start | bytes 786440 | tf_op jit(solution)/shard_map/ppermute | solution.py:14
  211.3 33.3 %collective-permute-start.2 = (bf16[128,1024]{1,0:T(8,128)(2,1)S(1)}, bf16[128,1024]{1,0:T(8,128)(2,1)}, u32[]{:S(2)}, u32[]{:S(2)}) collective-permute-start(bf16[128,1024]{1,0:T(8,128)(2,1)S(1)} %slice.255), channel_id=1, source_target_pairs={{0,4},{2,6},{4,0},{6,2},{8,12},{10,14},{12,8},{14,10},{16,20},{18,... | collective-permute-start | bytes 786440 | tf_op jit(solution)/shard_map/ppermute | solution.py:14
  224.0 25.2 %collective-permute-start.4 = (bf16[2048,768]{1,0:T(8,128)(2,1)}, bf16[2048,768]{1,0:T(8,128)(2,1)}, u32[]{:S(2)}, u32[]{:S(2)}) collective-permute-start(bf16[2048,768]{1,0:T(8,128)(2,1)} %bitcast), channel_id=1, source_target_pairs={{0,1},{1,0},{2,3},{3,2},{4,5},{5,4},{6,7},{7,6},{8,9},{9,8},{10,11... | collective-permute-start | bytes 9437192 | tf_op jit(solution)/shard_map/ppermute | solution.py:9
  237.3 18.0 %collective-permute-start.5 = (bf16[768,1024]{1,0:T(8,128)(2,1)S(1)}, bf16[768,1024]{1,0:T(8,128)(2,1)S(1)}, u32[]{:S(2)}, u32[]{:S(2)}) collective-permute-start(bf16[768,1024]{1,0:T(8,128)(2,1)S(1)} %bitcast.54), channel_id=1, source_target_pairs={{0,1},{1,0},{2,3},{3,2},{4,5},{5,4},{6,7},{7,6},{8,9},{9,8},{10,11... | collective-permute-start | bytes 4718600 | tf_op jit(solution)/shard_map/ppermute | solution.py:9
  256.3 25.1 %collective-permute-start.35 = (bf16[128,1024]{1,0:T(8,128)(2,1)S(1)}, bf16[128,1024]{1,0:T(8,128)(2,1)S(1)}, u32[]{:S(2)}, u32[]{:S(2)}) collective-permute-start(bf16[128,1024]{1,0:T(8,128)(2,1)S(1)} %get-tuple-element.27), channel_id=1, source_target_pairs={{0,2},{2,0},{4,6},{6,4},{8,10},{10,8},{12,14},{14,12},{16,18},{18,... | collective-permute-start | bytes 786440 | tf_op jit(solution)/shard_map/ppermute | solution.py:14
  257.1 25.2 %collective-permute-start.33 = (bf16[128,1024]{1,0:T(8,128)(2,1)S(1)}, bf16[128,1024]{1,0:T(8,128)(2,1)S(1)}, u32[]{:S(2)}, u32[]{:S(2)}) collective-permute-start(bf16[128,1024]{1,0:T(8,128)(2,1)S(1)} %get-tuple-element.25), channel_id=1, source_target_pairs={{0,4},{2,6},{4,0},{6,2},{8,12},{10,14},{12,8},{14,10},{16,20},{18,... | collective-permute-start | bytes 786440 | tf_op jit(solution)/shard_map/ppermute | solution.py:14
  264.5 19.4 %collective-permute-start.26 = (bf16[128,1024]{1,0:T(8,128)(2,1)S(1)}, bf16[128,1024]{1,0:T(8,128)(2,1)S(1)}, u32[]{:S(2)}, u32[]{:S(2)}) collective-permute-start(bf16[128,1024]{1,0:T(8,128)(2,1)S(1)} %get-tuple-element.21), channel_id=1, source_target_pairs={{0,2},{2,0},{4,6},{6,4},{8,10},{10,8},{12,14},{14,12},{16,18},{18,... | collective-permute-start | bytes 786440 | tf_op jit(solution)/shard_map/ppermute | solution.py:14
  266.0 19.3 %collective-permute-start.24 = (bf16[128,1024]{1,0:T(8,128)(2,1)S(1)}, bf16[128,1024]{1,0:T(8,128)(2,1)S(1)}, u32[]{:S(2)}, u32[]{:S(2)}) collective-permute-start(bf16[128,1024]{1,0:T(8,128)(2,1)S(1)} %get-tuple-element.19), channel_id=1, source_target_pairs={{0,4},{2,6},{4,0},{6,2},{8,12},{10,14},{12,8},{14,10},{16,20},{18,... | collective-permute-start | bytes 786440 | tf_op jit(solution)/shard_map/ppermute | solution.py:14
  282.3 23.8 %collective-permute-start.8 = (bf16[128,1024]{1,0:T(8,128)(2,1)S(1)}, bf16[128,1024]{1,0:T(8,128)(2,1)S(1)}, u32[]{:S(2)}, u32[]{:S(2)}) collective-permute-start(bf16[128,1024]{1,0:T(8,128)(2,1)S(1)} %get-tuple-element.9), channel_id=1, source_target_pairs={{0,2},{2,0},{4,6},{6,4},{8,10},{10,8},{12,14},{14,12},{16,18},{18,... | collective-permute-start | bytes 786440 | tf_op jit(solution)/shard_map/ppermute | solution.py:14
  283.9 18.1 %collective-permute-start.36 = (bf16[128,2048]{1,0:T(8,128)(2,1)S(1)}, bf16[128,2048]{1,0:T(8,128)(2,1)S(1)}, u32[]{:S(2)}, u32[]{:S(2)}) collective-permute-start(bf16[128,2048]{1,0:T(8,128)(2,1)S(1)} %pad_maximum_fusion.8), channel_id=1, source_target_pairs={{0,4},{2,6},{4,0},{6,2},{8,12},{10,14},{12,8},{14,10},{16,20},{18,... | collective-permute-start | bytes 1572872 | tf_op jit(solution)/shard_map/ppermute | solution.py:14
  285.4 18.0 %collective-permute-start.34 = (bf16[128,2048]{1,0:T(8,128)(2,1)S(1)}, bf16[128,2048]{1,0:T(8,128)(2,1)S(1)}, u32[]{:S(2)}, u32[]{:S(2)}) collective-permute-start(bf16[128,2048]{1,0:T(8,128)(2,1)S(1)} %pad_maximum_fusion.7), channel_id=1, source_target_pairs={{0,2},{2,0},{4,6},{6,4},{8,10},{10,8},{12,14},{14,12},{16,18},{18,... | collective-permute-start | bytes 1572872 | tf_op jit(solution)/shard_map/ppermute | solution.py:14
  286.3 37.4 %collective-permute-start.6 = (bf16[128,1024]{1,0:T(8,128)(2,1)S(1)}, bf16[128,1024]{1,0:T(8,128)(2,1)S(1)}, u32[]{:S(2)}, u32[]{:S(2)}) collective-permute-start(bf16[128,1024]{1,0:T(8,128)(2,1)S(1)} %get-tuple-element.7), channel_id=1, source_target_pairs={{0,4},{2,6},{4,0},{6,2},{8,12},{10,14},{12,8},{14,10},{16,20},{18,... | collective-permute-start | bytes 786440 | tf_op jit(solution)/shard_map/ppermute | solution.py:14
  290.8 28.1 %collective-permute-start.27 = (bf16[128,2048]{1,0:T(8,128)(2,1)S(1)}, bf16[128,2048]{1,0:T(8,128)(2,1)S(1)}, u32[]{:S(2)}, u32[]{:S(2)}) collective-permute-start(bf16[128,2048]{1,0:T(8,128)(2,1)S(1)} %pad_maximum_fusion.6), channel_id=1, source_target_pairs={{0,4},{2,6},{4,0},{6,2},{8,12},{10,14},{12,8},{14,10},{16,20},{18,... | collective-permute-start | bytes 1572872 | tf_op jit(solution)/shard_map/ppermute | solution.py:14
  302.0 18.2 %collective-permute-start.25 = (bf16[128,2048]{1,0:T(8,128)(2,1)S(1)}, bf16[128,2048]{1,0:T(8,128)(2,1)S(1)}, u32[]{:S(2)}, u32[]{:S(2)}) collective-permute-start(bf16[128,2048]{1,0:T(8,128)(2,1)S(1)} %pad_maximum_fusion.5), channel_id=1, source_target_pairs={{0,2},{2,0},{4,6},{6,4},{8,10},{10,8},{12,14},{14,12},{16,18},{18,... | collective-permute-start | bytes 1572872 | tf_op jit(solution)/shard_map/ppermute | solution.py:14
  303.6 16.6 %collective-permute-start.37 = (bf16[128,2048]{1,0:T(8,128)(2,1)S(1)}, bf16[128,2048]{1,0:T(8,128)(2,1)S(1)}, u32[]{:S(2)}, u32[]{:S(2)}) collective-permute-start(bf16[128,2048]{1,0:T(8,128)(2,1)S(1)} %add_convert_fusion.2), channel_id=1, source_target_pairs={{0,24},{2,26},{4,28},{6,30},{8,0},{10,2},{12,4},{14,6},{16,8},{18,... | collective-permute-start | bytes 1572872 | tf_op jit(solution)/shard_map/ppermute | solution.py:19
  306.1 24.0 %collective-permute-start.18 = (bf16[128,2048]{1,0:T(8,128)(2,1)S(1)}, bf16[128,2048]{1,0:T(8,128)(2,1)S(1)}, u32[]{:S(2)}, u32[]{:S(2)}) collective-permute-start(bf16[128,2048]{1,0:T(8,128)(2,1)S(1)} %pad_maximum_fusion.4), channel_id=1, source_target_pairs={{0,4},{2,6},{4,0},{6,2},{8,12},{10,14},{12,8},{14,10},{16,20},{18,... | collective-permute-start | bytes 1572872 | tf_op jit(solution)/shard_map/ppermute | solution.py:14
  322.9 15.9 %collective-permute-start.9 = (bf16[128,2048]{1,0:T(8,128)(2,1)S(1)}, bf16[128,2048]{1,0:T(8,128)(2,1)S(1)}, u32[]{:S(2)}, u32[]{:S(2)}) collective-permute-start(bf16[128,2048]{1,0:T(8,128)(2,1)S(1)} %pad_maximum_fusion.2), channel_id=1, source_target_pairs={{0,4},{2,6},{4,0},{6,2},{8,12},{10,14},{12,8},{14,10},{16,20},{18,... | collective-permute-start | bytes 1572872 | tf_op jit(solution)/shard_map/ppermute | solution.py:14
  (23 other events, 381.2 us)

commit v2 on v1

v2 whole, which is shorter than its diff:
```python
import functools

import jax
import jax.numpy as jnp
from jax import lax
from jax.experimental import pallas as pl
from jax.experimental.pallas import tpu as pltpu
from jax.sharding import PartitionSpec as P

PIECES = 1


def swap_cores(x):
    size = lax.axis_size("dp")
    return lax.ppermute(x, "dp", [(i, i ^ 1) for i in range(size)])


def flip(x, bit):
    size = lax.axis_size("expert")
    return lax.ppermute(x, "expert", [(i, i ^ bit) for i in range(size)])


def turn(x, by):
    size = lax.axis_size("expert")
    return lax.ppermute(x, "expert", [(i, (i + 4 * by) % size) for i in range(size)])


def spread(w):
    return lax.all_to_all(w, "expert", split_axis=0, concat_axis=0, tiled=True)


def after(x, *others):
    return lax.optimization_barrier((x, *others))[0]


def hidden_kernel(blocks, rows, model, experts, place, *refs):
    tokens, weights = refs[:blocks], refs[blocks : blocks + 2 * PIECES]
    hidden, scale = refs[blocks + 2 * PIECES : blocks + 2 * PIECES + 2]
    held, loaded, token_sems, weight_sems = refs[blocks + 2 * PIECES + 2 :]
    me, core = place[0], place[1]
    token_copies = [
        pltpu.make_async_copy(tokens[i], held.at[pl.ds(i * rows, rows)], token_sems.at[i]) for i in range(blocks)
    ]
    weight_copies = [
        pltpu.make_async_copy(weights[i], loaded.at[i], weight_sems.at[i]) for i in range(2 * PIECES)
    ]
    for i in range(4):
        token_copies[i].start()
    for copy in weight_copies:
        copy.start()
    for i in range(4, blocks):
        token_copies[i].start()
    for i in range(4):
        token_copies[i].wait()
    for copy in weight_copies:
        copy.wait()
    for i in range(4, blocks):
        token_copies[i].wait()
    group = 4 * rows
    piece = loaded.shape[2] // 2
    columns = held.shape[1] - model

    def step(s, carry):
        at = pl.ds(pl.multiple_of(s * group, group), group)
        lane = lax.broadcasted_iota(jnp.int32, (group, columns), 1)
        wanted = (lane == me) | (lane == me + experts) | (lane == me + 2 * experts)
        picked = jnp.where(wanted, held[at, model:].astype(jnp.float32), 0.0)
        scale[at, :] = jnp.broadcast_to(jnp.sum(picked, axis=1, keepdims=True), (group, 128))
        x = held[at, :model]
        for side in range(2):
            start = jnp.where(side == 0, core, 1 - core) * (piece * PIECES)
            for p in range(PIECES):
                both = jnp.dot(x, loaded[side * PIECES + p], preferred_element_type=jnp.float32)
                gate, up = both[:, :piece], both[:, piece:]
                value = gate / (1.0 + jnp.exp(-gate)) * up
                hidden[at, pl.ds(pl.multiple_of(start + p * piece, 128), piece)] = value.astype(jnp.bfloat16)
        return carry

    lax.fori_loop(0, blocks // 4, step, 0)


def out_kernel(rows, place, hidden, scale, own, other, *outs):
    core = place[1]
    part = own.shape[1]
    for side, w in ((0, own), (1, other)):
        start = pl.multiple_of(jnp.where(side == 0, core, 1 - core) * part, part)
        for c in range(0, part, 256):
            value = jnp.dot(hidden[...], w[:, c : c + 256], preferred_element_type=jnp.float32)
            value = (value * scale[:, :1]).astype(jnp.bfloat16)
            for q in range(4):
                outs[q][:, pl.ds(pl.multiple_of(start + c, 256), 256)] = value[q * rows : (q + 1) * rows]


def local(tokens, route_ids, route_weights, w_gate, w_up, w_down):
    devices = lax.axis_size("expert")
    experts, depth, width = w_gate.shape
    rows, model = tokens.shape
    line = devices // 4
    me = lax.axis_index("expert")
    core = lax.axis_index("dp") % 2
    place = jnp.stack([me, core]).astype(jnp.int32)
    half, part = width // 2, model // 2
    piece = half // PIECES
    f32, bf16 = jnp.float32, jnp.bfloat16

    share = jnp.sum(
        jnp.where(
            route_ids[:, :, None] == jnp.arange(experts, dtype=jnp.int32)[None, None, :],
            route_weights[:, :, None],
            0.0,
        ),
        axis=1,
    )
    first = share.astype(bf16)
    rest = share - first.astype(f32)
    second = rest.astype(bf16)
    third = (rest - second.astype(f32)).astype(bf16)
    extra = jnp.concatenate([first, second, third], axis=1)
    extra = jnp.pad(extra, ((0, 0), (0, -(3 * experts) % 128)))
    tokens = jnp.concatenate([tokens, extra], axis=1)

    held = [tokens]
    for s in range(1, line):
        held.append(turn(held[-1], 1))
    by_x, by_y, across = [], [], []
    for s in range(line):
        by_x.append(flip(held[s], 1))
        by_y.append(flip(held[s], 2))
        across.append(flip(by_x[s], 2) if s % 2 == 0 else flip(by_y[s], 1))

    wides = []
    for p in range(PIECES):
        at = core * half + p * piece
        wide = jnp.concatenate(
            [lax.dynamic_slice_in_dim(w, at, piece, axis=2) for w in (w_gate, w_up)], axis=2
        )
        wide = after(wide, *by_x[:2], *by_y[:2], held[-1])
        wides.append(spread(wide))
    flat = [w.reshape(devices * depth, 2 * piece) for w in wides]
    flat_other = [swap_cores(w) for w in flat]
    down = lax.dynamic_slice_in_dim(w_down, core * part, part, axis=2)
    down = spread(after(down, wides[-1], *by_x[1:], *by_y[1:], *across[:2])).reshape(width, part)
    down_other = swap_cores(down)

    gathered = [b for s in range(line) for b in (held[s], by_x[s], by_y[s], across[s])]
    total_rows = devices * rows
    any_spec = pl.BlockSpec(memory_space=pl.ANY)
    vmem_spec = pl.BlockSpec(memory_space=pltpu.VMEM)
    smem_spec = pl.BlockSpec(memory_space=pltpu.SMEM)
    hidden, scale = pl.pallas_call(
        functools.partial(hidden_kernel, devices, rows, model, experts),
        out_shape=[
            jax.ShapeDtypeStruct((total_rows, width), bf16),
            jax.ShapeDtypeStruct((total_rows, 128), f32),
        ],
        in_specs=[smem_spec] + [any_spec] * (devices + 2 * PIECES),
        out_specs=[vmem_spec, vmem_spec],
        scratch_shapes=[
            pltpu.VMEM((total_rows, tokens.shape[1]), bf16),
            pltpu.VMEM((2 * PIECES, devices * depth, 2 * piece), bf16),
            pltpu.SemaphoreType.DMA((devices,)),
            pltpu.SemaphoreType.DMA((2 * PIECES,)),
        ],
        compiler_params=pltpu.CompilerParams(vmem_limit_bytes=48 * 1024 * 1024),
        cost_estimate=pl.CostEstimate(
            flops=4 * total_rows * model * width, bytes_accessed=20_000_000, transcendentals=total_rows * width
        ),
        name="hidden",
    )(place, *gathered, *flat, *flat_other)

    group = 4 * rows
    arriving = None
    for s in reversed(range(line)):
        kept, to_x, to_y, over = pl.pallas_call(
            functools.partial(out_kernel, rows),
            out_shape=[jax.ShapeDtypeStruct((rows, model), bf16)] * 4,
            grid=(1,),
            in_specs=[
                smem_spec,
                pl.BlockSpec((group, width), lambda i, s=s: (s, 0)),
                pl.BlockSpec((group, 128), lambda i, s=s: (s, 0)),
                pl.BlockSpec((width, part), lambda i: (0, 0)),
                pl.BlockSpec((width, part), lambda i: (0, 0)),
            ],
            out_specs=[pl.BlockSpec((rows, model), lambda i: (0, 0))] * 4,
            compiler_params=pltpu.CompilerParams(vmem_limit_bytes=32 * 1024 * 1024),
            cost_estimate=pl.CostEstimate(
                flops=2 * group * model * width, bytes_accessed=6_500_000, transcendentals=0
            ),
            name="out",
        )(place, hidden, scale, down, down_other)
        if s % 2 == 0:
            to_x = (to_x.astype(f32) + flip(over, 2).astype(f32)).astype(bf16)
        else:
            to_y = (to_y.astype(f32) + flip(over, 1).astype(f32)).astype(bf16)
        total = kept.astype(f32) + flip(to_x, 1).astype(f32) + flip(to_y, 2).astype(f32)
        if arriving is not None:
            total = total + arriving.astype(f32)
        if s > 0:
            arriving = turn(total.astype(bf16), -1)
    return total.astype(bf16)


def solution(mesh):
    placed = (
        P(("dp", "expert"), None),
        P(("dp", "expert"), None),
        P(("dp", "expert"), None),
        P(None, "expert", None),
        P(None, "expert", None),
        P(None, "expert", None),
    )
    return jax.shard_map(
        local, mesh=mesh, in_specs=placed, out_specs=P(("dp", "expert"), None), check_vma=False
    )
```

time: 349 us -> 285 us (0.82)
  matrix products: 43.3 us -> 0 us
  Pallas kernels: 0 us -> 36.5 us
  blocking collectives: 35.2 us -> 0 us
  starting transfers between devices: 60.1 us -> 45.4 us
  local copies, waits for them, and re-layouts: 15.6 us -> 8.72 us
    ppermute x6, waiting for transfers between devices: 123 us -> 28.2 us  [turn(): lax.ppermute(x, 'expert', [(i, (i + 4 * by) % size) for i in range(size)])]
    ppermute x32 -> x24, waiting for transfers between devices: 50.9 us -> 123 us  [flip(): return lax.ppermute(x, 'expert', [(i, i ^ bit) for i in range(size)])]
    dot_general x16 -> x0, matrix products: 43.3 us -> none  [the longest x8 35.3 us: hidden_of(): both = jnp.dot(x, w, preferred_element_type=jnp.float32)]
    pallas_call x0 -> x5, Pallas kernels: none -> 36.5 us  [the longest x1 21.6 us: local(): pl.pallas_call(functools.partial(hidden_kernel, devices, rows, model, exp...]
    all_gather x1 -> x0, blocking collectives: 35.2 us -> none  [local(): shares = lax.all_gather(share, 'expert', axis=0)]
    all_to_all x2, waiting for transfers between devices: 9.56 us -> 33.6 us  [spread(): return lax.all_to_all(w, 'expert', split_axis=0, concat_axis=0, tiled=True)]
    ppermute x32 -> x24, starting transfers between devices: 34.8 us -> 25.3 us  [flip(): return lax.ppermute(x, 'expert', [(i, i ^ bit) for i in range(size)])]
    slice x17 -> x0, local copies, waits for them, and re-layouts: 8.66 us -> none  [the longest x4 4.59 us: local(): by_x[:, :part]]
  transfers between devices with their start and end apart: 42 -> 34, of which waited for: 16 -> 20; matrix products, arithmetic and copies ran while one was open for 16% -> 3% of each run, Pallas kernels for 0% -> 12%
where the time goes in v2:
time: 285 us; the launch traced here: 283 us
  waiting for transfers between devices  185 us (65%)
  starting transfers between devices  45.4 us (16%)
  Pallas kernels  36.5 us (13%)
  local copies, waits for them, and re-layouts  8.72 us (3%)
  other arithmetic  7.42 us (3%)
    ppermute x24, waiting for transfers between devices, flip(): return lax.ppermute(x, 'expert', [(i, i ^ bit) for i in range(size)])  123 us
    all_to_all x2, waiting for transfers between devices, spread(): return lax.all_to_all(w, 'expert', split_axis=0, concat_axis=0, tiled=True)  33.6 us
    ppermute x6, waiting for transfers between devices, turn(): lax.ppermute(x, 'expert', [(i, (i + 4 * by) % size) for i in range(size)])  28.2 us
    ppermute x24, starting transfers between devices, flip(): return lax.ppermute(x, 'expert', [(i, i ^ bit) for i in range(size)])  25.3 us
    pallas_call x1, Pallas kernels, local(): pl.pallas_call(functools.partial(hidden_kernel, devices, rows, model, exp...  21.6 us
    pallas_call x4, Pallas kernels, local(): pl.pallas_call(functools.partial(out_kernel, rows), out_shape=[jax.ShapeD...  14.9 us
    all_to_all x2, starting transfers between devices, spread(): return lax.all_to_all(w, 'expert', split_axis=0, concat_axis=0, tiled=True)  14.3 us
  transfers between devices with their start and end apart: 34, of which 20 were waited for; matrix products, arithmetic and copies ran while one was open for 3% of the time, Pallas kernels for 12%

profile of v2, /device:TPU:12, one launch (start us, length us, event | category | flops | bytes accessed | tf_op | source)
XLA Modules:
  0.0 283.3 jit_solution(7815725052150221429)
XLA Ops:
  1.0 1.9 fusion.1.refs_0_
  2.9 1.6 collective-permute-start.3
  4.5 13.1 %collective-permute-done.3.refs_4_ = bf16[128,2176]{1,0:T(8,128)(2,1)} collective-permute-done((bf16[128,2176]{1,0:T(8,128)(2,1)}, bf16[128,2176]{1,0:T(8,128)(2,1)}, u32[]{:S(2)}, u32[]{:S(2)}) %collective-permute-start.3) | collective-permute-done | bytes 557088 | tf_op jit(solution)/shard_map/ppermute | solution.py:25
  17.6 1.6 collective-permute-start.7
  21.7 1.5 collective-permute-start.5
  23.2 8.8 %collective-permute-done.7.refs_8_ = bf16[128,2176]{1,0:T(8,128)(2,1)} collective-permute-done((bf16[128,2176]{1,0:T(8,128)(2,1)}, bf16[128,2176]{1,0:T(8,128)(2,1)}, u32[]{:S(2)}, u32[]{:S(2)}) %collective-permute-start.7) | collective-permute-done | bytes 557088 | tf_op jit(solution)/shard_map/ppermute | solution.py:25
  33.0 2.3 constant_dynamic-slice_fusion.1
  35.3 2.0 pad_maximum_fusion
  37.3 7.3 %collective-permute-done.4.refs_5_ = bf16[128,2176]{1,0:T(8,128)(2,1)} collective-permute-done((bf16[128,2176]{1,0:T(8,128)(2,1)}, bf16[128,2176]{1,0:T(8,128)(2,1)}, u32[]{:S(2)}, u32[]{:S(2)}) %collective-permute-start.4) | collective-permute-done | bytes 557088 | tf_op jit(solution)/shard_map/ppermute | solution.py:20
  46.8 8.2 %all-to-all-start = ((bf16[16,128,768]{2,1,0:T(8,128)(2,1)}), bf16[16,128,768]{2,1,0:T(8,128)(2,1)}, u32[]{:S(2)}, u32[]{:S(2)}) async-start(bf16[16,128,768]{2,1,0:T(8,128)(2,1)} %pad_maximum_fusion), calls=%async_computation | async-start | bytes 6291456 | tf_op jit(solution)/shard_map/all_to_all | solution.py:29
  60.6 25.3 %collective-permute-done.2.refs_3_ = bf16[128,2176]{1,0:T(8,128)(2,1)S(1)} collective-permute-done((bf16[128,2176]{1,0:T(8,128)(2,1)}, bf16[128,2176]{1,0:T(8,128)(2,1)S(1)}, u32[]{:S(2)}, u32[]{:S(2)}) %collective-permute-start.2) | collective-permute-done | bytes 557088 | tf_op jit(solution)/shard_map/ppermute | solution.py:20
  86.7 2.8 %collective-permute-start.13 = (bf16[128,2176]{1,0:T(8,128)(2,1)}, bf16[128,2176]{1,0:T(8,128)(2,1)}, u32[]{:S(2)}, u32[]{:S(2)}) collective-permute-start(bf16[128,2176]{1,0:T(8,128)(2,1)} %collective-permute-done.11.refs_12_), channel_id=1, source_target_pairs={{0,4},{2,6},{4,0},{6,2},{8,12},{10,14},{12,8},{14,10},{16,20},{18,... | collective-permute-start | bytes 1671176 | tf_op jit(solution)/shard_map/ppermute | solution.py:20
  90.9 2.0 collective-permute-done.6.refs_7_
  92.9 14.7 %collective-permute-done.8.refs_9_ = bf16[128,2176]{1,0:T(8,128)(2,1)} collective-permute-done((bf16[128,2176]{1,0:T(8,128)(2,1)}, bf16[128,2176]{1,0:T(8,128)(2,1)}, u32[]{:S(2)}, u32[]{:S(2)}) %collective-permute-start.8) | collective-permute-done | bytes 557088 | tf_op jit(solution)/shard_map/ppermute | solution.py:20
  108.3 16.0 %collective-permute-done.12.refs_13_ = bf16[128,2176]{1,0:T(8,128)(2,1)} collective-permute-done((bf16[128,2176]{1,0:T(8,128)(2,1)}, bf16[128,2176]{1,0:T(8,128)(2,1)}, u32[]{:S(2)}, u32[]{:S(2)}) %collective-permute-start.12) | collective-permute-done | bytes 557088 | tf_op jit(solution)/shard_map/ppermute | solution.py:20
  124.4 6.1 %all-to-all-start.1 = ((bf16[16,48,1024]{2,1,0:T(8,128)(2,1)}), bf16[16,48,1024]{2,1,0:T(8,128)(2,1)}, u32[]{:S(2)}, u32[]{:S(2)}) async-start(bf16[16,48,1024]{2,1,0:T(8,128)(2,1)} %constant_dynamic-slice_fusion), calls=%async_computation.1 | async-start | bytes 3145728 | tf_op jit(solution)/shard_map/all_to_all | solution.py:29
  132.6 33.6 %all-to-all-done.1 = bf16[16,48,1024]{2,1,0:T(8,128)(2,1)} async-done(((bf16[16,48,1024]{2,1,0:T(8,128)(2,1)}), bf16[16,48,1024]{2,1,0:T(8,128)(2,1)}, u32[]{:S(2)}, u32[]{:S(2)}) %all-to-all-start.1) | async-done | bytes 1572896 | tf_op jit(solution)/shard_map/all_to_all | solution.py:29
  167.3 21.6 %hidden.1 = (bf16[2048,768]{1,0:T(8,128)(2,1)}, f32[2048,128]{1,0:T(8,128)}) custom-call(s32[2]{0:T(128)S(1)} %pad_add_fusion.place, bf16[128,2176]{1,0:T(8,128)(2,1)} %fusion.1.refs_0_, bf16[128,2176]{1,0:T(8,128)(2,1)} %collective-permute-done.refs_1_, bf16[128,2176]{1,0:T(8,128)(2,1)} %collective-permute-done.1.refs_2_, bf16[128,2176]{1,0:T(8,128)(2,1)S(1)} %copy-done.4, ...), custom_call_target="tpu_custom_call" | custom-call | flops 12884901888 | bytes 20000000 | tf_op jit(solution)/shard_map/hidden/pallas_call | solution.py:150
  189.0 1.9 copy-done.1
  192.1 3.7 %out.7 = (bf16[128,2048]{1,0:T(8,128)(2,1)S(1)}, bf16[128,2048]{1,0:T(8,128)(2,1)S(1)}, bf16[128,2048]{1,0:T(8,128)(2,1)S(1)}, bf16[128,2048]{1,0:T(8,128)(2,1)S(1)}) custom-call(s32[2]{0:T(128)S(1)} %pad_add_fusion.place, bf16[2048,768]{1,0:T(8,128)(2,1)S(1)} %copy-done.1, f32[2048,128]{1,0:T(8,128)S(1)} %copy-done.2, bf16[768,1024]{1,0:T(8,128)(2,1)} %bitcast.3.own, ...), custom_call_target="tpu_custom_call" | custom-call | flops 1610612736 | bytes 6500000 | tf_op jit(solution)/shard_map/out/pallas_call | solution.py:174
  197.9 3.7 %out.6 = (bf16[128,2048]{1,0:T(8,128)(2,1)S(1)}, bf16[128,2048]{1,0:T(8,128)(2,1)S(1)}, bf16[128,2048]{1,0:T(8,128)(2,1)S(1)}, bf16[128,2048]{1,0:T(8,128)(2,1)S(1)}) custom-call(s32[2]{0:T(128)S(1)} %pad_add_fusion.place, bf16[2048,768]{1,0:T(8,128)(2,1)S(1)} %copy-done.1, f32[2048,128]{1,0:T(8,128)S(1)} %copy-done.2, bf16[768,1024]{1,0:T(8,128)(2,1)} %bitcast.3.own, ...), custom_call_target="tpu_custom_call" | custom-call | flops 1610612736 | bytes 6500000 | tf_op jit(solution)/shard_map/out/pallas_call | solution.py:174
  202.1 1.6 collective-permute-start.23
  203.7 6.9 %collective-permute-done.27 = bf16[128,2048]{1,0:T(8,128)(2,1)S(1)} collective-permute-done((bf16[128,2048]{1,0:T(8,128)(2,1)S(1)}, bf16[128,2048]{1,0:T(8,128)(2,1)S(1)}, u32[]{:S(2)}, u32[]{:S(2)}) %collective-permute-start.27) | collective-permute-done | bytes 524320 | tf_op jit(solution)/shard_map/ppermute | solution.py:20
  211.2 3.7 %out.5 = (bf16[128,2048]{1,0:T(8,128)(2,1)S(1)}, bf16[128,2048]{1,0:T(8,128)(2,1)S(1)}, bf16[128,2048]{1,0:T(8,128)(2,1)S(1)}, bf16[128,2048]{1,0:T(8,128)(2,1)S(1)}) custom-call(s32[2]{0:T(128)S(1)} %pad_add_fusion.place, bf16[2048,768]{1,0:T(8,128)(2,1)S(1)} %copy-done.1, f32[2048,128]{1,0:T(8,128)S(1)} %copy-done.2, bf16[768,1024]{1,0:T(8,128)(2,1)} %bitcast.3.own, ...), custom_call_target="tpu_custom_call" | custom-call | flops 1610612736 | bytes 6500000 | tf_op jit(solution)/shard_map/out/pallas_call | solution.py:174
  215.7 12.1 %collective-permute-done.23 = bf16[128,2048]{1,0:T(8,128)(2,1)S(1)} collective-permute-done((bf16[128,2048]{1,0:T(8,128)(2,1)S(1)}, bf16[128,2048]{1,0:T(8,128)(2,1)S(1)}, u32[]{:S(2)}, u32[]{:S(2)}) %collective-permute-start.23) | collective-permute-done | bytes 524320 | tf_op jit(solution)/shard_map/ppermute | solution.py:20
  229.9 8.0 %collective-permute-done.28 = bf16[128,2048]{1,0:T(8,128)(2,1)S(1)} collective-permute-done((bf16[128,2048]{1,0:T(8,128)(2,1)S(1)}, bf16[128,2048]{1,0:T(8,128)(2,1)S(1)}, u32[]{:S(2)}, u32[]{:S(2)}) %collective-permute-start.28) | collective-permute-done | bytes 524320 | tf_op jit(solution)/shard_map/ppermute | solution.py:20
  238.4 3.7 %out.4 = (bf16[128,2048]{1,0:T(8,128)(2,1)S(1)}, bf16[128,2048]{1,0:T(8,128)(2,1)S(1)}, bf16[128,2048]{1,0:T(8,128)(2,1)S(1)}, bf16[128,2048]{1,0:T(8,128)(2,1)S(1)}) custom-call(s32[2]{0:T(128)S(1)} %pad_add_fusion.place, bf16[2048,768]{1,0:T(8,128)(2,1)S(1)} %copy-done.1, f32[2048,128]{1,0:T(8,128)S(1)} %copy-done.2, bf16[768,1024]{1,0:T(8,128)(2,1)} %bitcast.3.own, ...), custom_call_target="tpu_custom_call" | custom-call | flops 1610612736 | bytes 6500000 | tf_op jit(solution)/shard_map/out/pallas_call | solution.py:174
  242.8 1.7 collective-permute-start.22
  244.5 10.7 %collective-permute-done.24 = bf16[128,2048]{1,0:T(8,128)(2,1)S(1)} collective-permute-done((bf16[128,2048]{1,0:T(8,128)(2,1)S(1)}, bf16[128,2048]{1,0:T(8,128)(2,1)S(1)}, u32[]{:S(2)}, u32[]{:S(2)}) %collective-permute-start.24) | collective-permute-done | bytes 524320 | tf_op jit(solution)/shard_map/ppermute | solution.py:20
  258.0 10.4 %collective-permute-done.22 = bf16[128,2048]{1,0:T(8,128)(2,1)S(1)} collective-permute-done((bf16[128,2048]{1,0:T(8,128)(2,1)S(1)}, bf16[128,2048]{1,0:T(8,128)(2,1)S(1)}, u32[]{:S(2)}, u32[]{:S(2)}) %collective-permute-start.22) | collective-permute-done | bytes 524320 | tf_op jit(solution)/shard_map/ppermute | solution.py:20
  270.7 6.9 %collective-permute-done.19 = bf16[128,2048]{1,0:T(8,128)(2,1)S(1)} collective-permute-done((bf16[128,2048]{1,0:T(8,128)(2,1)S(1)}, bf16[128,2048]{1,0:T(8,128)(2,1)S(1)}, u32[]{:S(2)}, u32[]{:S(2)}) %collective-permute-start.19) | collective-permute-done | bytes 524320 | tf_op jit(solution)/shard_map/ppermute | solution.py:20
  277.6 4.5 %collective-permute-done.31 = bf16[128,2048]{1,0:T(8,128)(2,1)S(1)} collective-permute-done((bf16[128,2048]{1,0:T(8,128)(2,1)S(1)}, bf16[128,2048]{1,0:T(8,128)(2,1)S(1)}, u32[]{:S(2)}, u32[]{:S(2)}) %collective-permute-start.31) | collective-permute-done | bytes 524320 | tf_op jit(solution)/shard_map/ppermute | solution.py:25
  (68 shorter events, 33.1 us)
Async XLA Ops:
  2.9 14.7 %collective-permute-start.3 = (bf16[128,2176]{1,0:T(8,128)(2,1)}, bf16[128,2176]{1,0:T(8,128)(2,1)}, u32[]{:S(2)}, u32[]{:S(2)}) collective-permute-start(bf16[128,2176]{1,0:T(8,128)(2,1)} %fusion.1.refs_0_), channel_id=1, source_target_pairs={{0,8},{2,10},{4,12},{6,14},{8,16},{10,18},{12,20},{14,22},{16,24},... | collective-permute-start | bytes 1671176 | tf_op jit(solution)/shard_map/ppermute | solution.py:25
  17.6 14.4 %collective-permute-start.7 = (bf16[128,2176]{1,0:T(8,128)(2,1)}, bf16[128,2176]{1,0:T(8,128)(2,1)}, u32[]{:S(2)}, u32[]{:S(2)}) collective-permute-start(bf16[128,2176]{1,0:T(8,128)(2,1)} %collective-permute-done.3.refs_4_), channel_id=1, source_target_pairs={{0,8},{2,10},{4,12},{6,14},{8,16},{10,18},{12,20},{14,22},{16,24},... | collective-permute-start | bytes 1671176 | tf_op jit(solution)/shard_map/ppermute | solution.py:25
  19.2 18.1 %collective-permute-start = (bf16[128,2176]{1,0:T(8,128)(2,1)}, bf16[128,2176]{1,0:T(8,128)(2,1)}, u32[]{:S(2)}, u32[]{:S(2)}) collective-permute-start(bf16[128,2176]{1,0:T(8,128)(2,1)} %fusion.1.refs_0_), channel_id=1, source_target_pairs={{0,2},{2,0},{4,6},{6,4},{8,10},{10,8},{12,14},{14,12},{16,18},{18,... | collective-permute-start | bytes 1671176 | tf_op jit(solution)/shard_map/ppermute | solution.py:20
  20.7 16.6 %collective-permute-start.1 = (bf16[128,2176]{1,0:T(8,128)(2,1)}, bf16[128,2176]{1,0:T(8,128)(2,1)}, u32[]{:S(2)}, u32[]{:S(2)}) collective-permute-start(bf16[128,2176]{1,0:T(8,128)(2,1)} %fusion.1.refs_0_), channel_id=1, source_target_pairs={{0,4},{2,6},{4,0},{6,2},{8,12},{10,14},{12,8},{14,10},{16,20},{18,... | collective-permute-start | bytes 1671176 | tf_op jit(solution)/shard_map/ppermute | solution.py:20
  21.2 23.5 %collective-permute-start.4 = (bf16[128,2176]{1,0:T(8,128)(2,1)}, bf16[128,2176]{1,0:T(8,128)(2,1)}, u32[]{:S(2)}, u32[]{:S(2)}) collective-permute-start(bf16[128,2176]{1,0:T(8,128)(2,1)} %collective-permute-done.3.refs_4_), channel_id=1, source_target_pairs={{0,2},{2,0},{4,6},{6,4},{8,10},{10,8},{12,14},{14,12},{16,18},{18,... | collective-permute-start | bytes 1671176 | tf_op jit(solution)/shard_map/ppermute | solution.py:20
  21.7 24.1 %collective-permute-start.5 = (bf16[128,2176]{1,0:T(8,128)(2,1)}, bf16[128,2176]{1,0:T(8,128)(2,1)}, u32[]{:S(2)}, u32[]{:S(2)}) collective-permute-start(bf16[128,2176]{1,0:T(8,128)(2,1)} %collective-permute-done.3.refs_4_), channel_id=1, source_target_pairs={{0,4},{2,6},{4,0},{6,2},{8,12},{10,14},{12,8},{14,10},{16,20},{18,... | collective-permute-start | bytes 1671176 | tf_op jit(solution)/shard_map/ppermute | solution.py:20
  32.0 14.8 %collective-permute-start.11 = (bf16[128,2176]{1,0:T(8,128)(2,1)}, bf16[128,2176]{1,0:T(8,128)(2,1)}, u32[]{:S(2)}, u32[]{:S(2)}) collective-permute-start(bf16[128,2176]{1,0:T(8,128)(2,1)} %collective-permute-done.7.refs_8_), channel_id=1, source_target_pairs={{0,8},{2,10},{4,12},{6,14},{8,16},{10,18},{12,20},{14,22},{16,24},... | collective-permute-start | bytes 1671176 | tf_op jit(solution)/shard_map/ppermute | solution.py:25
  46.8 77.6 %all-to-all-start = ((bf16[16,128,768]{2,1,0:T(8,128)(2,1)}), bf16[16,128,768]{2,1,0:T(8,128)(2,1)}, u32[]{:S(2)}, u32[]{:S(2)}) async-start(bf16[16,128,768]{2,1,0:T(8,128)(2,1)} %pad_maximum_fusion), calls=%async_computation | async-start | bytes 6291456 | tf_op jit(solution)/shard_map/all_to_all | solution.py:29
  55.0 30.8 %collective-permute-start.2 = (bf16[128,2176]{1,0:T(8,128)(2,1)}, bf16[128,2176]{1,0:T(8,128)(2,1)S(1)}, u32[]{:S(2)}, u32[]{:S(2)}) collective-permute-start(bf16[128,2176]{1,0:T(8,128)(2,1)} %collective-permute-done.refs_1_), channel_id=1, source_target_pairs={{0,4},{2,6},{4,0},{6,2},{8,12},{10,14},{12,8},{14,10},{16,20},{18,... | collective-permute-start | bytes 1671176 | tf_op jit(solution)/shard_map/ppermute | solution.py:20
  55.6 37.3 %collective-permute-start.6 = (bf16[128,2176]{1,0:T(8,128)(2,1)}, bf16[128,2176]{1,0:T(8,128)(2,1)}, u32[]{:S(2)}, u32[]{:S(2)}) collective-permute-start(bf16[128,2176]{1,0:T(8,128)(2,1)} %collective-permute-done.5.refs_6_), channel_id=1, source_target_pairs={{0,2},{2,0},{4,6},{6,4},{8,10},{10,8},{12,14},{14,12},{16,18},{18,... | collective-permute-start | bytes 1671176 | tf_op jit(solution)/shard_map/ppermute | solution.py:20
  57.0 50.5 %collective-permute-start.8 = (bf16[128,2176]{1,0:T(8,128)(2,1)}, bf16[128,2176]{1,0:T(8,128)(2,1)}, u32[]{:S(2)}, u32[]{:S(2)}) collective-permute-start(bf16[128,2176]{1,0:T(8,128)(2,1)} %collective-permute-done.7.refs_8_), channel_id=1, source_target_pairs={{0,2},{2,0},{4,6},{6,4},{8,10},{10,8},{12,14},{14,12},{16,18},{18,... | collective-permute-start | bytes 1671176 | tf_op jit(solution)/shard_map/ppermute | solution.py:20
  57.6 50.7 %collective-permute-start.9 = (bf16[128,2176]{1,0:T(8,128)(2,1)}, bf16[128,2176]{1,0:T(8,128)(2,1)}, u32[]{:S(2)}, u32[]{:S(2)}) collective-permute-start(bf16[128,2176]{1,0:T(8,128)(2,1)} %collective-permute-done.7.refs_8_), channel_id=1, source_target_pairs={{0,4},{2,6},{4,0},{6,2},{8,12},{10,14},{12,8},{14,10},{16,20},{18,... | collective-permute-start | bytes 1671176 | tf_op jit(solution)/shard_map/ppermute | solution.py:20
  59.1 65.3 %collective-permute-start.12 = (bf16[128,2176]{1,0:T(8,128)(2,1)}, bf16[128,2176]{1,0:T(8,128)(2,1)}, u32[]{:S(2)}, u32[]{:S(2)}) collective-permute-start(bf16[128,2176]{1,0:T(8,128)(2,1)} %collective-permute-done.11.refs_12_), channel_id=1, source_target_pairs={{0,2},{2,0},{4,6},{6,4},{8,10},{10,8},{12,14},{14,12},{16,18},{18,... | collective-permute-start | bytes 1671176 | tf_op jit(solution)/shard_map/ppermute | solution.py:20
  86.7 37.7 %collective-permute-start.13 = (bf16[128,2176]{1,0:T(8,128)(2,1)}, bf16[128,2176]{1,0:T(8,128)(2,1)}, u32[]{:S(2)}, u32[]{:S(2)}) collective-permute-start(bf16[128,2176]{1,0:T(8,128)(2,1)} %collective-permute-done.11.refs_12_), channel_id=1, source_target_pairs={{0,4},{2,6},{4,0},{6,2},{8,12},{10,14},{12,8},{14,10},{16,20},{18,... | collective-permute-start | bytes 1671176 | tf_op jit(solution)/shard_map/ppermute | solution.py:20
  124.4 41.8 %all-to-all-start.1 = ((bf16[16,48,1024]{2,1,0:T(8,128)(2,1)}), bf16[16,48,1024]{2,1,0:T(8,128)(2,1)}, u32[]{:S(2)}, u32[]{:S(2)}) async-start(bf16[16,48,1024]{2,1,0:T(8,128)(2,1)} %constant_dynamic-slice_fusion), calls=%async_computation.1 | async-start | bytes 3145728 | tf_op jit(solution)/shard_map/all_to_all | solution.py:29
  130.5 35.8 %collective-permute-start.15 = (bf16[2048,768]{1,0:T(8,128)(2,1)}, bf16[2048,768]{1,0:T(8,128)(2,1)}, u32[]{:S(2)}, u32[]{:S(2)}) collective-permute-start(bf16[2048,768]{1,0:T(8,128)(2,1)} %bitcast.2.refs_16_), channel_id=1, source_target_pairs={{0,1},{1,0},{2,3},{3,2},{4,5},{5,4},{6,7},{7,6},{8,9},{9,8},{10,11... | collective-permute-start | bytes 9437192 | tf_op jit(solution)/shard_map/ppermute | solution.py:15
  130.5 35.8 %collective-permute-start.10 = (bf16[128,2176]{1,0:T(8,128)(2,1)}, bf16[128,2176]{1,0:T(8,128)(2,1)}, u32[]{:S(2)}, u32[]{:S(2)}) collective-permute-start(bf16[128,2176]{1,0:T(8,128)(2,1)} %collective-permute-done.8.refs_9_), channel_id=1, source_target_pairs={{0,4},{2,6},{4,0},{6,2},{8,12},{10,14},{12,8},{14,10},{16,20},{18,... | collective-permute-start | bytes 1671176 | tf_op jit(solution)/shard_map/ppermute | solution.py:20
  131.1 35.2 %collective-permute-start.14 = (bf16[128,2176]{1,0:T(8,128)(2,1)}, bf16[128,2176]{1,0:T(8,128)(2,1)}, u32[]{:S(2)}, u32[]{:S(2)}) collective-permute-start(bf16[128,2176]{1,0:T(8,128)(2,1)} %collective-permute-done.13.refs_14_), channel_id=1, source_target_pairs={{0,2},{2,0},{4,6},{6,4},{8,10},{10,8},{12,14},{14,12},{16,18},{18,... | collective-permute-start | bytes 1671176 | tf_op jit(solution)/shard_map/ppermute | solution.py:20
  166.2 22.7 %collective-permute-start.16 = (bf16[768,1024]{1,0:T(8,128)(2,1)}, bf16[768,1024]{1,0:T(8,128)(2,1)}, u32[]{:S(2)}, u32[]{:S(2)}) collective-permute-start(bf16[768,1024]{1,0:T(8,128)(2,1)} %bitcast.3.own), channel_id=1, source_target_pairs={{0,1},{1,0},{2,3},{3,2},{4,5},{5,4},{6,7},{7,6},{8,9},{9,8},{10,11... | collective-permute-start | bytes 4718600 | tf_op jit(solution)/shard_map/ppermute | solution.py:15
  195.8 14.8 %collective-permute-start.27 = (bf16[128,2048]{1,0:T(8,128)(2,1)S(1)}, bf16[128,2048]{1,0:T(8,128)(2,1)S(1)}, u32[]{:S(2)}, u32[]{:S(2)}) collective-permute-start(bf16[128,2048]{1,0:T(8,128)(2,1)S(1)} %get-tuple-element.44), channel_id=1, source_target_pairs={{0,2},{2,0},{4,6},{6,4},{8,10},{10,8},{12,14},{14,12},{16,18},{18,... | collective-permute-start | bytes 1572872 | tf_op jit(solution)/shard_map/ppermute | solution.py:20
  196.5 32.0 %collective-permute-start.26 = (bf16[128,2048]{1,0:T(8,128)(2,1)S(1)}, bf16[128,2048]{1,0:T(8,128)(2,1)S(1)}, u32[]{:S(2)}, u32[]{:S(2)}) collective-permute-start(bf16[128,2048]{1,0:T(8,128)(2,1)S(1)} %get-tuple-element.42), channel_id=1, source_target_pairs={{0,2},{2,0},{4,6},{6,4},{8,10},{10,8},{12,14},{14,12},{16,18},{18,... | collective-permute-start | bytes 1572872 | tf_op jit(solution)/shard_map/ppermute | solution.py:20
  201.6 41.2 %collective-permute-start.25 = (bf16[128,2048]{1,0:T(8,128)(2,1)S(1)}, bf16[128,2048]{1,0:T(8,128)(2,1)S(1)}, u32[]{:S(2)}, u32[]{:S(2)}) collective-permute-start(bf16[128,2048]{1,0:T(8,128)(2,1)S(1)} %get-tuple-element.40), channel_id=1, source_target_pairs={{0,4},{2,6},{4,0},{6,2},{8,12},{10,14},{12,8},{14,10},{16,20},{18,... | collective-permute-start | bytes 1572872 | tf_op jit(solution)/shard_map/ppermute | solution.py:20
  202.1 25.6 %collective-permute-start.23 = (bf16[128,2048]{1,0:T(8,128)(2,1)S(1)}, bf16[128,2048]{1,0:T(8,128)(2,1)S(1)}, u32[]{:S(2)}, u32[]{:S(2)}) collective-permute-start(bf16[128,2048]{1,0:T(8,128)(2,1)S(1)} %get-tuple-element.39), channel_id=1, source_target_pairs={{0,4},{2,6},{4,0},{6,2},{8,12},{10,14},{12,8},{14,10},{16,20},{18,... | collective-permute-start | bytes 1572872 | tf_op jit(solution)/shard_map/ppermute | solution.py:20
  210.7 27.2 %collective-permute-start.28 = (bf16[128,2048]{1,0:T(8,128)(2,1)S(1)}, bf16[128,2048]{1,0:T(8,128)(2,1)S(1)}, u32[]{:S(2)}, u32[]{:S(2)}) collective-permute-start(bf16[128,2048]{1,0:T(8,128)(2,1)S(1)} %add_convert_fusion.4), channel_id=1, source_target_pairs={{0,4},{2,6},{4,0},{6,2},{8,12},{10,14},{12,8},{14,10},{16,20},{18,... | collective-permute-start | bytes 1572872 | tf_op jit(solution)/shard_map/ppermute | solution.py:20
  214.9 27.2 %collective-permute-start.21 = (bf16[128,2048]{1,0:T(8,128)(2,1)S(1)}, bf16[128,2048]{1,0:T(8,128)(2,1)S(1)}, u32[]{:S(2)}, u32[]{:S(2)}) collective-permute-start(bf16[128,2048]{1,0:T(8,128)(2,1)S(1)} %get-tuple-element.36), channel_id=1, source_target_pairs={{0,2},{2,0},{4,6},{6,4},{8,10},{10,8},{12,14},{14,12},{16,18},{18,... | collective-permute-start | bytes 1572872 | tf_op jit(solution)/shard_map/ppermute | solution.py:20
  227.7 30.3 %collective-permute-start.20 = (bf16[128,2048]{1,0:T(8,128)(2,1)S(1)}, bf16[128,2048]{1,0:T(8,128)(2,1)S(1)}, u32[]{:S(2)}, u32[]{:S(2)}) collective-permute-start(bf16[128,2048]{1,0:T(8,128)(2,1)S(1)} %get-tuple-element.34), channel_id=1, source_target_pairs={{0,2},{2,0},{4,6},{6,4},{8,10},{10,8},{12,14},{14,12},{16,18},{18,... | collective-permute-start | bytes 1572872 | tf_op jit(solution)/shard_map/ppermute | solution.py:20
  228.5 26.6 %collective-permute-start.24 = (bf16[128,2048]{1,0:T(8,128)(2,1)S(1)}, bf16[128,2048]{1,0:T(8,128)(2,1)S(1)}, u32[]{:S(2)}, u32[]{:S(2)}) collective-permute-start(bf16[128,2048]{1,0:T(8,128)(2,1)S(1)} %add_convert_fusion.5), channel_id=1, source_target_pairs={{0,2},{2,0},{4,6},{6,4},{8,10},{10,8},{12,14},{14,12},{16,18},{18,... | collective-permute-start | bytes 1572872 | tf_op jit(solution)/shard_map/ppermute | solution.py:20
  238.2 17.0 %collective-permute-start.29 = (bf16[128,2048]{1,0:T(8,128)(2,1)S(1)}, bf16[128,2048]{1,0:T(8,128)(2,1)S(1)}, u32[]{:S(2)}, u32[]{:S(2)}) collective-permute-start(bf16[128,2048]{1,0:T(8,128)(2,1)S(1)} %add_convert_fusion.3), channel_id=1, source_target_pairs={{0,24},{2,26},{4,28},{6,30},{8,0},{10,2},{12,4},{14,6},{16,8},{18,... | collective-permute-start | bytes 1572872 | tf_op jit(solution)/shard_map/ppermute | solution.py:25
  242.2 14.9 %collective-permute-start.17 = (bf16[128,2048]{1,0:T(8,128)(2,1)S(1)}, bf16[128,2048]{1,0:T(8,128)(2,1)S(1)}, u32[]{:S(2)}, u32[]{:S(2)}) collective-permute-start(bf16[128,2048]{1,0:T(8,128)(2,1)S(1)} %get-tuple-element.31), channel_id=1, source_target_pairs={{0,4},{2,6},{4,0},{6,2},{8,12},{10,14},{12,8},{14,10},{16,20},{18,... | collective-permute-start | bytes 1572872 | tf_op jit(solution)/shard_map/ppermute | solution.py:20
  242.8 25.5 %collective-permute-start.22 = (bf16[128,2048]{1,0:T(8,128)(2,1)S(1)}, bf16[128,2048]{1,0:T(8,128)(2,1)S(1)}, u32[]{:S(2)}, u32[]{:S(2)}) collective-permute-start(bf16[128,2048]{1,0:T(8,128)(2,1)S(1)} %add_convert_fusion.6), channel_id=1, source_target_pairs={{0,4},{2,6},{4,0},{6,2},{8,12},{10,14},{12,8},{14,10},{16,20},{18,... | collective-permute-start | bytes 1572872 | tf_op jit(solution)/shard_map/ppermute | solution.py:20
  255.6 22.1 %collective-permute-start.19 = (bf16[128,2048]{1,0:T(8,128)(2,1)S(1)}, bf16[128,2048]{1,0:T(8,128)(2,1)S(1)}, u32[]{:S(2)}, u32[]{:S(2)}) collective-permute-start(bf16[128,2048]{1,0:T(8,128)(2,1)S(1)} %get-tuple-element.32), channel_id=1, source_target_pairs={{0,4},{2,6},{4,0},{6,2},{8,12},{10,14},{12,8},{14,10},{16,20},{18,... | collective-permute-start | bytes 1572872 | tf_op jit(solution)/shard_map/ppermute | solution.py:20
  257.2 20.4 %collective-permute-start.18 = (bf16[128,2048]{1,0:T(8,128)(2,1)S(1)}, bf16[128,2048]{1,0:T(8,128)(2,1)S(1)}, u32[]{:S(2)}, u32[]{:S(2)}) collective-permute-start(bf16[128,2048]{1,0:T(8,128)(2,1)S(1)} %add_convert_fusion.7), channel_id=1, source_target_pairs={{0,2},{2,0},{4,6},{6,4},{8,10},{10,8},{12,14},{14,12},{16,18},{18,... | collective-permute-start | bytes 1572872 | tf_op jit(solution)/shard_map/ppermute | solution.py:20
  (7 other events, 120.8 us)

commit v3 on v2

v3 whole, which is shorter than its diff:
```python
import functools

import jax
import jax.numpy as jnp
from jax import lax
from jax.experimental import pallas as pl
from jax.experimental.pallas import tpu as pltpu
from jax.sharding import PartitionSpec as P

def swap_cores(x):
    size = lax.axis_size("dp")
    return lax.ppermute(x, "dp", [(i, i ^ 1) for i in range(size)])


def flip(x, bit):
    size = lax.axis_size("expert")
    return lax.ppermute(x, "expert", [(i, i ^ bit) for i in range(size)])


def turn(x, by):
    size = lax.axis_size("expert")
    return lax.ppermute(x, "expert", [(i, (i + 4 * by) % size) for i in range(size)])


def spread(w):
    return lax.all_to_all(w, "expert", split_axis=0, concat_axis=0, tiled=True)


def after(x, *others):
    return lax.optimization_barrier((x, *others))[0]


def hidden_kernel(blocks, rows, model, experts, place, *refs):
    tokens, weights = refs[:blocks], refs[blocks : blocks + 2]
    hidden, scale, held, loaded, token_sems, weight_sems = refs[blocks + 2 :]
    me, core = place[0], place[1]
    token_copies = [
        pltpu.make_async_copy(tokens[i], held.at[pl.ds(i * rows, rows)], token_sems.at[i]) for i in range(blocks)
    ]
    weight_copies = [pltpu.make_async_copy(weights[i], loaded.at[i], weight_sems.at[i]) for i in range(2)]
    for copy in token_copies[:4]:
        copy.start()
    weight_copies[0].start()
    for copy in token_copies[4:]:
        copy.start()
    weight_copies[1].start()
    group = 4 * rows
    piece = loaded.shape[2] // 2
    columns = held.shape[1] - model
    for side in range(2):
        start = pl.multiple_of(jnp.where(side == 0, core, 1 - core) * piece, 128)
        weight_copies[side].wait()
        for s in range(blocks // 4):
            if side == 0:
                for copy in token_copies[4 * s : 4 * s + 4]:
                    copy.wait()
            for half in range(2):
                at = pl.ds(s * group + half * group // 2, group // 2)
                if side == 0:
                    lane = lax.broadcasted_iota(jnp.int32, (group // 2, columns), 1)
                    wanted = (lane == me) | (lane == me + experts) | (lane == me + 2 * experts)
                    picked = jnp.where(wanted, held[at, model:].astype(jnp.float32), 0.0)
                    scale[at, :] = jnp.broadcast_to(jnp.sum(picked, axis=1, keepdims=True), (group // 2, 128))
                both = jnp.dot(held[at, :model], loaded[side], preferred_element_type=jnp.float32)
                gate, up = both[:, :piece], both[:, piece:]
                value = gate / (1.0 + jnp.exp(-gate)) * up
                hidden[at, pl.ds(start, piece)] = value.astype(jnp.bfloat16)


def out_kernel(rows, place, hidden, scale, own, other, *outs):
    core = place[1]
    part = own.shape[1]
    for side, w in ((0, own), (1, other)):
        start = pl.multiple_of(jnp.where(side == 0, core, 1 - core) * part, part)
        for c in range(0, part, 256):
            value = jnp.dot(hidden[...], w[:, c : c + 256], preferred_element_type=jnp.float32)
            value = (value * scale[:, :1]).astype(jnp.bfloat16)
            for q in range(4):
                outs[q][:, pl.ds(pl.multiple_of(start + c, 256), 256)] = value[q * rows : (q + 1) * rows]


def local(tokens, route_ids, route_weights, w_gate, w_up, w_down):
    devices = lax.axis_size("expert")
    experts, depth, width = w_gate.shape
    rows, model = tokens.shape
    line = devices // 4
    me = lax.axis_index("expert")
    core = lax.axis_index("dp") % 2
    place = jnp.stack([me, core]).astype(jnp.int32)
    half, part = width // 2, model // 2
    f32, bf16 = jnp.float32, jnp.bfloat16

    share = jnp.sum(
        jnp.where(
            route_ids[:, :, None] == jnp.arange(experts, dtype=jnp.int32)[None, None, :],
            route_weights[:, :, None],
            0.0,
        ),
        axis=1,
    )
    first = share.astype(bf16)
    rest = share - first.astype(f32)
    second = rest.astype(bf16)
    third = (rest - second.astype(f32)).astype(bf16)
    extra = jnp.concatenate([first, second, third], axis=1)
    extra = jnp.pad(extra, ((0, 0), (0, -(3 * experts) % 128)))
    tokens = jnp.concatenate([tokens, extra], axis=1)

    held, by_x, by_y, across = [tokens] + [None] * (line - 1), [None] * line, [None] * line, [None] * line

    def near(s):
        by_x[s], by_y[s] = flip(held[s], 1), flip(held[s], 2)

    def far(s):
        across[s] = flip(by_x[s], 2) if s % 2 == 0 else flip(by_y[s], 1)

    def settle(*extra):
        done = lax.optimization_barrier((held, by_x, by_y, across, extra))
        held[:], by_x[:], by_y[:], across[:] = done[:4]
        return done[4]

    at = core * half
    wide = jnp.concatenate([lax.dynamic_slice_in_dim(w, at, half, axis=2) for w in (w_gate, w_up)], axis=2)
    down = lax.dynamic_slice_in_dim(w_down, core * part, part, axis=2)
    for s in range(1, line):
        held[s] = turn(held[s - 1], 1)
        near(s - 1)
        wide, down = settle(wide, down)
    near(line - 1)
    for s in range(line - 1):
        far(s)
    wide = spread(wide)
    wide, down = settle(wide.reshape(devices * depth, width), down)
    down = spread(down)
    far(line - 1)
    wide_other = swap_cores(wide)
    down = down.reshape(width, part)

    any_spec = pl.BlockSpec(memory_space=pl.ANY)
    vmem_spec = pl.BlockSpec(memory_space=pltpu.VMEM)
    smem_spec = pl.BlockSpec(memory_space=pltpu.SMEM)
    group = 4 * rows

    def hidden_of(places):
        gathered = [b for s in places for b in (held[s], by_x[s], by_y[s], across[s])]
        count = len(gathered) * rows
        return pl.pallas_call(
            functools.partial(hidden_kernel, len(gathered), rows, model, experts),
            out_shape=[
                jax.ShapeDtypeStruct((count, width), bf16),
                jax.ShapeDtypeStruct((count, 128), f32),
            ],
            in_specs=[smem_spec] + [any_spec] * (len(gathered) + 2),
            out_specs=[vmem_spec, vmem_spec],
            scratch_shapes=[
                pltpu.VMEM((count, tokens.shape[1]), bf16),
                pltpu.VMEM((2, devices * depth, width), bf16),
                pltpu.SemaphoreType.DMA((len(gathered),)),
                pltpu.SemaphoreType.DMA((2,)),
            ],
            compiler_params=pltpu.CompilerParams(vmem_limit_bytes=48 * 1024 * 1024),
            cost_estimate=pl.CostEstimate(
                flops=4 * count * model * width, bytes_accessed=10_000_000, transcendentals=count * width
            ),
            name="hidden",
        )(place, *gathered, wide, wide_other)

    hidden, scale = {}, {}

    def work(places):
        h, w = hidden_of(places)
        for i, s in enumerate(places):
            hidden[s], scale[s] = (h, i), (w, i)
        return h

    first = work(range(line - 1))
    wide, wide_other = lax.optimization_barrier((wide, wide_other, first))[:2]
    second = work(range(line - 1, line))
    down_other = swap_cores(after(down, second))
    outs = [None] * line
    for s in reversed(range(line)):
        outs[s] = pl.pallas_call(
            functools.partial(out_kernel, rows),
            out_shape=[jax.ShapeDtypeStruct((rows, model), bf16)] * 4,
            grid=(1,),
            in_specs=[
                smem_spec,
                pl.BlockSpec((group, width), lambda i, s=hidden[s][1]: (s, 0)),
                pl.BlockSpec((group, 128), lambda i, s=scale[s][1]: (s, 0)),
                pl.BlockSpec((width, part), lambda i: (0, 0)),
                pl.BlockSpec((width, part), lambda i: (0, 0)),
            ],
            out_specs=[pl.BlockSpec((rows, model), lambda i: (0, 0))] * 4,
            compiler_params=pltpu.CompilerParams(vmem_limit_bytes=32 * 1024 * 1024),
            cost_estimate=pl.CostEstimate(
                flops=2 * group * model * width, bytes_accessed=6_500_000, transcendentals=0
            ),
            name="out",
        )(place, hidden[s][0], scale[s][0], down, down_other)
    def add(*terms):
        return sum(term.astype(f32) for term in terms).astype(bf16)

    beside = [None] * line
    for s in range(1, line, 2):
        beside[s] = turn(outs[s][3], -1)
    total = None
    from_x, from_y = [None] * line, [None] * line
    for s in reversed(range(line)):
        kept, to_x, to_y, over = outs[s]
        if s % 2 == 0 and s + 1 < line:
            over = add(over, beside[s + 1])
        if s % 4 == 0:
            to_x = add(to_x, flip(over, 2))
        elif s % 2 == 0:
            to_y = add(to_y, flip(over, 1))
        from_x[s], from_y[s] = flip(to_x, 1), flip(to_y, 2)
    for s in reversed(range(line)):
        terms = [outs[s][0], from_x[s], from_y[s]]
        total = add(*terms) if s == line - 1 else add(*terms, turn(total, -1))
    return total


def solution(mesh):
    placed = (
        P(("dp", "expert"), None),
        P(("dp", "expert"), None),
        P(("dp", "expert"), None),
        P(None, "expert", None),
        P(None, "expert", None),
        P(None, "expert", None),
    )
    return jax.shard_map(
        local, mesh=mesh, in_specs=placed, out_specs=P(("dp", "expert"), None), check_vma=False
    )
```

time: 285 us -> 261 us (0.916); the launches traced: 283 us -> 256 us
  waiting for transfers between devices: 185 us -> 151 us
  local copies, waits for them, and re-layouts: 8.72 us -> 20.1 us
  starting transfers between devices: 45.4 us -> 41.9 us
    all_to_all x2, waiting for transfers between devices: 33.6 us -> 3.09 us  [spread(): return lax.all_to_all(w, 'expert', split_axis=0, concat_axis=0, tiled=True)]
    ppermute x24 -> x22, waiting for transfers between devices: 123 us -> 110 us  [flip(): return lax.ppermute(x, 'expert', [(i, i ^ bit) for i in range(size)])]
    unnamed x10 -> x48, local copies, waits for them, and re-layouts: 4.97 us -> 16.7 us
    ppermute x6 -> x8, waiting for transfers between devices: 28.2 us -> 35 us  [turn(): lax.ppermute(x, 'expert', [(i, (i + 4 * by) % size) for i in range(size)])]
    ppermute x24 -> x22, starting transfers between devices: 25.3 us -> 18.7 us  [flip(): return lax.ppermute(x, 'expert', [(i, i ^ bit) for i in range(size)])]
    ppermute x2, waiting for transfers between devices: 0.01 us -> 3.62 us  [swap_cores(): return lax.ppermute(x, 'dp', [(i, i ^ 1) for i in range(size)])]
    ppermute x6 -> x8, starting transfers between devices: 5.69 us -> 8.39 us  [turn(): lax.ppermute(x, 'expert', [(i, (i + 4 * by) % size) for i in range(size)])]
    pallas_call x1 -> x2, Pallas kernels: 21.6 us -> 21.6 us  [hidden_of(): pl.pallas_call(functools.partial(hidden_kernel, len(gathered), rows, mode...]
  transfers between devices with their start and end apart: 34 -> 34, of which waited for: 20 -> 21; matrix products, arithmetic and copies ran while one was open for 3% -> 3% of each run, Pallas kernels for 12% -> 12%
where the time goes in v3:
time: 261 us; the launch traced here: 256 us
  waiting for transfers between devices  151 us (58%)
  starting transfers between devices  41.9 us (16%)
  Pallas kernels  34.7 us (13%)
  local copies, waits for them, and re-layouts  20.1 us (8%)
  other arithmetic  7.52 us (3%)
    ppermute x22, waiting for transfers between devices, flip(): return lax.ppermute(x, 'expert', [(i, i ^ bit) for i in range(size)])  110 us
    ppermute x8, waiting for transfers between devices, turn(): lax.ppermute(x, 'expert', [(i, (i + 4 * by) % size) for i in range(size)])  35 us
    pallas_call x2, Pallas kernels, hidden_of(): pl.pallas_call(functools.partial(hidden_kernel, len(gathered), rows, mode...  21.6 us
    ppermute x22, starting transfers between devices, flip(): return lax.ppermute(x, 'expert', [(i, i ^ bit) for i in range(size)])  18.7 us
    unnamed x48, local copies, waits for them, and re-layouts  16.7 us
    all_to_all x2, starting transfers between devices, spread(): return lax.all_to_all(w, 'expert', split_axis=0, concat_axis=0, tiled=True)  14.8 us
    pallas_call x4, Pallas kernels, local(): pl.pallas_call(functools.partial(out_kernel, rows), out_shape=[jax.ShapeD...  13.2 us
    ppermute x8, starting transfers between devices, turn(): lax.ppermute(x, 'expert', [(i, (i + 4 * by) % size) for i in range(size)])  8.39 us
  transfers between devices with their start and end apart: 34, of which 21 were waited for; matrix products, arithmetic and copies ran while one was open for 3% of the time, Pallas kernels for 12%

profile of v3, /device:TPU:12, one launch (start us, length us, event | category | flops | bytes accessed | tf_op | source)
XLA Modules:
  0.0 255.8 jit_solution(8779698117289940362)
XLA Ops:
  1.0 1.9 fusion.1.refs_0_
  2.9 1.6 collective-permute-start
  4.5 1.5 collective-permute-start.1
  9.0 1.9 constant_dynamic-slice_fusion.1
  10.9 2.1 pad_maximum_fusion
  13.0 4.6 %collective-permute-done.refs_4_ = bf16[128,2176]{1,0:T(8,128)(2,1)} collective-permute-done((bf16[128,2176]{1,0:T(8,128)(2,1)}, bf16[128,2176]{1,0:T(8,128)(2,1)}, u32[]{:S(2)}, u32[]{:S(2)}) %collective-permute-start) | collective-permute-done | bytes 557088 | tf_op jit(solution)/shard_map/ppermute | solution.py:22
  20.1 1.6 collective-permute-start.3
  22.7 10.5 %collective-permute-done.3.refs_8_ = bf16[128,2176]{1,0:T(8,128)(2,1)S(1)} collective-permute-done((bf16[128,2176]{1,0:T(8,128)(2,1)}, bf16[128,2176]{1,0:T(8,128)(2,1)S(1)}, u32[]{:S(2)}, u32[]{:S(2)}) %collective-permute-start.3) | collective-permute-done | bytes 557088 | tf_op jit(solution)/shard_map/ppermute | solution.py:22
  37.9 9.1 %collective-permute-done.6.refs_0_ = bf16[128,2176]{1,0:T(8,128)(2,1)S(1)} collective-permute-done((bf16[128,2176]{1,0:T(8,128)(2,1)S(1)}, bf16[128,2176]{1,0:T(8,128)(2,1)S(1)}, u32[]{:S(2)}, u32[]{:S(2)}) %collective-permute-start.6) | collective-permute-done | bytes 557088 | tf_op jit(solution)/shard_map/ppermute | solution.py:22
  49.4 7.8 %all-to-all-start = ((bf16[16,128,768]{2,1,0:T(8,128)(2,1)}), bf16[16,128,768]{2,1,0:T(8,128)(2,1)}, u32[]{:S(2)}, u32[]{:S(2)}) async-start(bf16[16,128,768]{2,1,0:T(8,128)(2,1)} %pad_maximum_fusion), calls=%async_computation | async-start | bytes 6291456 | tf_op jit(solution)/shard_map/all_to_all | solution.py:26
  59.3 1.5 collective-permute-start.12
  61.9 26.7 %collective-permute-done.10.refs_2_ = bf16[128,2176]{1,0:T(8,128)(2,1)} collective-permute-done((bf16[128,2176]{1,0:T(8,128)(2,1)}, bf16[128,2176]{1,0:T(8,128)(2,1)}, u32[]{:S(2)}, u32[]{:S(2)}) %collective-permute-start.10) | collective-permute-done | bytes 557088 | tf_op jit(solution)/shard_map/ppermute | solution.py:17
  88.6 21.4 %collective-permute-done.11.refs_3_ = bf16[128,2176]{1,0:T(8,128)(2,1)S(1)} collective-permute-done((bf16[128,2176]{1,0:T(8,128)(2,1)}, bf16[128,2176]{1,0:T(8,128)(2,1)S(1)}, u32[]{:S(2)}, u32[]{:S(2)}) %collective-permute-start.11) | collective-permute-done | bytes 557088 | tf_op jit(solution)/shard_map/ppermute | solution.py:17
  111.6 13.4 %collective-permute-done.13.refs_11_ = bf16[128,2176]{1,0:T(8,128)(2,1)} collective-permute-done((bf16[128,2176]{1,0:T(8,128)(2,1)}, bf16[128,2176]{1,0:T(8,128)(2,1)}, u32[]{:S(2)}, u32[]{:S(2)}) %collective-permute-start.13) | collective-permute-done | bytes 557088 | tf_op jit(solution)/shard_map/ppermute | solution.py:17
  125.8 7.0 %all-to-all-start.1 = ((bf16[16,48,1024]{2,1,0:T(8,128)(2,1)}), bf16[16,48,1024]{2,1,0:T(8,128)(2,1)}, u32[]{:S(2)}, u32[]{:S(2)}) async-start(bf16[16,48,1024]{2,1,0:T(8,128)(2,1)} %constant_dynamic-slice_fusion), calls=%async_computation.1 | async-start | bytes 3145728 | tf_op jit(solution)/shard_map/all_to_all | solution.py:26
  141.7 15.0 %hidden.2 = (bf16[1536,768]{1,0:T(8,128)(2,1)}, f32[1536,128]{1,0:T(8,128)}) custom-call(s32[2]{0:T(128)S(1)} %pad_add_fusion.place, bf16[128,2176]{1,0:T(8,128)(2,1)} %fusion.1.refs_0_, bf16[128,2176]{1,0:T(8,128)(2,1)} %collective-permute-done.1.refs_1_, bf16[128,2176]{1,0:T(8,128)(2,1)} %collective-permute-done.2.refs_2_, ...), custom_call_target="tpu_custom_call" | custom-call | flops 9663676416 | bytes 10000000 | tf_op jit(solution)/shard_map/hidden/pallas_call | solution.py:147
  156.7 3.2 %collective-permute-done.15.refs_3_ = bf16[128,2176]{1,0:T(8,128)(2,1)S(1)} collective-permute-done((bf16[128,2176]{1,0:T(8,128)(2,1)}, bf16[128,2176]{1,0:T(8,128)(2,1)S(1)}, u32[]{:S(2)}, u32[]{:S(2)}) %collective-permute-start.15) | collective-permute-done | bytes 557088 | tf_op jit(solution)/shard_map/ppermute | solution.py:17
  159.9 6.6 %hidden.3 = (bf16[512,768]{1,0:T(8,128)(2,1)S(1)}, f32[512,128]{1,0:T(8,128)S(1)}) custom-call(s32[2]{0:T(128)S(1)} %pad_add_fusion.place, bf16[128,2176]{1,0:T(8,128)(2,1)S(1)} %copy-done.10, bf16[128,2176]{1,0:T(8,128)(2,1)S(1)} %copy-done.18, bf16[128,2176]{1,0:T(8,128)(2,1)} %collective-permute-done.10.refs_2_, ...), custom_call_target="tpu_custom_call" | custom-call | flops 3221225472 | bytes 10000000 | tf_op jit(solution)/shard_map/hidden/pallas_call | solution.py:147
  167.4 3.1 %all-to-all-done.1 = bf16[16,48,1024]{2,1,0:T(8,128)(2,1)} async-done(((bf16[16,48,1024]{2,1,0:T(8,128)(2,1)}), bf16[16,48,1024]{2,1,0:T(8,128)(2,1)}, u32[]{:S(2)}, u32[]{:S(2)}) %all-to-all-start.1) | async-done | bytes 1572896 | tf_op jit(solution)/shard_map/all_to_all | solution.py:26
  170.5 3.6 %collective-permute-done.16.other = bf16[768,1024]{1,0:T(8,128)(2,1)S(1)} collective-permute-done((bf16[768,1024]{1,0:T(8,128)(2,1)}, bf16[768,1024]{1,0:T(8,128)(2,1)S(1)}, u32[]{:S(2)}, u32[]{:S(2)}) %collective-permute-start.16) | collective-permute-done | bytes 1572896 | tf_op jit(solution)/shard_map/ppermute | solution.py:12
  175.2 3.4 %out.7 = (bf16[128,2048]{1,0:T(8,128)(2,1)S(1)}, bf16[128,2048]{1,0:T(8,128)(2,1)S(1)}, bf16[128,2048]{1,0:T(8,128)(2,1)S(1)}, bf16[128,2048]{1,0:T(8,128)(2,1)S(1)}) custom-call(s32[2]{0:T(128)S(1)} %pad_add_fusion.place, bf16[512,768]{1,0:T(8,128)(2,1)S(1)} %copy-done.22, f32[512,128]{1,0:T(8,128)S(1)} %get-tuple-element.134.scale, ...), custom_call_target="tpu_custom_call" | custom-call | flops 1610612736 | bytes 6500000 | tf_op jit(solution)/shard_map/out/pallas_call | solution.py:182
  180.0 3.2 %out.6 = (bf16[128,2048]{1,0:T(8,128)(2,1)S(1)}, bf16[128,2048]{1,0:T(8,128)(2,1)S(1)}, bf16[128,2048]{1,0:T(8,128)(2,1)S(1)}, bf16[128,2048]{1,0:T(8,128)(2,1)S(1)}) custom-call(s32[2]{0:T(128)S(1)} %pad_add_fusion.place, bf16[1536,768]{1,0:T(8,128)(2,1)S(1)} %copy-done.1, f32[1536,128]{1,0:T(8,128)S(1)} %copy-done.2, bf16[768,1024]{1,0:T(8,128)(2,1)} %bitcast.3.own, ...), custom_call_target="tpu_custom_call" | custom-call | flops 1610612736 | bytes 6500000 | tf_op jit(solution)/shard_map/out/pallas_call | solution.py:182
  183.3 10.0 %collective-permute-done.24 = bf16[128,2048]{1,0:T(8,128)(2,1)S(1)} collective-permute-done((bf16[128,2048]{1,0:T(8,128)(2,1)S(1)}, bf16[128,2048]{1,0:T(8,128)(2,1)S(1)}, u32[]{:S(2)}, u32[]{:S(2)}) %collective-permute-start.24) | collective-permute-done | bytes 524320 | tf_op jit(solution)/shard_map/ppermute | solution.py:22
  194.1 3.2 %out.5 = (bf16[128,2048]{1,0:T(8,128)(2,1)S(1)}, bf16[128,2048]{1,0:T(8,128)(2,1)S(1)}, bf16[128,2048]{1,0:T(8,128)(2,1)S(1)}, bf16[128,2048]{1,0:T(8,128)(2,1)S(1)}) custom-call(s32[2]{0:T(128)S(1)} %pad_add_fusion.place, bf16[1536,768]{1,0:T(8,128)(2,1)S(1)} %copy-done.1, f32[1536,128]{1,0:T(8,128)S(1)} %copy-done.2, bf16[768,1024]{1,0:T(8,128)(2,1)} %bitcast.3.own, ...), custom_call_target="tpu_custom_call" | custom-call | flops 1610612736 | bytes 6500000 | tf_op jit(solution)/shard_map/out/pallas_call | solution.py:182
  199.9 3.8 %collective-permute-start.29 = (bf16[128,2048]{1,0:T(8,128)(2,1)S(1)}, bf16[128,2048]{1,0:T(8,128)(2,1)S(1)}, u32[]{:S(2)}, u32[]{:S(2)}) collective-permute-start(bf16[128,2048]{1,0:T(8,128)(2,1)S(1)} %add_convert_fusion.3), channel_id=1, source_target_pairs={{0,24},{2,26},{4,28},{6,30},{8,0},{10,2},{12,4},{14,6},{16,8},{18,... | collective-permute-start | bytes 1572872 | tf_op jit(solution)/shard_map/ppermute | solution.py:22
  203.8 4.6 %collective-permute-done.25 = bf16[128,2048]{1,0:T(8,128)(2,1)S(1)} collective-permute-done((bf16[128,2048]{1,0:T(8,128)(2,1)S(1)}, bf16[128,2048]{1,0:T(8,128)(2,1)S(1)}, u32[]{:S(2)}, u32[]{:S(2)}) %collective-permute-start.25) | collective-permute-done | bytes 524320 | tf_op jit(solution)/shard_map/ppermute | solution.py:17
  208.5 3.3 %out.4 = (bf16[128,2048]{1,0:T(8,128)(2,1)S(1)}, bf16[128,2048]{1,0:T(8,128)(2,1)S(1)}, bf16[128,2048]{1,0:T(8,128)(2,1)S(1)}, bf16[128,2048]{1,0:T(8,128)(2,1)S(1)}) custom-call(s32[2]{0:T(128)S(1)} %pad_add_fusion.place, bf16[1536,768]{1,0:T(8,128)(2,1)S(1)} %copy-done.1, f32[1536,128]{1,0:T(8,128)S(1)} %copy-done.2, bf16[768,1024]{1,0:T(8,128)(2,1)} %bitcast.3.own, ...), custom_call_target="tpu_custom_call" | custom-call | flops 1610612736 | bytes 6500000 | tf_op jit(solution)/shard_map/out/pallas_call | solution.py:182
  212.2 1.6 collective-permute-start.22
  214.0 15.4 %collective-permute-done.23 = bf16[128,2048]{1,0:T(8,128)(2,1)S(1)} collective-permute-done((bf16[128,2048]{1,0:T(8,128)(2,1)S(1)}, bf16[128,2048]{1,0:T(8,128)(2,1)S(1)}, u32[]{:S(2)}, u32[]{:S(2)}) %collective-permute-start.23) | collective-permute-done | bytes 524320 | tf_op jit(solution)/shard_map/ppermute | solution.py:17
  229.8 2.1 collective-permute-start.20
  231.9 12.4 %collective-permute-done.18 = bf16[128,2048]{1,0:T(8,128)(2,1)S(1)} collective-permute-done((bf16[128,2048]{1,0:T(8,128)(2,1)S(1)}, bf16[128,2048]{1,0:T(8,128)(2,1)S(1)}, u32[]{:S(2)}, u32[]{:S(2)}) %collective-permute-start.18) | collective-permute-done | bytes 524320 | tf_op jit(solution)/shard_map/ppermute | solution.py:17
  245.8 7.7 %collective-permute-done.20 = bf16[128,2048]{1,0:T(8,128)(2,1)S(1)} collective-permute-done((bf16[128,2048]{1,0:T(8,128)(2,1)S(1)}, bf16[128,2048]{1,0:T(8,128)(2,1)S(1)}, u32[]{:S(2)}, u32[]{:S(2)}) %collective-permute-start.20) | collective-permute-done | bytes 524320 | tf_op jit(solution)/shard_map/ppermute | solution.py:17
  (107 shorter events, 41.0 us)
Async XLA Ops:
  2.9 14.7 %collective-permute-start = (bf16[128,2176]{1,0:T(8,128)(2,1)}, bf16[128,2176]{1,0:T(8,128)(2,1)}, u32[]{:S(2)}, u32[]{:S(2)}) collective-permute-start(bf16[128,2176]{1,0:T(8,128)(2,1)} %fusion.1.refs_0_), channel_id=1, source_target_pairs={{0,8},{2,10},{4,12},{6,14},{8,16},{10,18},{12,20},{14,22},{16,24},... | collective-permute-start | bytes 1671176 | tf_op jit(solution)/shard_map/ppermute | solution.py:22
  4.5 14.4 %collective-permute-start.1 = (bf16[128,2176]{1,0:T(8,128)(2,1)}, bf16[128,2176]{1,0:T(8,128)(2,1)}, u32[]{:S(2)}, u32[]{:S(2)}) collective-permute-start(bf16[128,2176]{1,0:T(8,128)(2,1)} %fusion.1.refs_0_), channel_id=1, source_target_pairs={{0,2},{2,0},{4,6},{6,4},{8,10},{10,8},{12,14},{14,12},{16,18},{18,... | collective-permute-start | bytes 1671176 | tf_op jit(solution)/shard_map/ppermute | solution.py:17
  6.0 14.1 %collective-permute-start.2 = (bf16[128,2176]{1,0:T(8,128)(2,1)}, bf16[128,2176]{1,0:T(8,128)(2,1)}, u32[]{:S(2)}, u32[]{:S(2)}) collective-permute-start(bf16[128,2176]{1,0:T(8,128)(2,1)} %fusion.1.refs_0_), channel_id=1, source_target_pairs={{0,4},{2,6},{4,0},{6,2},{8,12},{10,14},{12,8},{14,10},{16,20},{18,... | collective-permute-start | bytes 1671176 | tf_op jit(solution)/shard_map/ppermute | solution.py:17
  20.1 13.1 %collective-permute-start.3 = (bf16[128,2176]{1,0:T(8,128)(2,1)}, bf16[128,2176]{1,0:T(8,128)(2,1)S(1)}, u32[]{:S(2)}, u32[]{:S(2)}) collective-permute-start(bf16[128,2176]{1,0:T(8,128)(2,1)} %collective-permute-done.refs_4_), channel_id=1, source_target_pairs={{0,8},{2,10},{4,12},{6,14},{8,16},{10,18},{12,20},{14,22},{16,24},... | collective-permute-start | bytes 1671176 | tf_op jit(solution)/shard_map/ppermute | solution.py:22
  21.7 12.8 %collective-permute-start.4 = (bf16[128,2176]{1,0:T(8,128)(2,1)}, bf16[128,2176]{1,0:T(8,128)(2,1)S(1)}, u32[]{:S(2)}, u32[]{:S(2)}) collective-permute-start(bf16[128,2176]{1,0:T(8,128)(2,1)} %collective-permute-done.refs_4_), channel_id=1, source_target_pairs={{0,2},{2,0},{4,6},{6,4},{8,10},{10,8},{12,14},{14,12},{16,18},{18,... | collective-permute-start | bytes 1671176 | tf_op jit(solution)/shard_map/ppermute | solution.py:17
  22.2 13.1 %collective-permute-start.5 = (bf16[128,2176]{1,0:T(8,128)(2,1)}, bf16[128,2176]{1,0:T(8,128)(2,1)S(1)}, u32[]{:S(2)}, u32[]{:S(2)}) collective-permute-start(bf16[128,2176]{1,0:T(8,128)(2,1)} %collective-permute-done.refs_4_), channel_id=1, source_target_pairs={{0,4},{2,6},{4,0},{6,2},{8,12},{10,14},{12,8},{14,10},{16,20},{18,... | collective-permute-start | bytes 1671176 | tf_op jit(solution)/shard_map/ppermute | solution.py:17
  35.3 11.7 %collective-permute-start.6 = (bf16[128,2176]{1,0:T(8,128)(2,1)S(1)}, bf16[128,2176]{1,0:T(8,128)(2,1)S(1)}, u32[]{:S(2)}, u32[]{:S(2)}) collective-permute-start(bf16[128,2176]{1,0:T(8,128)(2,1)S(1)} %collective-permute-done.3.refs_8_), channel_id=1, source_target_pairs={{0,8},{2,10},{4,12},{6,14},{8,16},{10,18},{12,20},{14,22},{16,24},... | collective-permute-start | bytes 1671176 | tf_op jit(solution)/shard_map/ppermute | solution.py:22
  35.7 11.6 %collective-permute-start.7 = (bf16[128,2176]{1,0:T(8,128)(2,1)S(1)}, bf16[128,2176]{1,0:T(8,128)(2,1)S(1)}, u32[]{:S(2)}, u32[]{:S(2)}) collective-permute-start(bf16[128,2176]{1,0:T(8,128)(2,1)S(1)} %collective-permute-done.3.refs_8_), channel_id=1, source_target_pairs={{0,2},{2,0},{4,6},{6,4},{8,10},{10,8},{12,14},{14,12},{16,18},{18,... | collective-permute-start | bytes 1671176 | tf_op jit(solution)/shard_map/ppermute | solution.py:17
  36.6 12.0 %collective-permute-start.8 = (bf16[128,2176]{1,0:T(8,128)(2,1)S(1)}, bf16[128,2176]{1,0:T(8,128)(2,1)S(1)}, u32[]{:S(2)}, u32[]{:S(2)}) collective-permute-start(bf16[128,2176]{1,0:T(8,128)(2,1)S(1)} %collective-permute-done.3.refs_8_), channel_id=1, source_target_pairs={{0,4},{2,6},{4,0},{6,2},{8,12},{10,14},{12,8},{14,10},{16,20},{18,... | collective-permute-start | bytes 1671176 | tf_op jit(solution)/shard_map/ppermute | solution.py:17
  49.4 76.4 %all-to-all-start = ((bf16[16,128,768]{2,1,0:T(8,128)(2,1)}), bf16[16,128,768]{2,1,0:T(8,128)(2,1)}, u32[]{:S(2)}, u32[]{:S(2)}) async-start(bf16[16,128,768]{2,1,0:T(8,128)(2,1)} %pad_maximum_fusion), calls=%async_computation | async-start | bytes 6291456 | tf_op jit(solution)/shard_map/all_to_all | solution.py:26
  57.2 31.3 %collective-permute-start.10 = (bf16[128,2176]{1,0:T(8,128)(2,1)}, bf16[128,2176]{1,0:T(8,128)(2,1)}, u32[]{:S(2)}, u32[]{:S(2)}) collective-permute-start(bf16[128,2176]{1,0:T(8,128)(2,1)} %copy-done.9), channel_id=1, source_target_pairs={{0,4},{2,6},{4,0},{6,2},{8,12},{10,14},{12,8},{14,10},{16,20},{18,... | collective-permute-start | bytes 1671176 | tf_op jit(solution)/shard_map/ppermute | solution.py:17
  57.8 52.2 %collective-permute-start.11 = (bf16[128,2176]{1,0:T(8,128)(2,1)}, bf16[128,2176]{1,0:T(8,128)(2,1)S(1)}, u32[]{:S(2)}, u32[]{:S(2)}) collective-permute-start(bf16[128,2176]{1,0:T(8,128)(2,1)} %collective-permute-done.1.refs_1_), channel_id=1, source_target_pairs={{0,4},{2,6},{4,0},{6,2},{8,12},{10,14},{12,8},{14,10},{16,20},{18,... | collective-permute-start | bytes 1671176 | tf_op jit(solution)/shard_map/ppermute | solution.py:17
  59.3 51.5 %collective-permute-start.12 = (bf16[128,2176]{1,0:T(8,128)(2,1)}, bf16[128,2176]{1,0:T(8,128)(2,1)S(1)}, u32[]{:S(2)}, u32[]{:S(2)}) collective-permute-start(bf16[128,2176]{1,0:T(8,128)(2,1)} %copy-done.7), channel_id=1, source_target_pairs={{0,2},{2,0},{4,6},{6,4},{8,10},{10,8},{12,14},{14,12},{16,18},{18,... | collective-permute-start | bytes 1671176 | tf_op jit(solution)/shard_map/ppermute | solution.py:17
  60.7 64.3 %collective-permute-start.13 = (bf16[128,2176]{1,0:T(8,128)(2,1)}, bf16[128,2176]{1,0:T(8,128)(2,1)}, u32[]{:S(2)}, u32[]{:S(2)}) collective-permute-start(bf16[128,2176]{1,0:T(8,128)(2,1)} %copy-done.11), channel_id=1, source_target_pairs={{0,4},{2,6},{4,0},{6,2},{8,12},{10,14},{12,8},{14,10},{16,20},{18,... | collective-permute-start | bytes 1671176 | tf_op jit(solution)/shard_map/ppermute | solution.py:17
  61.3 63.7 %collective-permute-start.9 = (bf16[128,2176]{1,0:T(8,128)(2,1)}, bf16[128,2176]{1,0:T(8,128)(2,1)S(1)}, u32[]{:S(2)}, u32[]{:S(2)}) collective-permute-start(bf16[128,2176]{1,0:T(8,128)(2,1)} %copy-done.9), channel_id=1, source_target_pairs={{0,2},{2,0},{4,6},{6,4},{8,10},{10,8},{12,14},{14,12},{16,18},{18,... | collective-permute-start | bytes 1671176 | tf_op jit(solution)/shard_map/ppermute | solution.py:17
  125.8 44.6 %all-to-all-start.1 = ((bf16[16,48,1024]{2,1,0:T(8,128)(2,1)}), bf16[16,48,1024]{2,1,0:T(8,128)(2,1)}, u32[]{:S(2)}, u32[]{:S(2)}) async-start(bf16[16,48,1024]{2,1,0:T(8,128)(2,1)} %constant_dynamic-slice_fusion), calls=%async_computation.1 | async-start | bytes 3145728 | tf_op jit(solution)/shard_map/all_to_all | solution.py:26
  132.9 27.0 %collective-permute-start.15 = (bf16[128,2176]{1,0:T(8,128)(2,1)}, bf16[128,2176]{1,0:T(8,128)(2,1)S(1)}, u32[]{:S(2)}, u32[]{:S(2)}) collective-permute-start(bf16[128,2176]{1,0:T(8,128)(2,1)} %collective-permute-done.10.refs_2_), channel_id=1, source_target_pairs={{0,2},{2,0},{4,6},{6,4},{8,10},{10,8},{12,14},{14,12},{16,18},{18,... | collective-permute-start | bytes 1671176 | tf_op jit(solution)/shard_map/ppermute | solution.py:17
  178.6 14.7 %collective-permute-start.24 = (bf16[128,2048]{1,0:T(8,128)(2,1)S(1)}, bf16[128,2048]{1,0:T(8,128)(2,1)S(1)}, u32[]{:S(2)}, u32[]{:S(2)}) collective-permute-start(bf16[128,2048]{1,0:T(8,128)(2,1)S(1)} %get-tuple-element.135), channel_id=1, source_target_pairs={{0,24},{2,26},{4,28},{6,30},{8,0},{10,2},{12,4},{14,6},{16,8},{18,... | collective-permute-start | bytes 1572872 | tf_op jit(solution)/shard_map/ppermute | solution.py:22
  178.7 20.2 %collective-permute-start.27 = (bf16[128,2048]{1,0:T(8,128)(2,1)S(1)}, bf16[128,2048]{1,0:T(8,128)(2,1)S(1)}, u32[]{:S(2)}, u32[]{:S(2)}) collective-permute-start(bf16[128,2048]{1,0:T(8,128)(2,1)S(1)} %get-tuple-element.137), channel_id=1, source_target_pairs={{0,2},{2,0},{4,6},{6,4},{8,10},{10,8},{12,14},{14,12},{16,18},{18,... | collective-permute-start | bytes 1572872 | tf_op jit(solution)/shard_map/ppermute | solution.py:17
  180.0 19.7 %collective-permute-start.28 = (bf16[128,2048]{1,0:T(8,128)(2,1)S(1)}, bf16[128,2048]{1,0:T(8,128)(2,1)S(1)}, u32[]{:S(2)}, u32[]{:S(2)}) collective-permute-start(bf16[128,2048]{1,0:T(8,128)(2,1)S(1)} %get-tuple-element.138), channel_id=1, source_target_pairs={{0,4},{2,6},{4,0},{6,2},{8,12},{10,14},{12,8},{14,10},{16,20},{18,... | collective-permute-start | bytes 1572872 | tf_op jit(solution)/shard_map/ppermute | solution.py:17
  193.4 14.9 %collective-permute-start.25 = (bf16[128,2048]{1,0:T(8,128)(2,1)S(1)}, bf16[128,2048]{1,0:T(8,128)(2,1)S(1)}, u32[]{:S(2)}, u32[]{:S(2)}) collective-permute-start(bf16[128,2048]{1,0:T(8,128)(2,1)S(1)} %add_convert_fusion.5), channel_id=1, source_target_pairs={{0,2},{2,0},{4,6},{6,4},{8,10},{10,8},{12,14},{14,12},{16,18},{18,... | collective-permute-start | bytes 1572872 | tf_op jit(solution)/shard_map/ppermute | solution.py:17
  197.3 14.9 %collective-permute-start.17 = (bf16[128,2048]{1,0:T(8,128)(2,1)S(1)}, bf16[128,2048]{1,0:T(8,128)(2,1)S(1)}, u32[]{:S(2)}, u32[]{:S(2)}) collective-permute-start(bf16[128,2048]{1,0:T(8,128)(2,1)S(1)} %get-tuple-element.125), channel_id=1, source_target_pairs={{0,24},{2,26},{4,28},{6,30},{8,0},{10,2},{12,4},{14,6},{16,8},{18,... | collective-permute-start | bytes 1572872 | tf_op jit(solution)/shard_map/ppermute | solution.py:22
  197.7 47.1 %collective-permute-start.21 = (bf16[128,2048]{1,0:T(8,128)(2,1)S(1)}, bf16[128,2048]{1,0:T(8,128)(2,1)S(1)}, u32[]{:S(2)}, u32[]{:S(2)}) collective-permute-start(bf16[128,2048]{1,0:T(8,128)(2,1)S(1)} %get-tuple-element.128), channel_id=1, source_target_pairs={{0,2},{2,0},{4,6},{6,4},{8,10},{10,8},{12,14},{14,12},{16,18},{18,... | collective-permute-start | bytes 1572872 | tf_op jit(solution)/shard_map/ppermute | solution.py:17
  198.9 30.5 %collective-permute-start.23 = (bf16[128,2048]{1,0:T(8,128)(2,1)S(1)}, bf16[128,2048]{1,0:T(8,128)(2,1)S(1)}, u32[]{:S(2)}, u32[]{:S(2)}) collective-permute-start(bf16[128,2048]{1,0:T(8,128)(2,1)S(1)} %get-tuple-element.131), channel_id=1, source_target_pairs={{0,2},{2,0},{4,6},{6,4},{8,10},{10,8},{12,14},{14,12},{16,18},{18,... | collective-permute-start | bytes 1572872 | tf_op jit(solution)/shard_map/ppermute | solution.py:17
  199.9 29.5 %collective-permute-start.29 = (bf16[128,2048]{1,0:T(8,128)(2,1)S(1)}, bf16[128,2048]{1,0:T(8,128)(2,1)S(1)}, u32[]{:S(2)}, u32[]{:S(2)}) collective-permute-start(bf16[128,2048]{1,0:T(8,128)(2,1)S(1)} %add_convert_fusion.3), channel_id=1, source_target_pairs={{0,24},{2,26},{4,28},{6,30},{8,0},{10,2},{12,4},{14,6},{16,8},{18,... | collective-permute-start | bytes 1572872 | tf_op jit(solution)/shard_map/ppermute | solution.py:22
  208.5 21.0 %collective-permute-start.26 = (bf16[128,2048]{1,0:T(8,128)(2,1)S(1)}, bf16[128,2048]{1,0:T(8,128)(2,1)S(1)}, u32[]{:S(2)}, u32[]{:S(2)}) collective-permute-start(bf16[128,2048]{1,0:T(8,128)(2,1)S(1)} %add_convert_fusion.4), channel_id=1, source_target_pairs={{0,4},{2,6},{4,0},{6,2},{8,12},{10,14},{12,8},{14,10},{16,20},{18,... | collective-permute-start | bytes 1572872 | tf_op jit(solution)/shard_map/ppermute | solution.py:17
  212.2 32.5 %collective-permute-start.22 = (bf16[128,2048]{1,0:T(8,128)(2,1)S(1)}, bf16[128,2048]{1,0:T(8,128)(2,1)S(1)}, u32[]{:S(2)}, u32[]{:S(2)}) collective-permute-start(bf16[128,2048]{1,0:T(8,128)(2,1)S(1)} %get-tuple-element.129), channel_id=1, source_target_pairs={{0,4},{2,6},{4,0},{6,2},{8,12},{10,14},{12,8},{14,10},{16,20},{18,... | collective-permute-start | bytes 1572872 | tf_op jit(solution)/shard_map/ppermute | solution.py:17
  229.4 14.9 %collective-permute-start.18 = (bf16[128,2048]{1,0:T(8,128)(2,1)S(1)}, bf16[128,2048]{1,0:T(8,128)(2,1)S(1)}, u32[]{:S(2)}, u32[]{:S(2)}) collective-permute-start(bf16[128,2048]{1,0:T(8,128)(2,1)S(1)} %add_convert_fusion.7), channel_id=1, source_target_pairs={{0,4},{2,6},{4,0},{6,2},{8,12},{10,14},{12,8},{14,10},{16,20},{18,... | collective-permute-start | bytes 1572872 | tf_op jit(solution)/shard_map/ppermute | solution.py:17
  229.8 15.0 %collective-permute-start.30 = (bf16[128,2048]{1,0:T(8,128)(2,1)S(1)}, bf16[128,2048]{1,0:T(8,128)(2,1)S(1)}, u32[]{:S(2)}, u32[]{:S(2)}) collective-permute-start(bf16[128,2048]{1,0:T(8,128)(2,1)S(1)} %add_convert_fusion.2), channel_id=1, source_target_pairs={{0,24},{2,26},{4,28},{6,30},{8,0},{10,2},{12,4},{14,6},{16,8},{18,... | collective-permute-start | bytes 1572872 | tf_op jit(solution)/shard_map/ppermute | solution.py:22
  229.8 23.6 %collective-permute-start.20 = (bf16[128,2048]{1,0:T(8,128)(2,1)S(1)}, bf16[128,2048]{1,0:T(8,128)(2,1)S(1)}, u32[]{:S(2)}, u32[]{:S(2)}) collective-permute-start(bf16[128,2048]{1,0:T(8,128)(2,1)S(1)} %get-tuple-element.126), channel_id=1, source_target_pairs={{0,4},{2,6},{4,0},{6,2},{8,12},{10,14},{12,8},{14,10},{16,20},{18,... | collective-permute-start | bytes 1572872 | tf_op jit(solution)/shard_map/ppermute | solution.py:17
  244.4 9.8 %collective-permute-start.19 = (bf16[128,2048]{1,0:T(8,128)(2,1)S(1)}, bf16[128,2048]{1,0:T(8,128)(2,1)S(1)}, u32[]{:S(2)}, u32[]{:S(2)}) collective-permute-start(bf16[128,2048]{1,0:T(8,128)(2,1)S(1)} %add_convert_fusion.6), channel_id=1, source_target_pairs={{0,2},{2,0},{4,6},{6,4},{8,10},{10,8},{12,14},{14,12},{16,18},{18,... | collective-permute-start | bytes 1572872 | tf_op jit(solution)/shard_map/ppermute | solution.py:17
  245.1 9.5 %collective-permute-start.31 = (bf16[128,2048]{1,0:T(8,128)(2,1)S(1)}, bf16[128,2048]{1,0:T(8,128)(2,1)S(1)}, u32[]{:S(2)}, u32[]{:S(2)}) collective-permute-start(bf16[128,2048]{1,0:T(8,128)(2,1)S(1)} %add_convert_fusion.1), channel_id=1, source_target_pairs={{0,24},{2,26},{4,28},{6,30},{8,0},{10,2},{12,4},{14,6},{16,8},{18,... | collective-permute-start | bytes 1572872 | tf_op jit(solution)/shard_map/ppermute | solution.py:22
  (26 other events, 95.0 us)

commit v4 on v3

--- a/solution.py
+++ b/solution.py
@@ -178,7 +178,7 @@
     second = work(range(line - 1, line))
     down_other = swap_cores(after(down, second))
     outs = [None] * line
-    for s in reversed(range(line)):
+    for s in [*range(line - 1, 0, -2), *range(line - 2, -1, -2)]:
         outs[s] = pl.pallas_call(
             functools.partial(out_kernel, rows),
             out_shape=[jax.ShapeDtypeStruct((rows, model), bf16)] * 4,
@@ -200,23 +200,27 @@
     def add(*terms):
         return sum(term.astype(f32) for term in terms).astype(bf16)
 
-    beside = [None] * line
-    for s in range(1, line, 2):
+    beside, corner = [None] * line, [None] * line
+    for s in reversed(range(1, line, 2)):
         beside[s] = turn(outs[s][3], -1)
-    total = None
     from_x, from_y = [None] * line, [None] * line
+    for s in reversed(range(0, line, 2)):
+        over = add(outs[s][3], beside[s + 1]) if s + 1 < line else outs[s][3]
+        corner[s] = flip(over, 2 if s % 4 == 0 else 1)
+    early = beside[line - 1]
     for s in reversed(range(line)):
         kept, to_x, to_y, over = outs[s]
-        if s % 2 == 0 and s + 1 < line:
-            over = add(over, beside[s + 1])
-        if s % 4 == 0:
-            to_x = add(to_x, flip(over, 2))
-        elif s % 2 == 0:
-            to_y = add(to_y, flip(over, 1))
+        if s % 2 == 1:
+            if s < line - 1:
+                to_x, to_y = after(to_x, early), to_y
+        elif s % 4 == 0:
+            to_x, to_y = add(to_x, corner[s]), after(to_y, early)
+        else:
+            to_x, to_y = after(to_x, early), add(to_y, corner[s])
         from_x[s], from_y[s] = flip(to_x, 1), flip(to_y, 2)
-    for s in reversed(range(line)):
-        terms = [outs[s][0], from_x[s], from_y[s]]
-        total = add(*terms) if s == line - 1 else add(*terms, turn(total, -1))
+    total = add(outs[line - 1][0], from_x[line - 1], from_y[line - 1])
+    for s in reversed(range(line - 1)):
+        total = add(outs[s][0], from_x[s], from_y[s], turn(total, -1))
     return total
 
 

time: 261 us -> 253 us (0.969)
  waiting for transfers between devices: 151 us -> 138 us
  starting transfers between devices: 41.9 us -> 47.9 us
    ppermute x22, waiting for transfers between devices: 110 us -> 91.6 us  [flip(): return lax.ppermute(x, 'expert', [(i, i ^ bit) for i in range(size)])]
    ppermute x8, starting transfers between devices: 8.39 us -> 15.9 us  [turn(): lax.ppermute(x, 'expert', [(i, (i + 4 * by) % size) for i in range(size)])]
    ppermute x8, waiting for transfers between devices: 35 us -> 40 us  [turn(): lax.ppermute(x, 'expert', [(i, (i + 4 * by) % size) for i in range(size)])]
  transfers between devices with their start and end apart: 34 -> 34, of which waited for: 21 -> 23; matrix products, arithmetic and copies ran while one was open for 3% -> 3% of each run, Pallas kernels for 12% -> 13%
where the time goes in v4:
time: 253 us; the launch traced here: 249 us
  waiting for transfers between devices  138 us (55%)
  starting transfers between devices  47.9 us (19%)
  Pallas kernels  34.7 us (14%)
  local copies, waits for them, and re-layouts  20.1 us (8%)
  other arithmetic  7.53 us (3%)
    ppermute x22, waiting for transfers between devices, flip(): return lax.ppermute(x, 'expert', [(i, i ^ bit) for i in range(size)])  91.6 us
    ppermute x8, waiting for transfers between devices, turn(): lax.ppermute(x, 'expert', [(i, (i + 4 * by) % size) for i in range(size)])  40 us
    pallas_call x2, Pallas kernels, hidden_of(): pl.pallas_call(functools.partial(hidden_kernel, len(gathered), rows, mode...  21.6 us
    ppermute x22, starting transfers between devices, flip(): return lax.ppermute(x, 'expert', [(i, i ^ bit) for i in range(size)])  17.2 us
    unnamed x48, local copies, waits for them, and re-layouts  16.7 us
    ppermute x8, starting transfers between devices, turn(): lax.ppermute(x, 'expert', [(i, (i + 4 * by) % size) for i in range(size)])  15.9 us
    all_to_all x2, starting transfers between devices, spread(): return lax.all_to_all(w, 'expert', split_axis=0, concat_axis=0, tiled=True)  14.8 us
    pallas_call x4, Pallas kernels, local(): pl.pallas_call(functools.partial(out_kernel, rows), out_shape=[jax.ShapeD...  13.2 us
  transfers between devices with their start and end apart: 34, of which 23 were waited for; matrix products, arithmetic and copies ran while one was open for 3% of the time, Pallas kernels for 13%

profile of v4, /device:TPU:12, one launch (start us, length us, event | category | flops | bytes accessed | tf_op | source)
XLA Modules:
  0.0 248.8 jit_solution(1641531281798363422)
XLA Ops:
  1.0 1.9 fusion.1.refs_0_
  9.0 1.9 constant_dynamic-slice_fusion.1
  10.9 2.1 pad_maximum_fusion
  13.0 4.6 %collective-permute-done.refs_4_ = bf16[128,2176]{1,0:T(8,128)(2,1)} collective-permute-done((bf16[128,2176]{1,0:T(8,128)(2,1)}, bf16[128,2176]{1,0:T(8,128)(2,1)}, u32[]{:S(2)}, u32[]{:S(2)}) %collective-permute-start) | collective-permute-done | bytes 557088 | tf_op jit(solution)/shard_map/ppermute | solution.py:22
  22.7 10.5 %collective-permute-done.3.refs_8_ = bf16[128,2176]{1,0:T(8,128)(2,1)S(1)} collective-permute-done((bf16[128,2176]{1,0:T(8,128)(2,1)}, bf16[128,2176]{1,0:T(8,128)(2,1)S(1)}, u32[]{:S(2)}, u32[]{:S(2)}) %collective-permute-start.3) | collective-permute-done | bytes 557088 | tf_op jit(solution)/shard_map/ppermute | solution.py:22
  37.9 9.1 %collective-permute-done.6.refs_0_ = bf16[128,2176]{1,0:T(8,128)(2,1)S(1)} collective-permute-done((bf16[128,2176]{1,0:T(8,128)(2,1)S(1)}, bf16[128,2176]{1,0:T(8,128)(2,1)S(1)}, u32[]{:S(2)}, u32[]{:S(2)}) %collective-permute-start.6) | collective-permute-done | bytes 557088 | tf_op jit(solution)/shard_map/ppermute | solution.py:22
  49.4 7.8 %all-to-all-start = ((bf16[16,128,768]{2,1,0:T(8,128)(2,1)}), bf16[16,128,768]{2,1,0:T(8,128)(2,1)}, u32[]{:S(2)}, u32[]{:S(2)}) async-start(bf16[16,128,768]{2,1,0:T(8,128)(2,1)} %pad_maximum_fusion), calls=%async_computation | async-start | bytes 6291456 | tf_op jit(solution)/shard_map/all_to_all | solution.py:26
  61.9 26.7 %collective-permute-done.10.refs_2_ = bf16[128,2176]{1,0:T(8,128)(2,1)} collective-permute-done((bf16[128,2176]{1,0:T(8,128)(2,1)}, bf16[128,2176]{1,0:T(8,128)(2,1)}, u32[]{:S(2)}, u32[]{:S(2)}) %collective-permute-start.10) | collective-permute-done | bytes 557088 | tf_op jit(solution)/shard_map/ppermute | solution.py:17
  88.6 21.4 %collective-permute-done.11.refs_3_ = bf16[128,2176]{1,0:T(8,128)(2,1)S(1)} collective-permute-done((bf16[128,2176]{1,0:T(8,128)(2,1)}, bf16[128,2176]{1,0:T(8,128)(2,1)S(1)}, u32[]{:S(2)}, u32[]{:S(2)}) %collective-permute-start.11) | collective-permute-done | bytes 557088 | tf_op jit(solution)/shard_map/ppermute | solution.py:17
  111.6 13.4 %collective-permute-done.13.refs_11_ = bf16[128,2176]{1,0:T(8,128)(2,1)} collective-permute-done((bf16[128,2176]{1,0:T(8,128)(2,1)}, bf16[128,2176]{1,0:T(8,128)(2,1)}, u32[]{:S(2)}, u32[]{:S(2)}) %collective-permute-start.13) | collective-permute-done | bytes 557088 | tf_op jit(solution)/shard_map/ppermute | solution.py:17
  125.8 7.0 %all-to-all-start.1 = ((bf16[16,48,1024]{2,1,0:T(8,128)(2,1)}), bf16[16,48,1024]{2,1,0:T(8,128)(2,1)}, u32[]{:S(2)}, u32[]{:S(2)}) async-start(bf16[16,48,1024]{2,1,0:T(8,128)(2,1)} %constant_dynamic-slice_fusion), calls=%async_computation.1 | async-start | bytes 3145728 | tf_op jit(solution)/shard_map/all_to_all | solution.py:26
  141.7 15.0 %hidden.2 = (bf16[1536,768]{1,0:T(8,128)(2,1)}, f32[1536,128]{1,0:T(8,128)}) custom-call(s32[2]{0:T(128)S(1)} %pad_add_fusion.place, bf16[128,2176]{1,0:T(8,128)(2,1)} %fusion.1.refs_0_, bf16[128,2176]{1,0:T(8,128)(2,1)} %collective-permute-done.1.refs_1_, bf16[128,2176]{1,0:T(8,128)(2,1)} %collective-permute-done.2.refs_2_, ...), custom_call_target="tpu_custom_call" | custom-call | flops 9663676416 | bytes 10000000 | tf_op jit(solution)/shard_map/hidden/pallas_call | solution.py:147
  156.7 3.2 %collective-permute-done.15.refs_3_ = bf16[128,2176]{1,0:T(8,128)(2,1)S(1)} collective-permute-done((bf16[128,2176]{1,0:T(8,128)(2,1)}, bf16[128,2176]{1,0:T(8,128)(2,1)S(1)}, u32[]{:S(2)}, u32[]{:S(2)}) %collective-permute-start.15) | collective-permute-done | bytes 557088 | tf_op jit(solution)/shard_map/ppermute | solution.py:17
  159.9 6.6 %hidden.3 = (bf16[512,768]{1,0:T(8,128)(2,1)S(1)}, f32[512,128]{1,0:T(8,128)S(1)}) custom-call(s32[2]{0:T(128)S(1)} %pad_add_fusion.place, bf16[128,2176]{1,0:T(8,128)(2,1)S(1)} %copy-done.10, bf16[128,2176]{1,0:T(8,128)(2,1)S(1)} %copy-done.18, bf16[128,2176]{1,0:T(8,128)(2,1)} %collective-permute-done.10.refs_2_, ...), custom_call_target="tpu_custom_call" | custom-call | flops 3221225472 | bytes 10000000 | tf_op jit(solution)/shard_map/hidden/pallas_call | solution.py:147
  167.4 3.1 %all-to-all-done.1 = bf16[16,48,1024]{2,1,0:T(8,128)(2,1)} async-done(((bf16[16,48,1024]{2,1,0:T(8,128)(2,1)}), bf16[16,48,1024]{2,1,0:T(8,128)(2,1)}, u32[]{:S(2)}, u32[]{:S(2)}) %all-to-all-start.1) | async-done | bytes 1572896 | tf_op jit(solution)/shard_map/all_to_all | solution.py:26
  170.5 3.6 %collective-permute-done.16.other = bf16[768,1024]{1,0:T(8,128)(2,1)S(1)} collective-permute-done((bf16[768,1024]{1,0:T(8,128)(2,1)}, bf16[768,1024]{1,0:T(8,128)(2,1)S(1)}, u32[]{:S(2)}, u32[]{:S(2)}) %collective-permute-start.16) | collective-permute-done | bytes 1572896 | tf_op jit(solution)/shard_map/ppermute | solution.py:12
  175.2 3.4 %out.6 = (bf16[128,2048]{1,0:T(8,128)(2,1)S(1)}, bf16[128,2048]{1,0:T(8,128)(2,1)S(1)}, bf16[128,2048]{1,0:T(8,128)(2,1)S(1)}, bf16[128,2048]{1,0:T(8,128)(2,1)S(1)}) custom-call(s32[2]{0:T(128)S(1)} %pad_add_fusion.place, bf16[512,768]{1,0:T(8,128)(2,1)S(1)} %copy-done.22, f32[512,128]{1,0:T(8,128)S(1)} %get-tuple-element.130.scale, ...), custom_call_target="tpu_custom_call" | custom-call | flops 1610612736 | bytes 6500000 | tf_op jit(solution)/shard_map/out/pallas_call | solution.py:182
  180.0 3.2 %out.7 = (bf16[128,2048]{1,0:T(8,128)(2,1)S(1)}, bf16[128,2048]{1,0:T(8,128)(2,1)S(1)}, bf16[128,2048]{1,0:T(8,128)(2,1)S(1)}, bf16[128,2048]{1,0:T(8,128)(2,1)S(1)}) custom-call(s32[2]{0:T(128)S(1)} %pad_add_fusion.place, bf16[1536,768]{1,0:T(8,128)(2,1)S(1)} %copy-done.1, f32[1536,128]{1,0:T(8,128)S(1)} %copy-done.2, bf16[768,1024]{1,0:T(8,128)(2,1)} %bitcast.3.own, ...), custom_call_target="tpu_custom_call" | custom-call | flops 1610612736 | bytes 6500000 | tf_op jit(solution)/shard_map/out/pallas_call | solution.py:182
  183.3 10.0 %collective-permute-done.20 = bf16[128,2048]{1,0:T(8,128)(2,1)S(1)} collective-permute-done((bf16[128,2048]{1,0:T(8,128)(2,1)S(1)}, bf16[128,2048]{1,0:T(8,128)(2,1)S(1)}, u32[]{:S(2)}, u32[]{:S(2)}) %collective-permute-start.20) | collective-permute-done | bytes 524320 | tf_op jit(solution)/shard_map/ppermute | solution.py:22
  194.1 3.2 %out.5 = (bf16[128,2048]{1,0:T(8,128)(2,1)S(1)}, bf16[128,2048]{1,0:T(8,128)(2,1)S(1)}, bf16[128,2048]{1,0:T(8,128)(2,1)S(1)}, bf16[128,2048]{1,0:T(8,128)(2,1)S(1)}) custom-call(s32[2]{0:T(128)S(1)} %pad_add_fusion.place, bf16[1536,768]{1,0:T(8,128)(2,1)S(1)} %copy-done.1, f32[1536,128]{1,0:T(8,128)S(1)} %copy-done.2, bf16[768,1024]{1,0:T(8,128)(2,1)} %bitcast.3.own, ...), custom_call_target="tpu_custom_call" | custom-call | flops 1610612736 | bytes 6500000 | tf_op jit(solution)/shard_map/out/pallas_call | solution.py:182
  199.2 4.1 %collective-permute-start.29 = (bf16[128,2048]{1,0:T(8,128)(2,1)S(1)}, bf16[128,2048]{1,0:T(8,128)(2,1)S(1)}, u32[]{:S(2)}, u32[]{:S(2)}) collective-permute-start(bf16[128,2048]{1,0:T(8,128)(2,1)S(1)} %add_convert_fusion.3), channel_id=1, source_target_pairs={{0,24},{2,26},{4,28},{6,30},{8,0},{10,2},{12,4},{14,6},{16,8},{18,... | collective-permute-start | bytes 1572872 | tf_op jit(solution)/shard_map/ppermute | solution.py:22
  203.3 5.0 %collective-permute-done.25 = bf16[128,2048]{1,0:T(8,128)(2,1)S(1)} collective-permute-done((bf16[128,2048]{1,0:T(8,128)(2,1)S(1)}, bf16[128,2048]{1,0:T(8,128)(2,1)S(1)}, u32[]{:S(2)}, u32[]{:S(2)}) %collective-permute-start.25) | collective-permute-done | bytes 524320 | tf_op jit(solution)/shard_map/ppermute | solution.py:17
  208.5 3.3 %out.4 = (bf16[128,2048]{1,0:T(8,128)(2,1)S(1)}, bf16[128,2048]{1,0:T(8,128)(2,1)S(1)}, bf16[128,2048]{1,0:T(8,128)(2,1)S(1)}, bf16[128,2048]{1,0:T(8,128)(2,1)S(1)}) custom-call(s32[2]{0:T(128)S(1)} %pad_add_fusion.place, bf16[1536,768]{1,0:T(8,128)(2,1)S(1)} %copy-done.1, f32[1536,128]{1,0:T(8,128)S(1)} %copy-done.2, bf16[768,1024]{1,0:T(8,128)(2,1)} %bitcast.3.own, ...), custom_call_target="tpu_custom_call" | custom-call | flops 1610612736 | bytes 6500000 | tf_op jit(solution)/shard_map/out/pallas_call | solution.py:182
  212.4 1.6 collective-permute-start.18
  214.0 4.2 %collective-permute-done.24 = bf16[128,2048]{1,0:T(8,128)(2,1)S(1)} collective-permute-done((bf16[128,2048]{1,0:T(8,128)(2,1)S(1)}, bf16[128,2048]{1,0:T(8,128)(2,1)S(1)}, u32[]{:S(2)}, u32[]{:S(2)}) %collective-permute-start.24) | collective-permute-done | bytes 524320 | tf_op jit(solution)/shard_map/ppermute | solution.py:17
  218.5 3.0 %collective-permute-done.29 = bf16[128,2048]{1,0:T(8,128)(2,1)S(1)} collective-permute-done((bf16[128,2048]{1,0:T(8,128)(2,1)S(1)}, bf16[128,2048]{1,0:T(8,128)(2,1)S(1)}, u32[]{:S(2)}, u32[]{:S(2)}) %collective-permute-start.29) | collective-permute-done | bytes 524320 | tf_op jit(solution)/shard_map/ppermute | solution.py:22
  221.5 2.2 collective-permute-done.26
  224.1 3.8 %collective-permute-start.30 = (bf16[128,2048]{1,0:T(8,128)(2,1)S(1)}, bf16[128,2048]{1,0:T(8,128)(2,1)S(1)}, u32[]{:S(2)}, u32[]{:S(2)}) collective-permute-start(bf16[128,2048]{1,0:T(8,128)(2,1)S(1)} %add_convert_fusion.2), channel_id=1, source_target_pairs={{0,24},{2,26},{4,28},{6,30},{8,0},{10,2},{12,4},{14,6},{16,8},{18,... | collective-permute-start | bytes 1572872 | tf_op jit(solution)/shard_map/ppermute | solution.py:22
  227.9 7.1 %collective-permute-done.18 = bf16[128,2048]{1,0:T(8,128)(2,1)S(1)} collective-permute-done((bf16[128,2048]{1,0:T(8,128)(2,1)S(1)}, bf16[128,2048]{1,0:T(8,128)(2,1)S(1)}, u32[]{:S(2)}, u32[]{:S(2)}) %collective-permute-start.18) | collective-permute-done | bytes 524320 | tf_op jit(solution)/shard_map/ppermute | solution.py:17
  236.8 4.1 %collective-permute-start.31 = (bf16[128,2048]{1,0:T(8,128)(2,1)S(1)}, bf16[128,2048]{1,0:T(8,128)(2,1)S(1)}, u32[]{:S(2)}, u32[]{:S(2)}) collective-permute-start(bf16[128,2048]{1,0:T(8,128)(2,1)S(1)} %add_convert_fusion.1), channel_id=1, source_target_pairs={{0,24},{2,26},{4,28},{6,30},{8,0},{10,2},{12,4},{14,6},{16,8},{18,... | collective-permute-start | bytes 1572872 | tf_op jit(solution)/shard_map/ppermute | solution.py:22
  240.9 3.3 %collective-permute-done.21 = bf16[128,2048]{1,0:T(8,128)(2,1)S(1)} collective-permute-done((bf16[128,2048]{1,0:T(8,128)(2,1)S(1)}, bf16[128,2048]{1,0:T(8,128)(2,1)S(1)}, u32[]{:S(2)}, u32[]{:S(2)}) %collective-permute-start.21) | collective-permute-done | bytes 524320 | tf_op jit(solution)/shard_map/ppermute | solution.py:17
  245.3 2.4 collective-permute-done.31
  (107 shorter events, 46.7 us)
Async XLA Ops:
  2.9 14.7 %collective-permute-start = (bf16[128,2176]{1,0:T(8,128)(2,1)}, bf16[128,2176]{1,0:T(8,128)(2,1)}, u32[]{:S(2)}, u32[]{:S(2)}) collective-permute-start(bf16[128,2176]{1,0:T(8,128)(2,1)} %fusion.1.refs_0_), channel_id=1, source_target_pairs={{0,8},{2,10},{4,12},{6,14},{8,16},{10,18},{12,20},{14,22},{16,24},... | collective-permute-start | bytes 1671176 | tf_op jit(solution)/shard_map/ppermute | solution.py:22
  4.5 14.4 %collective-permute-start.1 = (bf16[128,2176]{1,0:T(8,128)(2,1)}, bf16[128,2176]{1,0:T(8,128)(2,1)}, u32[]{:S(2)}, u32[]{:S(2)}) collective-permute-start(bf16[128,2176]{1,0:T(8,128)(2,1)} %fusion.1.refs_0_), channel_id=1, source_target_pairs={{0,2},{2,0},{4,6},{6,4},{8,10},{10,8},{12,14},{14,12},{16,18},{18,... | collective-permute-start | bytes 1671176 | tf_op jit(solution)/shard_map/ppermute | solution.py:17
  6.0 14.1 %collective-permute-start.2 = (bf16[128,2176]{1,0:T(8,128)(2,1)}, bf16[128,2176]{1,0:T(8,128)(2,1)}, u32[]{:S(2)}, u32[]{:S(2)}) collective-permute-start(bf16[128,2176]{1,0:T(8,128)(2,1)} %fusion.1.refs_0_), channel_id=1, source_target_pairs={{0,4},{2,6},{4,0},{6,2},{8,12},{10,14},{12,8},{14,10},{16,20},{18,... | collective-permute-start | bytes 1671176 | tf_op jit(solution)/shard_map/ppermute | solution.py:17
  20.1 13.1 %collective-permute-start.3 = (bf16[128,2176]{1,0:T(8,128)(2,1)}, bf16[128,2176]{1,0:T(8,128)(2,1)S(1)}, u32[]{:S(2)}, u32[]{:S(2)}) collective-permute-start(bf16[128,2176]{1,0:T(8,128)(2,1)} %collective-permute-done.refs_4_), channel_id=1, source_target_pairs={{0,8},{2,10},{4,12},{6,14},{8,16},{10,18},{12,20},{14,22},{16,24},... | collective-permute-start | bytes 1671176 | tf_op jit(solution)/shard_map/ppermute | solution.py:22
  21.7 12.8 %collective-permute-start.4 = (bf16[128,2176]{1,0:T(8,128)(2,1)}, bf16[128,2176]{1,0:T(8,128)(2,1)S(1)}, u32[]{:S(2)}, u32[]{:S(2)}) collective-permute-start(bf16[128,2176]{1,0:T(8,128)(2,1)} %collective-permute-done.refs_4_), channel_id=1, source_target_pairs={{0,2},{2,0},{4,6},{6,4},{8,10},{10,8},{12,14},{14,12},{16,18},{18,... | collective-permute-start | bytes 1671176 | tf_op jit(solution)/shard_map/ppermute | solution.py:17
  22.2 13.1 %collective-permute-start.5 = (bf16[128,2176]{1,0:T(8,128)(2,1)}, bf16[128,2176]{1,0:T(8,128)(2,1)S(1)}, u32[]{:S(2)}, u32[]{:S(2)}) collective-permute-start(bf16[128,2176]{1,0:T(8,128)(2,1)} %collective-permute-done.refs_4_), channel_id=1, source_target_pairs={{0,4},{2,6},{4,0},{6,2},{8,12},{10,14},{12,8},{14,10},{16,20},{18,... | collective-permute-start | bytes 1671176 | tf_op jit(solution)/shard_map/ppermute | solution.py:17
  35.3 11.7 %collective-permute-start.6 = (bf16[128,2176]{1,0:T(8,128)(2,1)S(1)}, bf16[128,2176]{1,0:T(8,128)(2,1)S(1)}, u32[]{:S(2)}, u32[]{:S(2)}) collective-permute-start(bf16[128,2176]{1,0:T(8,128)(2,1)S(1)} %collective-permute-done.3.refs_8_), channel_id=1, source_target_pairs={{0,8},{2,10},{4,12},{6,14},{8,16},{10,18},{12,20},{14,22},{16,24},... | collective-permute-start | bytes 1671176 | tf_op jit(solution)/shard_map/ppermute | solution.py:22
  35.7 11.6 %collective-permute-start.7 = (bf16[128,2176]{1,0:T(8,128)(2,1)S(1)}, bf16[128,2176]{1,0:T(8,128)(2,1)S(1)}, u32[]{:S(2)}, u32[]{:S(2)}) collective-permute-start(bf16[128,2176]{1,0:T(8,128)(2,1)S(1)} %collective-permute-done.3.refs_8_), channel_id=1, source_target_pairs={{0,2},{2,0},{4,6},{6,4},{8,10},{10,8},{12,14},{14,12},{16,18},{18,... | collective-permute-start | bytes 1671176 | tf_op jit(solution)/shard_map/ppermute | solution.py:17
  36.6 12.0 %collective-permute-start.8 = (bf16[128,2176]{1,0:T(8,128)(2,1)S(1)}, bf16[128,2176]{1,0:T(8,128)(2,1)S(1)}, u32[]{:S(2)}, u32[]{:S(2)}) collective-permute-start(bf16[128,2176]{1,0:T(8,128)(2,1)S(1)} %collective-permute-done.3.refs_8_), channel_id=1, source_target_pairs={{0,4},{2,6},{4,0},{6,2},{8,12},{10,14},{12,8},{14,10},{16,20},{18,... | collective-permute-start | bytes 1671176 | tf_op jit(solution)/shard_map/ppermute | solution.py:17
  49.4 76.4 %all-to-all-start = ((bf16[16,128,768]{2,1,0:T(8,128)(2,1)}), bf16[16,128,768]{2,1,0:T(8,128)(2,1)}, u32[]{:S(2)}, u32[]{:S(2)}) async-start(bf16[16,128,768]{2,1,0:T(8,128)(2,1)} %pad_maximum_fusion), calls=%async_computation | async-start | bytes 6291456 | tf_op jit(solution)/shard_map/all_to_all | solution.py:26
  57.2 31.3 %collective-permute-start.10 = (bf16[128,2176]{1,0:T(8,128)(2,1)}, bf16[128,2176]{1,0:T(8,128)(2,1)}, u32[]{:S(2)}, u32[]{:S(2)}) collective-permute-start(bf16[128,2176]{1,0:T(8,128)(2,1)} %copy-done.9), channel_id=1, source_target_pairs={{0,4},{2,6},{4,0},{6,2},{8,12},{10,14},{12,8},{14,10},{16,20},{18,... | collective-permute-start | bytes 1671176 | tf_op jit(solution)/shard_map/ppermute | solution.py:17
  57.8 52.2 %collective-permute-start.11 = (bf16[128,2176]{1,0:T(8,128)(2,1)}, bf16[128,2176]{1,0:T(8,128)(2,1)S(1)}, u32[]{:S(2)}, u32[]{:S(2)}) collective-permute-start(bf16[128,2176]{1,0:T(8,128)(2,1)} %collective-permute-done.1.refs_1_), channel_id=1, source_target_pairs={{0,4},{2,6},{4,0},{6,2},{8,12},{10,14},{12,8},{14,10},{16,20},{18,... | collective-permute-start | bytes 1671176 | tf_op jit(solution)/shard_map/ppermute | solution.py:17
  59.3 51.5 %collective-permute-start.12 = (bf16[128,2176]{1,0:T(8,128)(2,1)}, bf16[128,2176]{1,0:T(8,128)(2,1)S(1)}, u32[]{:S(2)}, u32[]{:S(2)}) collective-permute-start(bf16[128,2176]{1,0:T(8,128)(2,1)} %copy-done.7), channel_id=1, source_target_pairs={{0,2},{2,0},{4,6},{6,4},{8,10},{10,8},{12,14},{14,12},{16,18},{18,... | collective-permute-start | bytes 1671176 | tf_op jit(solution)/shard_map/ppermute | solution.py:17
  60.7 64.3 %collective-permute-start.13 = (bf16[128,2176]{1,0:T(8,128)(2,1)}, bf16[128,2176]{1,0:T(8,128)(2,1)}, u32[]{:S(2)}, u32[]{:S(2)}) collective-permute-start(bf16[128,2176]{1,0:T(8,128)(2,1)} %copy-done.11), channel_id=1, source_target_pairs={{0,4},{2,6},{4,0},{6,2},{8,12},{10,14},{12,8},{14,10},{16,20},{18,... | collective-permute-start | bytes 1671176 | tf_op jit(solution)/shard_map/ppermute | solution.py:17
  61.3 63.7 %collective-permute-start.9 = (bf16[128,2176]{1,0:T(8,128)(2,1)}, bf16[128,2176]{1,0:T(8,128)(2,1)S(1)}, u32[]{:S(2)}, u32[]{:S(2)}) collective-permute-start(bf16[128,2176]{1,0:T(8,128)(2,1)} %copy-done.9), channel_id=1, source_target_pairs={{0,2},{2,0},{4,6},{6,4},{8,10},{10,8},{12,14},{14,12},{16,18},{18,... | collective-permute-start | bytes 1671176 | tf_op jit(solution)/shard_map/ppermute | solution.py:17
  125.8 44.6 %all-to-all-start.1 = ((bf16[16,48,1024]{2,1,0:T(8,128)(2,1)}), bf16[16,48,1024]{2,1,0:T(8,128)(2,1)}, u32[]{:S(2)}, u32[]{:S(2)}) async-start(bf16[16,48,1024]{2,1,0:T(8,128)(2,1)} %constant_dynamic-slice_fusion), calls=%async_computation.1 | async-start | bytes 3145728 | tf_op jit(solution)/shard_map/all_to_all | solution.py:26
  132.9 27.0 %collective-permute-start.15 = (bf16[128,2176]{1,0:T(8,128)(2,1)}, bf16[128,2176]{1,0:T(8,128)(2,1)S(1)}, u32[]{:S(2)}, u32[]{:S(2)}) collective-permute-start(bf16[128,2176]{1,0:T(8,128)(2,1)} %collective-permute-done.10.refs_2_), channel_id=1, source_target_pairs={{0,2},{2,0},{4,6},{6,4},{8,10},{10,8},{12,14},{14,12},{16,18},{18,... | collective-permute-start | bytes 1671176 | tf_op jit(solution)/shard_map/ppermute | solution.py:17
  178.6 14.7 %collective-permute-start.20 = (bf16[128,2048]{1,0:T(8,128)(2,1)S(1)}, bf16[128,2048]{1,0:T(8,128)(2,1)S(1)}, u32[]{:S(2)}, u32[]{:S(2)}) collective-permute-start(bf16[128,2048]{1,0:T(8,128)(2,1)S(1)} %get-tuple-element.131), channel_id=1, source_target_pairs={{0,24},{2,26},{4,28},{6,30},{8,0},{10,2},{12,4},{14,6},{16,8},{18,... | collective-permute-start | bytes 1572872 | tf_op jit(solution)/shard_map/ppermute | solution.py:22
  178.7 19.0 %collective-permute-start.27 = (bf16[128,2048]{1,0:T(8,128)(2,1)S(1)}, bf16[128,2048]{1,0:T(8,128)(2,1)S(1)}, u32[]{:S(2)}, u32[]{:S(2)}) collective-permute-start(bf16[128,2048]{1,0:T(8,128)(2,1)S(1)} %get-tuple-element.143), channel_id=1, source_target_pairs={{0,2},{2,0},{4,6},{6,4},{8,10},{10,8},{12,14},{14,12},{16,18},{18,... | collective-permute-start | bytes 1572872 | tf_op jit(solution)/shard_map/ppermute | solution.py:17
  180.0 19.0 %collective-permute-start.28 = (bf16[128,2048]{1,0:T(8,128)(2,1)S(1)}, bf16[128,2048]{1,0:T(8,128)(2,1)S(1)}, u32[]{:S(2)}, u32[]{:S(2)}) collective-permute-start(bf16[128,2048]{1,0:T(8,128)(2,1)S(1)} %get-tuple-element.144), channel_id=1, source_target_pairs={{0,4},{2,6},{4,0},{6,2},{8,12},{10,14},{12,8},{14,10},{16,20},{18,... | collective-permute-start | bytes 1572872 | tf_op jit(solution)/shard_map/ppermute | solution.py:17
  193.4 14.9 %collective-permute-start.25 = (bf16[128,2048]{1,0:T(8,128)(2,1)S(1)}, bf16[128,2048]{1,0:T(8,128)(2,1)S(1)}, u32[]{:S(2)}, u32[]{:S(2)}) collective-permute-start(bf16[128,2048]{1,0:T(8,128)(2,1)S(1)} %add_convert_fusion.5), channel_id=1, source_target_pairs={{0,2},{2,0},{4,6},{6,4},{8,10},{10,8},{12,14},{14,12},{16,18},{18,... | collective-permute-start | bytes 1572872 | tf_op jit(solution)/shard_map/ppermute | solution.py:17
  197.3 14.9 %collective-permute-start.17 = (bf16[128,2048]{1,0:T(8,128)(2,1)S(1)}, bf16[128,2048]{1,0:T(8,128)(2,1)S(1)}, u32[]{:S(2)}, u32[]{:S(2)}) collective-permute-start(bf16[128,2048]{1,0:T(8,128)(2,1)S(1)} %get-tuple-element.128), channel_id=1, source_target_pairs={{0,24},{2,26},{4,28},{6,30},{8,0},{10,2},{12,4},{14,6},{16,8},{18,... | collective-permute-start | bytes 1572872 | tf_op jit(solution)/shard_map/ppermute | solution.py:22
  197.7 38.8 %collective-permute-start.23 = (bf16[128,2048]{1,0:T(8,128)(2,1)S(1)}, bf16[128,2048]{1,0:T(8,128)(2,1)S(1)}, u32[]{:S(2)}, u32[]{:S(2)}) collective-permute-start(bf16[128,2048]{1,0:T(8,128)(2,1)S(1)} %get-tuple-element.136), channel_id=1, source_target_pairs={{0,4},{2,6},{4,0},{6,2},{8,12},{10,14},{12,8},{14,10},{16,20},{18,... | collective-permute-start | bytes 1572872 | tf_op jit(solution)/shard_map/ppermute | solution.py:17
  197.7 20.5 %collective-permute-start.24 = (bf16[128,2048]{1,0:T(8,128)(2,1)S(1)}, bf16[128,2048]{1,0:T(8,128)(2,1)S(1)}, u32[]{:S(2)}, u32[]{:S(2)}) collective-permute-start(bf16[128,2048]{1,0:T(8,128)(2,1)S(1)} %get-tuple-element.139), channel_id=1, source_target_pairs={{0,2},{2,0},{4,6},{6,4},{8,10},{10,8},{12,14},{14,12},{16,18},{18,... | collective-permute-start | bytes 1572872 | tf_op jit(solution)/shard_map/ppermute | solution.py:17
  199.2 22.3 %collective-permute-start.29 = (bf16[128,2048]{1,0:T(8,128)(2,1)S(1)}, bf16[128,2048]{1,0:T(8,128)(2,1)S(1)}, u32[]{:S(2)}, u32[]{:S(2)}) collective-permute-start(bf16[128,2048]{1,0:T(8,128)(2,1)S(1)} %add_convert_fusion.3), channel_id=1, source_target_pairs={{0,24},{2,26},{4,28},{6,30},{8,0},{10,2},{12,4},{14,6},{16,8},{18,... | collective-permute-start | bytes 1572872 | tf_op jit(solution)/shard_map/ppermute | solution.py:22
  208.5 15.3 %collective-permute-start.26 = (bf16[128,2048]{1,0:T(8,128)(2,1)S(1)}, bf16[128,2048]{1,0:T(8,128)(2,1)S(1)}, u32[]{:S(2)}, u32[]{:S(2)}) collective-permute-start(bf16[128,2048]{1,0:T(8,128)(2,1)S(1)} %add_convert_fusion.4), channel_id=1, source_target_pairs={{0,4},{2,6},{4,0},{6,2},{8,12},{10,14},{12,8},{14,10},{16,20},{18,... | collective-permute-start | bytes 1572872 | tf_op jit(solution)/shard_map/ppermute | solution.py:17
  212.4 22.6 %collective-permute-start.18 = (bf16[128,2048]{1,0:T(8,128)(2,1)S(1)}, bf16[128,2048]{1,0:T(8,128)(2,1)S(1)}, u32[]{:S(2)}, u32[]{:S(2)}) collective-permute-start(bf16[128,2048]{1,0:T(8,128)(2,1)S(1)} %add_convert_fusion.7), channel_id=1, source_target_pairs={{0,4},{2,6},{4,0},{6,2},{8,12},{10,14},{12,8},{14,10},{16,20},{18,... | collective-permute-start | bytes 1572872 | tf_op jit(solution)/shard_map/ppermute | solution.py:17
  218.2 18.3 %collective-permute-start.22 = (bf16[128,2048]{1,0:T(8,128)(2,1)S(1)}, bf16[128,2048]{1,0:T(8,128)(2,1)S(1)}, u32[]{:S(2)}, u32[]{:S(2)}) collective-permute-start(bf16[128,2048]{1,0:T(8,128)(2,1)S(1)} %get-tuple-element.135), channel_id=1, source_target_pairs={{0,2},{2,0},{4,6},{6,4},{8,10},{10,8},{12,14},{14,12},{16,18},{18,... | collective-permute-start | bytes 1572872 | tf_op jit(solution)/shard_map/ppermute | solution.py:17
  224.1 12.3 %collective-permute-start.30 = (bf16[128,2048]{1,0:T(8,128)(2,1)S(1)}, bf16[128,2048]{1,0:T(8,128)(2,1)S(1)}, u32[]{:S(2)}, u32[]{:S(2)}) collective-permute-start(bf16[128,2048]{1,0:T(8,128)(2,1)S(1)} %add_convert_fusion.2), channel_id=1, source_target_pairs={{0,24},{2,26},{4,28},{6,30},{8,0},{10,2},{12,4},{14,6},{16,8},{18,... | collective-permute-start | bytes 1572872 | tf_op jit(solution)/shard_map/ppermute | solution.py:22
  227.9 16.4 %collective-permute-start.21 = (bf16[128,2048]{1,0:T(8,128)(2,1)S(1)}, bf16[128,2048]{1,0:T(8,128)(2,1)S(1)}, u32[]{:S(2)}, u32[]{:S(2)}) collective-permute-start(bf16[128,2048]{1,0:T(8,128)(2,1)S(1)} %get-tuple-element.132), channel_id=1, source_target_pairs={{0,4},{2,6},{4,0},{6,2},{8,12},{10,14},{12,8},{14,10},{16,20},{18,... | collective-permute-start | bytes 1572872 | tf_op jit(solution)/shard_map/ppermute | solution.py:17
  235.1 10.1 %collective-permute-start.19 = (bf16[128,2048]{1,0:T(8,128)(2,1)S(1)}, bf16[128,2048]{1,0:T(8,128)(2,1)S(1)}, u32[]{:S(2)}, u32[]{:S(2)}) collective-permute-start(bf16[128,2048]{1,0:T(8,128)(2,1)S(1)} %add_convert_fusion.6), channel_id=1, source_target_pairs={{0,2},{2,0},{4,6},{6,4},{8,10},{10,8},{12,14},{14,12},{16,18},{18,... | collective-permute-start | bytes 1572872 | tf_op jit(solution)/shard_map/ppermute | solution.py:17
  236.8 10.8 %collective-permute-start.31 = (bf16[128,2048]{1,0:T(8,128)(2,1)S(1)}, bf16[128,2048]{1,0:T(8,128)(2,1)S(1)}, u32[]{:S(2)}, u32[]{:S(2)}) collective-permute-start(bf16[128,2048]{1,0:T(8,128)(2,1)S(1)} %add_convert_fusion.1), channel_id=1, source_target_pairs={{0,24},{2,26},{4,28},{6,30},{8,0},{10,2},{12,4},{14,6},{16,8},{18,... | collective-permute-start | bytes 1572872 | tf_op jit(solution)/shard_map/ppermute | solution.py:22
  (26 other events, 95.0 us)

commit v5 on v4

--- a/solution.py
+++ b/solution.py
@@ -112,7 +112,11 @@
         by_x[s], by_y[s] = flip(held[s], 1), flip(held[s], 2)
 
     def far(s):
-        across[s] = flip(by_x[s], 2) if s % 2 == 0 else flip(by_y[s], 1)
+        if s != line - 2:
+            across[s] = flip(by_x[s], 2) if s % 2 == 0 else flip(by_y[s], 1)
+        else:
+            cut = rows // 2
+            across[s] = jnp.concatenate([flip(by_x[s][:cut], 2), flip(by_y[s][cut:], 1)], axis=0)
 
     def settle(*extra):
         done = lax.optimization_barrier((held, by_x, by_y, across, extra))

time: 253 us -> 249 us (0.984)
  waiting for transfers between devices: 138 us -> 134 us
    ppermute x22 -> x23, waiting for transfers between devices: 91.6 us -> 79.3 us  [flip(): return lax.ppermute(x, 'expert', [(i, i ^ bit) for i in range(size)])]
    all_to_all x2, waiting for transfers between devices: 3.09 us -> 10.9 us  [spread(): return lax.all_to_all(w, 'expert', split_axis=0, concat_axis=0, tiled=True)]
    unnamed x48 -> x40, local copies, waits for them, and re-layouts: 16.7 us -> 13.1 us
    ppermute x22 -> x23, starting transfers between devices: 17.2 us -> 20 us  [flip(): return lax.ppermute(x, 'expert', [(i, i ^ bit) for i in range(size)])]
  transfers between devices with their start and end apart: 34 -> 35, of which waited for: 23 -> 25; matrix products, arithmetic and copies ran while one was open for 3% -> 4% of each run, Pallas kernels for 13% -> 13%
where the time goes in v5:
time: 249 us; the launch traced here: 245 us
  waiting for transfers between devices  134 us (54%)
  starting transfers between devices  49.4 us (20%)
  Pallas kernels  34.8 us (14%)
  local copies, waits for them, and re-layouts  18.4 us (7%)
  other arithmetic  8.28 us (3%)
    ppermute x23, waiting for transfers between devices, flip(): return lax.ppermute(x, 'expert', [(i, i ^ bit) for i in range(size)])  79.3 us
    ppermute x8, waiting for transfers between devices, turn(): lax.ppermute(x, 'expert', [(i, (i + 4 * by) % size) for i in range(size)])  40.1 us
    pallas_call x2, Pallas kernels, hidden_of(): pl.pallas_call(functools.partial(hidden_kernel, len(gathered), rows, mode...  21.7 us
    ppermute x23, starting transfers between devices, flip(): return lax.ppermute(x, 'expert', [(i, i ^ bit) for i in range(size)])  20 us
    ppermute x8, starting transfers between devices, turn(): lax.ppermute(x, 'expert', [(i, (i + 4 * by) % size) for i in range(size)])  15.9 us
    all_to_all x2, starting transfers between devices, spread(): return lax.all_to_all(w, 'expert', split_axis=0, concat_axis=0, tiled=True)  13.5 us
    pallas_call x4, Pallas kernels, local(): pl.pallas_call(functools.partial(out_kernel, rows), out_shape=[jax.ShapeD...  13.2 us
    unnamed x40, local copies, waits for them, and re-layouts  13.1 us
  transfers between devices with their start and end apart: 35, of which 25 were waited for; matrix products, arithmetic and copies ran while one was open for 4% of the time, Pallas kernels for 13%

profile of v5, /device:TPU:12, one launch (start us, length us, event | category | flops | bytes accessed | tf_op | source)
XLA Modules:
  0.0 245.1 jit_solution(741209141156166718)
XLA Ops:
  8.9 1.9 constant_dynamic-slice_fusion.1
  10.8 2.0 pad_maximum_fusion
  12.9 4.7 %collective-permute-done.refs_4_ = bf16[128,2176]{1,0:T(8,128)(2,1)} collective-permute-done((bf16[128,2176]{1,0:T(8,128)(2,1)}, bf16[128,2176]{1,0:T(8,128)(2,1)}, u32[]{:S(2)}, u32[]{:S(2)}) %collective-permute-start) | collective-permute-done | bytes 557088 | tf_op jit(solution)/shard_map/ppermute | solution.py:22
  22.7 10.5 %collective-permute-done.3.refs_8_ = bf16[128,2176]{1,0:T(8,128)(2,1)S(1)} collective-permute-done((bf16[128,2176]{1,0:T(8,128)(2,1)}, bf16[128,2176]{1,0:T(8,128)(2,1)S(1)}, u32[]{:S(2)}, u32[]{:S(2)}) %collective-permute-start.3) | collective-permute-done | bytes 557088 | tf_op jit(solution)/shard_map/ppermute | solution.py:22
  37.9 9.1 %collective-permute-done.6.refs_0_ = bf16[128,2176]{1,0:T(8,128)(2,1)S(1)} collective-permute-done((bf16[128,2176]{1,0:T(8,128)(2,1)S(1)}, bf16[128,2176]{1,0:T(8,128)(2,1)S(1)}, u32[]{:S(2)}, u32[]{:S(2)}) %collective-permute-start.6) | collective-permute-done | bytes 557088 | tf_op jit(solution)/shard_map/ppermute | solution.py:22
  48.1 7.9 %all-to-all-start = ((bf16[16,128,768]{2,1,0:T(8,128)(2,1)}), bf16[16,128,768]{2,1,0:T(8,128)(2,1)}, u32[]{:S(2)}, u32[]{:S(2)}) async-start(bf16[16,128,768]{2,1,0:T(8,128)(2,1)} %pad_maximum_fusion), calls=%async_computation | async-start | bytes 6291456 | tf_op jit(solution)/shard_map/all_to_all | solution.py:26
  62.7 14.9 %collective-permute-done.13 = bf16[64,2176]{1,0:T(8,128)(2,1)S(1)} collective-permute-done((bf16[64,2176]{1,0:T(8,128)(2,1)S(1)}, bf16[64,2176]{1,0:T(8,128)(2,1)S(1)}, u32[]{:S(2)}, u32[]{:S(2)}) %collective-permute-start.13) | collective-permute-done | bytes 278560 | tf_op jit(solution)/shard_map/ppermute | solution.py:17
  77.7 2.7 %collective-permute-start.9 = (bf16[128,2176]{1,0:T(8,128)(2,1)}, bf16[128,2176]{1,0:T(8,128)(2,1)S(1)}, u32[]{:S(2)}, u32[]{:S(2)}) collective-permute-start(bf16[128,2176]{1,0:T(8,128)(2,1)} %copy-done.9), channel_id=1, source_target_pairs={{0,2},{2,0},{4,6},{6,4},{8,10},{10,8},{12,14},{14,12},{16,18},{18,... | collective-permute-start | bytes 1671176 | tf_op jit(solution)/shard_map/ppermute | solution.py:17
  81.2 19.5 %collective-permute-done.10.refs_2_ = bf16[128,2176]{1,0:T(8,128)(2,1)} collective-permute-done((bf16[128,2176]{1,0:T(8,128)(2,1)}, bf16[128,2176]{1,0:T(8,128)(2,1)}, u32[]{:S(2)}, u32[]{:S(2)}) %collective-permute-start.10) | collective-permute-done | bytes 557088 | tf_op jit(solution)/shard_map/ppermute | solution.py:17
  100.7 12.4 %collective-permute-done.11.refs_3_ = bf16[128,2176]{1,0:T(8,128)(2,1)S(1)} collective-permute-done((bf16[128,2176]{1,0:T(8,128)(2,1)}, bf16[128,2176]{1,0:T(8,128)(2,1)S(1)}, u32[]{:S(2)}, u32[]{:S(2)}) %collective-permute-start.11) | collective-permute-done | bytes 557088 | tf_op jit(solution)/shard_map/ppermute | solution.py:17
  115.6 7.8 %all-to-all-done = bf16[16,128,768]{2,1,0:T(8,128)(2,1)} async-done(((bf16[16,128,768]{2,1,0:T(8,128)(2,1)}), bf16[16,128,768]{2,1,0:T(8,128)(2,1)}, u32[]{:S(2)}, u32[]{:S(2)}) %all-to-all-start) | async-done | bytes 3145760 | tf_op jit(solution)/shard_map/all_to_all | solution.py:26
  123.5 5.6 %all-to-all-start.1 = ((bf16[16,48,1024]{2,1,0:T(8,128)(2,1)}), bf16[16,48,1024]{2,1,0:T(8,128)(2,1)}, u32[]{:S(2)}, u32[]{:S(2)}) async-start(bf16[16,48,1024]{2,1,0:T(8,128)(2,1)} %constant_dynamic-slice_fusion), calls=%async_computation.1 | async-start | bytes 3145728 | tf_op jit(solution)/shard_map/all_to_all | solution.py:26
  135.9 15.1 %hidden.2 = (bf16[1536,768]{1,0:T(8,128)(2,1)}, f32[1536,128]{1,0:T(8,128)}) custom-call(s32[2]{0:T(128)S(1)} %pad_add_fusion.place, bf16[128,2176]{1,0:T(8,128)(2,1)} %fusion.1.refs_0_, bf16[128,2176]{1,0:T(8,128)(2,1)} %collective-permute-done.1.refs_1_, bf16[128,2176]{1,0:T(8,128)(2,1)} %collective-permute-done.2.refs_2_, ...), custom_call_target="tpu_custom_call" | custom-call | flops 9663676416 | bytes 10000000 | tf_op jit(solution)/shard_map/hidden/pallas_call | solution.py:151
  151.0 5.2 %collective-permute-done.16.refs_3_ = bf16[128,2176]{1,0:T(8,128)(2,1)S(1)} collective-permute-done((bf16[128,2176]{1,0:T(8,128)(2,1)}, bf16[128,2176]{1,0:T(8,128)(2,1)S(1)}, u32[]{:S(2)}, u32[]{:S(2)}) %collective-permute-start.16) | collective-permute-done | bytes 557088 | tf_op jit(solution)/shard_map/ppermute | solution.py:17
  156.2 6.6 %hidden.3 = (bf16[512,768]{1,0:T(8,128)(2,1)S(1)}, f32[512,128]{1,0:T(8,128)S(1)}) custom-call(s32[2]{0:T(128)S(1)} %pad_add_fusion.place, bf16[128,2176]{1,0:T(8,128)(2,1)S(1)} %copy-done.10, bf16[128,2176]{1,0:T(8,128)(2,1)S(1)} %copy-done.14, bf16[128,2176]{1,0:T(8,128)(2,1)} %collective-permute-done.10.refs_2_, ...), custom_call_target="tpu_custom_call" | custom-call | flops 3221225472 | bytes 10000000 | tf_op jit(solution)/shard_map/hidden/pallas_call | solution.py:151
  163.7 3.1 %all-to-all-done.1 = bf16[16,48,1024]{2,1,0:T(8,128)(2,1)} async-done(((bf16[16,48,1024]{2,1,0:T(8,128)(2,1)}), bf16[16,48,1024]{2,1,0:T(8,128)(2,1)}, u32[]{:S(2)}, u32[]{:S(2)}) %all-to-all-start.1) | async-done | bytes 1572896 | tf_op jit(solution)/shard_map/all_to_all | solution.py:26
  166.7 3.6 %collective-permute-done.17.other = bf16[768,1024]{1,0:T(8,128)(2,1)S(1)} collective-permute-done((bf16[768,1024]{1,0:T(8,128)(2,1)}, bf16[768,1024]{1,0:T(8,128)(2,1)S(1)}, u32[]{:S(2)}, u32[]{:S(2)}) %collective-permute-start.17) | collective-permute-done | bytes 1572896 | tf_op jit(solution)/shard_map/ppermute | solution.py:12
  171.5 3.4 %out.6 = (bf16[128,2048]{1,0:T(8,128)(2,1)S(1)}, bf16[128,2048]{1,0:T(8,128)(2,1)S(1)}, bf16[128,2048]{1,0:T(8,128)(2,1)S(1)}, bf16[128,2048]{1,0:T(8,128)(2,1)S(1)}) custom-call(s32[2]{0:T(128)S(1)} %pad_add_fusion.place, bf16[512,768]{1,0:T(8,128)(2,1)S(1)} %copy-done.18, f32[512,128]{1,0:T(8,128)S(1)} %get-tuple-element.130.scale, ...), custom_call_target="tpu_custom_call" | custom-call | flops 1610612736 | bytes 6500000 | tf_op jit(solution)/shard_map/out/pallas_call | solution.py:186
  176.3 3.2 %out.7 = (bf16[128,2048]{1,0:T(8,128)(2,1)S(1)}, bf16[128,2048]{1,0:T(8,128)(2,1)S(1)}, bf16[128,2048]{1,0:T(8,128)(2,1)S(1)}, bf16[128,2048]{1,0:T(8,128)(2,1)S(1)}) custom-call(s32[2]{0:T(128)S(1)} %pad_add_fusion.place, bf16[1536,768]{1,0:T(8,128)(2,1)S(1)} %copy-done.1, f32[1536,128]{1,0:T(8,128)S(1)} %copy-done.2, bf16[768,1024]{1,0:T(8,128)(2,1)} %bitcast.3.own, ...), custom_call_target="tpu_custom_call" | custom-call | flops 1610612736 | bytes 6500000 | tf_op jit(solution)/shard_map/out/pallas_call | solution.py:186
  179.6 10.0 %collective-permute-done.21 = bf16[128,2048]{1,0:T(8,128)(2,1)S(1)} collective-permute-done((bf16[128,2048]{1,0:T(8,128)(2,1)S(1)}, bf16[128,2048]{1,0:T(8,128)(2,1)S(1)}, u32[]{:S(2)}, u32[]{:S(2)}) %collective-permute-start.21) | collective-permute-done | bytes 524320 | tf_op jit(solution)/shard_map/ppermute | solution.py:22
  190.4 3.2 %out.5 = (bf16[128,2048]{1,0:T(8,128)(2,1)S(1)}, bf16[128,2048]{1,0:T(8,128)(2,1)S(1)}, bf16[128,2048]{1,0:T(8,128)(2,1)S(1)}, bf16[128,2048]{1,0:T(8,128)(2,1)S(1)}) custom-call(s32[2]{0:T(128)S(1)} %pad_add_fusion.place, bf16[1536,768]{1,0:T(8,128)(2,1)S(1)} %copy-done.1, f32[1536,128]{1,0:T(8,128)S(1)} %copy-done.2, bf16[768,1024]{1,0:T(8,128)(2,1)} %bitcast.3.own, ...), custom_call_target="tpu_custom_call" | custom-call | flops 1610612736 | bytes 6500000 | tf_op jit(solution)/shard_map/out/pallas_call | solution.py:186
  195.6 4.0 %collective-permute-start.30 = (bf16[128,2048]{1,0:T(8,128)(2,1)S(1)}, bf16[128,2048]{1,0:T(8,128)(2,1)S(1)}, u32[]{:S(2)}, u32[]{:S(2)}) collective-permute-start(bf16[128,2048]{1,0:T(8,128)(2,1)S(1)} %add_convert_fusion.3), channel_id=1, source_target_pairs={{0,24},{2,26},{4,28},{6,30},{8,0},{10,2},{12,4},{14,6},{16,8},{18,... | collective-permute-start | bytes 1572872 | tf_op jit(solution)/shard_map/ppermute | solution.py:22
  199.6 5.0 %collective-permute-done.26 = bf16[128,2048]{1,0:T(8,128)(2,1)S(1)} collective-permute-done((bf16[128,2048]{1,0:T(8,128)(2,1)S(1)}, bf16[128,2048]{1,0:T(8,128)(2,1)S(1)}, u32[]{:S(2)}, u32[]{:S(2)}) %collective-permute-start.26) | collective-permute-done | bytes 524320 | tf_op jit(solution)/shard_map/ppermute | solution.py:17
  204.9 3.3 %out.4 = (bf16[128,2048]{1,0:T(8,128)(2,1)S(1)}, bf16[128,2048]{1,0:T(8,128)(2,1)S(1)}, bf16[128,2048]{1,0:T(8,128)(2,1)S(1)}, bf16[128,2048]{1,0:T(8,128)(2,1)S(1)}) custom-call(s32[2]{0:T(128)S(1)} %pad_add_fusion.place, bf16[1536,768]{1,0:T(8,128)(2,1)S(1)} %copy-done.1, f32[1536,128]{1,0:T(8,128)S(1)} %copy-done.2, bf16[768,1024]{1,0:T(8,128)(2,1)} %bitcast.3.own, ...), custom_call_target="tpu_custom_call" | custom-call | flops 1610612736 | bytes 6500000 | tf_op jit(solution)/shard_map/out/pallas_call | solution.py:186
  210.3 4.2 %collective-permute-done.25 = bf16[128,2048]{1,0:T(8,128)(2,1)S(1)} collective-permute-done((bf16[128,2048]{1,0:T(8,128)(2,1)S(1)}, bf16[128,2048]{1,0:T(8,128)(2,1)S(1)}, u32[]{:S(2)}, u32[]{:S(2)}) %collective-permute-start.25) | collective-permute-done | bytes 524320 | tf_op jit(solution)/shard_map/ppermute | solution.py:17
  214.8 3.0 %collective-permute-done.30 = bf16[128,2048]{1,0:T(8,128)(2,1)S(1)} collective-permute-done((bf16[128,2048]{1,0:T(8,128)(2,1)S(1)}, bf16[128,2048]{1,0:T(8,128)(2,1)S(1)}, u32[]{:S(2)}, u32[]{:S(2)}) %collective-permute-start.30) | collective-permute-done | bytes 524320 | tf_op jit(solution)/shard_map/ppermute | solution.py:22
  217.8 2.2 collective-permute-done.27
  220.4 3.8 %collective-permute-start.31 = (bf16[128,2048]{1,0:T(8,128)(2,1)S(1)}, bf16[128,2048]{1,0:T(8,128)(2,1)S(1)}, u32[]{:S(2)}, u32[]{:S(2)}) collective-permute-start(bf16[128,2048]{1,0:T(8,128)(2,1)S(1)} %add_convert_fusion.2), channel_id=1, source_target_pairs={{0,24},{2,26},{4,28},{6,30},{8,0},{10,2},{12,4},{14,6},{16,8},{18,... | collective-permute-start | bytes 1572872 | tf_op jit(solution)/shard_map/ppermute | solution.py:22
  224.2 7.1 %collective-permute-done.19 = bf16[128,2048]{1,0:T(8,128)(2,1)S(1)} collective-permute-done((bf16[128,2048]{1,0:T(8,128)(2,1)S(1)}, bf16[128,2048]{1,0:T(8,128)(2,1)S(1)}, u32[]{:S(2)}, u32[]{:S(2)}) %collective-permute-start.19) | collective-permute-done | bytes 524320 | tf_op jit(solution)/shard_map/ppermute | solution.py:17
  233.1 4.1 %collective-permute-start.32 = (bf16[128,2048]{1,0:T(8,128)(2,1)S(1)}, bf16[128,2048]{1,0:T(8,128)(2,1)S(1)}, u32[]{:S(2)}, u32[]{:S(2)}) collective-permute-start(bf16[128,2048]{1,0:T(8,128)(2,1)S(1)} %add_convert_fusion.1), channel_id=1, source_target_pairs={{0,24},{2,26},{4,28},{6,30},{8,0},{10,2},{12,4},{14,6},{16,8},{18,... | collective-permute-start | bytes 1572872 | tf_op jit(solution)/shard_map/ppermute | solution.py:22
  237.2 3.3 %collective-permute-done.22 = bf16[128,2048]{1,0:T(8,128)(2,1)S(1)} collective-permute-done((bf16[128,2048]{1,0:T(8,128)(2,1)S(1)}, bf16[128,2048]{1,0:T(8,128)(2,1)S(1)}, u32[]{:S(2)}, u32[]{:S(2)}) %collective-permute-start.22) | collective-permute-done | bytes 524320 | tf_op jit(solution)/shard_map/ppermute | solution.py:17
  241.6 2.3 collective-permute-done.32
  (104 shorter events, 49.9 us)
Async XLA Ops:
  2.9 14.7 %collective-permute-start = (bf16[128,2176]{1,0:T(8,128)(2,1)}, bf16[128,2176]{1,0:T(8,128)(2,1)}, u32[]{:S(2)}, u32[]{:S(2)}) collective-permute-start(bf16[128,2176]{1,0:T(8,128)(2,1)} %fusion.1.refs_0_), channel_id=1, source_target_pairs={{0,8},{2,10},{4,12},{6,14},{8,16},{10,18},{12,20},{14,22},{16,24},... | collective-permute-start | bytes 1671176 | tf_op jit(solution)/shard_map/ppermute | solution.py:22
  4.5 14.4 %collective-permute-start.1 = (bf16[128,2176]{1,0:T(8,128)(2,1)}, bf16[128,2176]{1,0:T(8,128)(2,1)}, u32[]{:S(2)}, u32[]{:S(2)}) collective-permute-start(bf16[128,2176]{1,0:T(8,128)(2,1)} %fusion.1.refs_0_), channel_id=1, source_target_pairs={{0,2},{2,0},{4,6},{6,4},{8,10},{10,8},{12,14},{14,12},{16,18},{18,... | collective-permute-start | bytes 1671176 | tf_op jit(solution)/shard_map/ppermute | solution.py:17
  6.0 14.1 %collective-permute-start.2 = (bf16[128,2176]{1,0:T(8,128)(2,1)}, bf16[128,2176]{1,0:T(8,128)(2,1)}, u32[]{:S(2)}, u32[]{:S(2)}) collective-permute-start(bf16[128,2176]{1,0:T(8,128)(2,1)} %fusion.1.refs_0_), channel_id=1, source_target_pairs={{0,4},{2,6},{4,0},{6,2},{8,12},{10,14},{12,8},{14,10},{16,20},{18,... | collective-permute-start | bytes 1671176 | tf_op jit(solution)/shard_map/ppermute | solution.py:17
  20.1 13.1 %collective-permute-start.3 = (bf16[128,2176]{1,0:T(8,128)(2,1)}, bf16[128,2176]{1,0:T(8,128)(2,1)S(1)}, u32[]{:S(2)}, u32[]{:S(2)}) collective-permute-start(bf16[128,2176]{1,0:T(8,128)(2,1)} %collective-permute-done.refs_4_), channel_id=1, source_target_pairs={{0,8},{2,10},{4,12},{6,14},{8,16},{10,18},{12,20},{14,22},{16,24},... | collective-permute-start | bytes 1671176 | tf_op jit(solution)/shard_map/ppermute | solution.py:22
  21.7 12.8 %collective-permute-start.4 = (bf16[128,2176]{1,0:T(8,128)(2,1)}, bf16[128,2176]{1,0:T(8,128)(2,1)S(1)}, u32[]{:S(2)}, u32[]{:S(2)}) collective-permute-start(bf16[128,2176]{1,0:T(8,128)(2,1)} %collective-permute-done.refs_4_), channel_id=1, source_target_pairs={{0,2},{2,0},{4,6},{6,4},{8,10},{10,8},{12,14},{14,12},{16,18},{18,... | collective-permute-start | bytes 1671176 | tf_op jit(solution)/shard_map/ppermute | solution.py:17
  22.2 13.1 %collective-permute-start.5 = (bf16[128,2176]{1,0:T(8,128)(2,1)}, bf16[128,2176]{1,0:T(8,128)(2,1)S(1)}, u32[]{:S(2)}, u32[]{:S(2)}) collective-permute-start(bf16[128,2176]{1,0:T(8,128)(2,1)} %collective-permute-done.refs_4_), channel_id=1, source_target_pairs={{0,4},{2,6},{4,0},{6,2},{8,12},{10,14},{12,8},{14,10},{16,20},{18,... | collective-permute-start | bytes 1671176 | tf_op jit(solution)/shard_map/ppermute | solution.py:17
  35.3 11.7 %collective-permute-start.6 = (bf16[128,2176]{1,0:T(8,128)(2,1)S(1)}, bf16[128,2176]{1,0:T(8,128)(2,1)S(1)}, u32[]{:S(2)}, u32[]{:S(2)}) collective-permute-start(bf16[128,2176]{1,0:T(8,128)(2,1)S(1)} %collective-permute-done.3.refs_8_), channel_id=1, source_target_pairs={{0,8},{2,10},{4,12},{6,14},{8,16},{10,18},{12,20},{14,22},{16,24},... | collective-permute-start | bytes 1671176 | tf_op jit(solution)/shard_map/ppermute | solution.py:22
  35.7 11.7 %collective-permute-start.7 = (bf16[128,2176]{1,0:T(8,128)(2,1)S(1)}, bf16[128,2176]{1,0:T(8,128)(2,1)}, u32[]{:S(2)}, u32[]{:S(2)}) collective-permute-start(bf16[128,2176]{1,0:T(8,128)(2,1)S(1)} %collective-permute-done.3.refs_8_), channel_id=1, source_target_pairs={{0,2},{2,0},{4,6},{6,4},{8,10},{10,8},{12,14},{14,12},{16,18},{18,... | collective-permute-start | bytes 1671176 | tf_op jit(solution)/shard_map/ppermute | solution.py:17
  36.6 11.5 %collective-permute-start.8 = (bf16[128,2176]{1,0:T(8,128)(2,1)S(1)}, bf16[128,2176]{1,0:T(8,128)(2,1)}, u32[]{:S(2)}, u32[]{:S(2)}) collective-permute-start(bf16[128,2176]{1,0:T(8,128)(2,1)S(1)} %collective-permute-done.3.refs_8_), channel_id=1, source_target_pairs={{0,4},{2,6},{4,0},{6,2},{8,12},{10,14},{12,8},{14,10},{16,20},{18,... | collective-permute-start | bytes 1671176 | tf_op jit(solution)/shard_map/ppermute | solution.py:17
  48.1 75.4 %all-to-all-start = ((bf16[16,128,768]{2,1,0:T(8,128)(2,1)}), bf16[16,128,768]{2,1,0:T(8,128)(2,1)}, u32[]{:S(2)}, u32[]{:S(2)}) async-start(bf16[16,128,768]{2,1,0:T(8,128)(2,1)} %pad_maximum_fusion), calls=%async_computation | async-start | bytes 6291456 | tf_op jit(solution)/shard_map/all_to_all | solution.py:26
  57.0 20.6 %collective-permute-start.13 = (bf16[64,2176]{1,0:T(8,128)(2,1)S(1)}, bf16[64,2176]{1,0:T(8,128)(2,1)S(1)}, u32[]{:S(2)}, u32[]{:S(2)}) collective-permute-start(bf16[64,2176]{1,0:T(8,128)(2,1)S(1)} %slice.6), channel_id=1, source_target_pairs={{0,4},{2,6},{4,0},{6,2},{8,12},{10,14},{12,8},{14,10},{16,20},{18,... | collective-permute-start | bytes 835592 | tf_op jit(solution)/shard_map/ppermute | solution.py:17
  58.6 21.7 %collective-permute-start.14 = (bf16[64,2176]{1,0:T(8,128)(2,1)S(1)}, bf16[64,2176]{1,0:T(8,128)(2,1)S(1)}, u32[]{:S(2)}, u32[]{:S(2)}) collective-permute-start(bf16[64,2176]{1,0:T(8,128)(2,1)S(1)} %slice.7), channel_id=1, source_target_pairs={{0,2},{2,0},{4,6},{6,4},{8,10},{10,8},{12,14},{14,12},{16,18},{18,... | collective-permute-start | bytes 835592 | tf_op jit(solution)/shard_map/ppermute | solution.py:17
  60.1 40.5 %collective-permute-start.10 = (bf16[128,2176]{1,0:T(8,128)(2,1)}, bf16[128,2176]{1,0:T(8,128)(2,1)}, u32[]{:S(2)}, u32[]{:S(2)}) collective-permute-start(bf16[128,2176]{1,0:T(8,128)(2,1)} %copy-done.9), channel_id=1, source_target_pairs={{0,4},{2,6},{4,0},{6,2},{8,12},{10,14},{12,8},{14,10},{16,20},{18,... | collective-permute-start | bytes 1671176 | tf_op jit(solution)/shard_map/ppermute | solution.py:17
  61.6 51.5 %collective-permute-start.11 = (bf16[128,2176]{1,0:T(8,128)(2,1)}, bf16[128,2176]{1,0:T(8,128)(2,1)S(1)}, u32[]{:S(2)}, u32[]{:S(2)}) collective-permute-start(bf16[128,2176]{1,0:T(8,128)(2,1)} %collective-permute-done.1.refs_1_), channel_id=1, source_target_pairs={{0,4},{2,6},{4,0},{6,2},{8,12},{10,14},{12,8},{14,10},{16,20},{18,... | collective-permute-start | bytes 1671176 | tf_op jit(solution)/shard_map/ppermute | solution.py:17
  62.2 51.8 %collective-permute-start.12 = (bf16[128,2176]{1,0:T(8,128)(2,1)}, bf16[128,2176]{1,0:T(8,128)(2,1)S(1)}, u32[]{:S(2)}, u32[]{:S(2)}) collective-permute-start(bf16[128,2176]{1,0:T(8,128)(2,1)} %copy-done.7), channel_id=1, source_target_pairs={{0,2},{2,0},{4,6},{6,4},{8,10},{10,8},{12,14},{14,12},{16,18},{18,... | collective-permute-start | bytes 1671176 | tf_op jit(solution)/shard_map/ppermute | solution.py:17
  77.7 37.2 %collective-permute-start.9 = (bf16[128,2176]{1,0:T(8,128)(2,1)}, bf16[128,2176]{1,0:T(8,128)(2,1)S(1)}, u32[]{:S(2)}, u32[]{:S(2)}) collective-permute-start(bf16[128,2176]{1,0:T(8,128)(2,1)} %copy-done.9), channel_id=1, source_target_pairs={{0,2},{2,0},{4,6},{6,4},{8,10},{10,8},{12,14},{14,12},{16,18},{18,... | collective-permute-start | bytes 1671176 | tf_op jit(solution)/shard_map/ppermute | solution.py:17
  123.5 43.3 %all-to-all-start.1 = ((bf16[16,48,1024]{2,1,0:T(8,128)(2,1)}), bf16[16,48,1024]{2,1,0:T(8,128)(2,1)}, u32[]{:S(2)}, u32[]{:S(2)}) async-start(bf16[16,48,1024]{2,1,0:T(8,128)(2,1)} %constant_dynamic-slice_fusion), calls=%async_computation.1 | async-start | bytes 3145728 | tf_op jit(solution)/shard_map/all_to_all | solution.py:26
  129.2 27.0 %collective-permute-start.16 = (bf16[128,2176]{1,0:T(8,128)(2,1)}, bf16[128,2176]{1,0:T(8,128)(2,1)S(1)}, u32[]{:S(2)}, u32[]{:S(2)}) collective-permute-start(bf16[128,2176]{1,0:T(8,128)(2,1)} %collective-permute-done.10.refs_2_), channel_id=1, source_target_pairs={{0,2},{2,0},{4,6},{6,4},{8,10},{10,8},{12,14},{14,12},{16,18},{18,... | collective-permute-start | bytes 1671176 | tf_op jit(solution)/shard_map/ppermute | solution.py:17
  174.9 14.7 %collective-permute-start.21 = (bf16[128,2048]{1,0:T(8,128)(2,1)S(1)}, bf16[128,2048]{1,0:T(8,128)(2,1)S(1)}, u32[]{:S(2)}, u32[]{:S(2)}) collective-permute-start(bf16[128,2048]{1,0:T(8,128)(2,1)S(1)} %get-tuple-element.131), channel_id=1, source_target_pairs={{0,24},{2,26},{4,28},{6,30},{8,0},{10,2},{12,4},{14,6},{16,8},{18,... | collective-permute-start | bytes 1572872 | tf_op jit(solution)/shard_map/ppermute | solution.py:22
  175.0 19.0 %collective-permute-start.28 = (bf16[128,2048]{1,0:T(8,128)(2,1)S(1)}, bf16[128,2048]{1,0:T(8,128)(2,1)S(1)}, u32[]{:S(2)}, u32[]{:S(2)}) collective-permute-start(bf16[128,2048]{1,0:T(8,128)(2,1)S(1)} %get-tuple-element.143), channel_id=1, source_target_pairs={{0,2},{2,0},{4,6},{6,4},{8,10},{10,8},{12,14},{14,12},{16,18},{18,... | collective-permute-start | bytes 1572872 | tf_op jit(solution)/shard_map/ppermute | solution.py:17
  176.3 19.0 %collective-permute-start.29 = (bf16[128,2048]{1,0:T(8,128)(2,1)S(1)}, bf16[128,2048]{1,0:T(8,128)(2,1)S(1)}, u32[]{:S(2)}, u32[]{:S(2)}) collective-permute-start(bf16[128,2048]{1,0:T(8,128)(2,1)S(1)} %get-tuple-element.144), channel_id=1, source_target_pairs={{0,4},{2,6},{4,0},{6,2},{8,12},{10,14},{12,8},{14,10},{16,20},{18,... | collective-permute-start | bytes 1572872 | tf_op jit(solution)/shard_map/ppermute | solution.py:17
  189.7 14.9 %collective-permute-start.26 = (bf16[128,2048]{1,0:T(8,128)(2,1)S(1)}, bf16[128,2048]{1,0:T(8,128)(2,1)S(1)}, u32[]{:S(2)}, u32[]{:S(2)}) collective-permute-start(bf16[128,2048]{1,0:T(8,128)(2,1)S(1)} %add_convert_fusion.5), channel_id=1, source_target_pairs={{0,2},{2,0},{4,6},{6,4},{8,10},{10,8},{12,14},{14,12},{16,18},{18,... | collective-permute-start | bytes 1572872 | tf_op jit(solution)/shard_map/ppermute | solution.py:17
  193.6 14.9 %collective-permute-start.18 = (bf16[128,2048]{1,0:T(8,128)(2,1)S(1)}, bf16[128,2048]{1,0:T(8,128)(2,1)S(1)}, u32[]{:S(2)}, u32[]{:S(2)}) collective-permute-start(bf16[128,2048]{1,0:T(8,128)(2,1)S(1)} %get-tuple-element.128), channel_id=1, source_target_pairs={{0,24},{2,26},{4,28},{6,30},{8,0},{10,2},{12,4},{14,6},{16,8},{18,... | collective-permute-start | bytes 1572872 | tf_op jit(solution)/shard_map/ppermute | solution.py:22
  193.9 38.8 %collective-permute-start.24 = (bf16[128,2048]{1,0:T(8,128)(2,1)S(1)}, bf16[128,2048]{1,0:T(8,128)(2,1)S(1)}, u32[]{:S(2)}, u32[]{:S(2)}) collective-permute-start(bf16[128,2048]{1,0:T(8,128)(2,1)S(1)} %get-tuple-element.136), channel_id=1, source_target_pairs={{0,4},{2,6},{4,0},{6,2},{8,12},{10,14},{12,8},{14,10},{16,20},{18,... | collective-permute-start | bytes 1572872 | tf_op jit(solution)/shard_map/ppermute | solution.py:17
  194.0 20.5 %collective-permute-start.25 = (bf16[128,2048]{1,0:T(8,128)(2,1)S(1)}, bf16[128,2048]{1,0:T(8,128)(2,1)S(1)}, u32[]{:S(2)}, u32[]{:S(2)}) collective-permute-start(bf16[128,2048]{1,0:T(8,128)(2,1)S(1)} %get-tuple-element.139), channel_id=1, source_target_pairs={{0,2},{2,0},{4,6},{6,4},{8,10},{10,8},{12,14},{14,12},{16,18},{18,... | collective-permute-start | bytes 1572872 | tf_op jit(solution)/shard_map/ppermute | solution.py:17
  195.6 22.3 %collective-permute-start.30 = (bf16[128,2048]{1,0:T(8,128)(2,1)S(1)}, bf16[128,2048]{1,0:T(8,128)(2,1)S(1)}, u32[]{:S(2)}, u32[]{:S(2)}) collective-permute-start(bf16[128,2048]{1,0:T(8,128)(2,1)S(1)} %add_convert_fusion.3), channel_id=1, source_target_pairs={{0,24},{2,26},{4,28},{6,30},{8,0},{10,2},{12,4},{14,6},{16,8},{18,... | collective-permute-start | bytes 1572872 | tf_op jit(solution)/shard_map/ppermute | solution.py:22
  204.8 15.3 %collective-permute-start.27 = (bf16[128,2048]{1,0:T(8,128)(2,1)S(1)}, bf16[128,2048]{1,0:T(8,128)(2,1)S(1)}, u32[]{:S(2)}, u32[]{:S(2)}) collective-permute-start(bf16[128,2048]{1,0:T(8,128)(2,1)S(1)} %add_convert_fusion.4), channel_id=1, source_target_pairs={{0,4},{2,6},{4,0},{6,2},{8,12},{10,14},{12,8},{14,10},{16,20},{18,... | collective-permute-start | bytes 1572872 | tf_op jit(solution)/shard_map/ppermute | solution.py:17
  208.7 22.6 %collective-permute-start.19 = (bf16[128,2048]{1,0:T(8,128)(2,1)S(1)}, bf16[128,2048]{1,0:T(8,128)(2,1)S(1)}, u32[]{:S(2)}, u32[]{:S(2)}) collective-permute-start(bf16[128,2048]{1,0:T(8,128)(2,1)S(1)} %add_convert_fusion.7), channel_id=1, source_target_pairs={{0,4},{2,6},{4,0},{6,2},{8,12},{10,14},{12,8},{14,10},{16,20},{18,... | collective-permute-start | bytes 1572872 | tf_op jit(solution)/shard_map/ppermute | solution.py:17
  214.5 18.3 %collective-permute-start.23 = (bf16[128,2048]{1,0:T(8,128)(2,1)S(1)}, bf16[128,2048]{1,0:T(8,128)(2,1)S(1)}, u32[]{:S(2)}, u32[]{:S(2)}) collective-permute-start(bf16[128,2048]{1,0:T(8,128)(2,1)S(1)} %get-tuple-element.135), channel_id=1, source_target_pairs={{0,2},{2,0},{4,6},{6,4},{8,10},{10,8},{12,14},{14,12},{16,18},{18,... | collective-permute-start | bytes 1572872 | tf_op jit(solution)/shard_map/ppermute | solution.py:17
  220.4 12.4 %collective-permute-start.31 = (bf16[128,2048]{1,0:T(8,128)(2,1)S(1)}, bf16[128,2048]{1,0:T(8,128)(2,1)S(1)}, u32[]{:S(2)}, u32[]{:S(2)}) collective-permute-start(bf16[128,2048]{1,0:T(8,128)(2,1)S(1)} %add_convert_fusion.2), channel_id=1, source_target_pairs={{0,24},{2,26},{4,28},{6,30},{8,0},{10,2},{12,4},{14,6},{16,8},{18,... | collective-permute-start | bytes 1572872 | tf_op jit(solution)/shard_map/ppermute | solution.py:22
  224.2 16.4 %collective-permute-start.22 = (bf16[128,2048]{1,0:T(8,128)(2,1)S(1)}, bf16[128,2048]{1,0:T(8,128)(2,1)S(1)}, u32[]{:S(2)}, u32[]{:S(2)}) collective-permute-start(bf16[128,2048]{1,0:T(8,128)(2,1)S(1)} %get-tuple-element.132), channel_id=1, source_target_pairs={{0,4},{2,6},{4,0},{6,2},{8,12},{10,14},{12,8},{14,10},{16,20},{18,... | collective-permute-start | bytes 1572872 | tf_op jit(solution)/shard_map/ppermute | solution.py:17
  233.1 10.8 %collective-permute-start.32 = (bf16[128,2048]{1,0:T(8,128)(2,1)S(1)}, bf16[128,2048]{1,0:T(8,128)(2,1)S(1)}, u32[]{:S(2)}, u32[]{:S(2)}) collective-permute-start(bf16[128,2048]{1,0:T(8,128)(2,1)S(1)} %add_convert_fusion.1), channel_id=1, source_target_pairs={{0,24},{2,26},{4,28},{6,30},{8,0},{10,2},{12,4},{14,6},{16,8},{18,... | collective-permute-start | bytes 1572872 | tf_op jit(solution)/shard_map/ppermute | solution.py:22
  (23 other events, 104.5 us)

commit v6 on v5

--- a/solution.py
+++ b/solution.py
@@ -207,6 +207,7 @@
     beside, corner = [None] * line, [None] * line
     for s in reversed(range(1, line, 2)):
         beside[s] = turn(outs[s][3], -1)
+    beside[-1] = after(beside[-1], *(outs[s][0] for s in range(1, line, 2)))
     from_x, from_y = [None] * line, [None] * line
     for s in reversed(range(0, line, 2)):
         over = add(outs[s][3], beside[s + 1]) if s + 1 < line else outs[s][3]

time: 249 us -> 246 us (0.988)
  starting transfers between devices: 49.4 us -> 43.8 us
  waiting for transfers between devices: 134 us -> 137 us
    ppermute x23, waiting for transfers between devices: 79.3 us -> 90.4 us  [flip(): return lax.ppermute(x, 'expert', [(i, i ^ bit) for i in range(size)])]
    ppermute x8, waiting for transfers between devices: 40.1 us -> 32 us  [turn(): lax.ppermute(x, 'expert', [(i, (i + 4 * by) % size) for i in range(size)])]
    ppermute x8, starting transfers between devices: 15.9 us -> 10.7 us  [turn(): lax.ppermute(x, 'expert', [(i, (i + 4 * by) % size) for i in range(size)])]
  transfers between devices with their start and end apart: 35 -> 35, of which waited for: 25 -> 23; matrix products, arithmetic and copies ran while one was open for 4% -> 4% of each run, Pallas kernels for 13% -> 13%
where the time goes in v6:
time: 246 us; the launch traced here: 242 us
  waiting for transfers between devices  137 us (56%)
  starting transfers between devices  43.8 us (18%)
  Pallas kernels  34.8 us (14%)
  local copies, waits for them, and re-layouts  18.4 us (7%)
  other arithmetic  8.29 us (3%)
    ppermute x23, waiting for transfers between devices, flip(): return lax.ppermute(x, 'expert', [(i, i ^ bit) for i in range(size)])  90.4 us
    ppermute x8, waiting for transfers between devices, turn(): lax.ppermute(x, 'expert', [(i, (i + 4 * by) % size) for i in range(size)])  32 us
    pallas_call x2, Pallas kernels, hidden_of(): pl.pallas_call(functools.partial(hidden_kernel, len(gathered), rows, mode...  21.7 us
    ppermute x23, starting transfers between devices, flip(): return lax.ppermute(x, 'expert', [(i, i ^ bit) for i in range(size)])  19.6 us
    all_to_all x2, starting transfers between devices, spread(): return lax.all_to_all(w, 'expert', split_axis=0, concat_axis=0, tiled=True)  13.5 us
    pallas_call x4, Pallas kernels, local(): pl.pallas_call(functools.partial(out_kernel, rows), out_shape=[jax.ShapeD...  13.2 us
    unnamed x40, local copies, waits for them, and re-layouts  13.1 us
    all_to_all x2, waiting for transfers between devices, spread(): return lax.all_to_all(w, 'expert', split_axis=0, concat_axis=0, tiled=True)  10.9 us
  transfers between devices with their start and end apart: 35, of which 23 were waited for; matrix products, arithmetic and copies ran while one was open for 4% of the time, Pallas kernels for 13%

profile of v6, /device:TPU:12, one launch (start us, length us, event | category | flops | bytes accessed | tf_op | source)
XLA Modules:
  0.0 242.4 jit_solution(13132949033771211725)
XLA Ops:
  1.0 1.9 fusion.1.refs_0_
  8.9 1.9 constant_dynamic-slice_fusion.1
  10.8 2.0 pad_maximum_fusion
  12.9 4.7 %collective-permute-done.refs_4_ = bf16[128,2176]{1,0:T(8,128)(2,1)} collective-permute-done((bf16[128,2176]{1,0:T(8,128)(2,1)}, bf16[128,2176]{1,0:T(8,128)(2,1)}, u32[]{:S(2)}, u32[]{:S(2)}) %collective-permute-start) | collective-permute-done | bytes 557088 | tf_op jit(solution)/shard_map/ppermute | solution.py:22
  22.7 10.5 %collective-permute-done.3.refs_8_ = bf16[128,2176]{1,0:T(8,128)(2,1)S(1)} collective-permute-done((bf16[128,2176]{1,0:T(8,128)(2,1)}, bf16[128,2176]{1,0:T(8,128)(2,1)S(1)}, u32[]{:S(2)}, u32[]{:S(2)}) %collective-permute-start.3) | collective-permute-done | bytes 557088 | tf_op jit(solution)/shard_map/ppermute | solution.py:22
  37.9 9.1 %collective-permute-done.6.refs_0_ = bf16[128,2176]{1,0:T(8,128)(2,1)S(1)} collective-permute-done((bf16[128,2176]{1,0:T(8,128)(2,1)S(1)}, bf16[128,2176]{1,0:T(8,128)(2,1)S(1)}, u32[]{:S(2)}, u32[]{:S(2)}) %collective-permute-start.6) | collective-permute-done | bytes 557088 | tf_op jit(solution)/shard_map/ppermute | solution.py:22
  48.1 7.9 %all-to-all-start = ((bf16[16,128,768]{2,1,0:T(8,128)(2,1)}), bf16[16,128,768]{2,1,0:T(8,128)(2,1)}, u32[]{:S(2)}, u32[]{:S(2)}) async-start(bf16[16,128,768]{2,1,0:T(8,128)(2,1)} %pad_maximum_fusion), calls=%async_computation | async-start | bytes 6291456 | tf_op jit(solution)/shard_map/all_to_all | solution.py:26
  62.7 14.9 %collective-permute-done.13 = bf16[64,2176]{1,0:T(8,128)(2,1)S(1)} collective-permute-done((bf16[64,2176]{1,0:T(8,128)(2,1)S(1)}, bf16[64,2176]{1,0:T(8,128)(2,1)S(1)}, u32[]{:S(2)}, u32[]{:S(2)}) %collective-permute-start.13) | collective-permute-done | bytes 278560 | tf_op jit(solution)/shard_map/ppermute | solution.py:17
  77.7 2.7 %collective-permute-start.9 = (bf16[128,2176]{1,0:T(8,128)(2,1)}, bf16[128,2176]{1,0:T(8,128)(2,1)S(1)}, u32[]{:S(2)}, u32[]{:S(2)}) collective-permute-start(bf16[128,2176]{1,0:T(8,128)(2,1)} %copy-done.9), channel_id=1, source_target_pairs={{0,2},{2,0},{4,6},{6,4},{8,10},{10,8},{12,14},{14,12},{16,18},{18,... | collective-permute-start | bytes 1671176 | tf_op jit(solution)/shard_map/ppermute | solution.py:17
  81.2 19.5 %collective-permute-done.10.refs_2_ = bf16[128,2176]{1,0:T(8,128)(2,1)} collective-permute-done((bf16[128,2176]{1,0:T(8,128)(2,1)}, bf16[128,2176]{1,0:T(8,128)(2,1)}, u32[]{:S(2)}, u32[]{:S(2)}) %collective-permute-start.10) | collective-permute-done | bytes 557088 | tf_op jit(solution)/shard_map/ppermute | solution.py:17
  100.7 12.4 %collective-permute-done.11.refs_3_ = bf16[128,2176]{1,0:T(8,128)(2,1)S(1)} collective-permute-done((bf16[128,2176]{1,0:T(8,128)(2,1)}, bf16[128,2176]{1,0:T(8,128)(2,1)S(1)}, u32[]{:S(2)}, u32[]{:S(2)}) %collective-permute-start.11) | collective-permute-done | bytes 557088 | tf_op jit(solution)/shard_map/ppermute | solution.py:17
  115.6 7.8 %all-to-all-done = bf16[16,128,768]{2,1,0:T(8,128)(2,1)} async-done(((bf16[16,128,768]{2,1,0:T(8,128)(2,1)}), bf16[16,128,768]{2,1,0:T(8,128)(2,1)}, u32[]{:S(2)}, u32[]{:S(2)}) %all-to-all-start) | async-done | bytes 3145760 | tf_op jit(solution)/shard_map/all_to_all | solution.py:26
  123.5 5.6 %all-to-all-start.1 = ((bf16[16,48,1024]{2,1,0:T(8,128)(2,1)}), bf16[16,48,1024]{2,1,0:T(8,128)(2,1)}, u32[]{:S(2)}, u32[]{:S(2)}) async-start(bf16[16,48,1024]{2,1,0:T(8,128)(2,1)} %constant_dynamic-slice_fusion), calls=%async_computation.1 | async-start | bytes 3145728 | tf_op jit(solution)/shard_map/all_to_all | solution.py:26
  135.9 15.1 %hidden.2 = (bf16[1536,768]{1,0:T(8,128)(2,1)}, f32[1536,128]{1,0:T(8,128)}) custom-call(s32[2]{0:T(128)S(1)} %pad_add_fusion.place, bf16[128,2176]{1,0:T(8,128)(2,1)} %fusion.1.refs_0_, bf16[128,2176]{1,0:T(8,128)(2,1)} %collective-permute-done.1.refs_1_, bf16[128,2176]{1,0:T(8,128)(2,1)} %collective-permute-done.2.refs_2_, ...), custom_call_target="tpu_custom_call" | custom-call | flops 9663676416 | bytes 10000000 | tf_op jit(solution)/shard_map/hidden/pallas_call | solution.py:151
  151.0 5.2 %collective-permute-done.16.refs_3_ = bf16[128,2176]{1,0:T(8,128)(2,1)S(1)} collective-permute-done((bf16[128,2176]{1,0:T(8,128)(2,1)}, bf16[128,2176]{1,0:T(8,128)(2,1)S(1)}, u32[]{:S(2)}, u32[]{:S(2)}) %collective-permute-start.16) | collective-permute-done | bytes 557088 | tf_op jit(solution)/shard_map/ppermute | solution.py:17
  156.2 6.6 %hidden.3 = (bf16[512,768]{1,0:T(8,128)(2,1)S(1)}, f32[512,128]{1,0:T(8,128)S(1)}) custom-call(s32[2]{0:T(128)S(1)} %pad_add_fusion.place, bf16[128,2176]{1,0:T(8,128)(2,1)S(1)} %copy-done.10, bf16[128,2176]{1,0:T(8,128)(2,1)S(1)} %copy-done.14, bf16[128,2176]{1,0:T(8,128)(2,1)} %collective-permute-done.10.refs_2_, ...), custom_call_target="tpu_custom_call" | custom-call | flops 3221225472 | bytes 10000000 | tf_op jit(solution)/shard_map/hidden/pallas_call | solution.py:151
  163.7 3.1 %all-to-all-done.1 = bf16[16,48,1024]{2,1,0:T(8,128)(2,1)} async-done(((bf16[16,48,1024]{2,1,0:T(8,128)(2,1)}), bf16[16,48,1024]{2,1,0:T(8,128)(2,1)}, u32[]{:S(2)}, u32[]{:S(2)}) %all-to-all-start.1) | async-done | bytes 1572896 | tf_op jit(solution)/shard_map/all_to_all | solution.py:26
  166.7 3.6 %collective-permute-done.17.other = bf16[768,1024]{1,0:T(8,128)(2,1)S(1)} collective-permute-done((bf16[768,1024]{1,0:T(8,128)(2,1)}, bf16[768,1024]{1,0:T(8,128)(2,1)S(1)}, u32[]{:S(2)}, u32[]{:S(2)}) %collective-permute-start.17) | collective-permute-done | bytes 1572896 | tf_op jit(solution)/shard_map/ppermute | solution.py:12
  171.5 3.4 %out.6 = (bf16[128,2048]{1,0:T(8,128)(2,1)S(1)}, bf16[128,2048]{1,0:T(8,128)(2,1)S(1)}, bf16[128,2048]{1,0:T(8,128)(2,1)S(1)}, bf16[128,2048]{1,0:T(8,128)(2,1)S(1)}) custom-call(s32[2]{0:T(128)S(1)} %pad_add_fusion.place, bf16[512,768]{1,0:T(8,128)(2,1)S(1)} %copy-done.18, f32[512,128]{1,0:T(8,128)S(1)} %get-tuple-element.131.scale, ...), custom_call_target="tpu_custom_call" | custom-call | flops 1610612736 | bytes 6500000 | tf_op jit(solution)/shard_map/out/pallas_call | solution.py:186
  176.3 3.2 %out.5 = (bf16[128,2048]{1,0:T(8,128)(2,1)S(1)}, bf16[128,2048]{1,0:T(8,128)(2,1)S(1)}, bf16[128,2048]{1,0:T(8,128)(2,1)S(1)}, bf16[128,2048]{1,0:T(8,128)(2,1)S(1)}) custom-call(s32[2]{0:T(128)S(1)} %pad_add_fusion.place, bf16[1536,768]{1,0:T(8,128)(2,1)S(1)} %copy-done.1, f32[1536,128]{1,0:T(8,128)S(1)} %copy-done.2, bf16[768,1024]{1,0:T(8,128)(2,1)} %bitcast.3.own, ...), custom_call_target="tpu_custom_call" | custom-call | flops 1610612736 | bytes 6500000 | tf_op jit(solution)/shard_map/out/pallas_call | solution.py:186
  179.6 3.3 %out.7 = (bf16[128,2048]{1,0:T(8,128)(2,1)S(1)}, bf16[128,2048]{1,0:T(8,128)(2,1)S(1)}, bf16[128,2048]{1,0:T(8,128)(2,1)S(1)}, bf16[128,2048]{1,0:T(8,128)(2,1)S(1)}) custom-call(s32[2]{0:T(128)S(1)} %pad_add_fusion.place, bf16[1536,768]{1,0:T(8,128)(2,1)S(1)} %copy-done.1, f32[1536,128]{1,0:T(8,128)S(1)} %copy-done.2, bf16[768,1024]{1,0:T(8,128)(2,1)} %bitcast.3.own, ...), custom_call_target="tpu_custom_call" | custom-call | flops 1610612736 | bytes 6500000 | tf_op jit(solution)/shard_map/out/pallas_call | solution.py:186
  182.8 6.8 %collective-permute-done.21 = bf16[128,2048]{1,0:T(8,128)(2,1)S(1)} collective-permute-done((bf16[128,2048]{1,0:T(8,128)(2,1)S(1)}, bf16[128,2048]{1,0:T(8,128)(2,1)S(1)}, u32[]{:S(2)}, u32[]{:S(2)}) %collective-permute-start.21) | collective-permute-done | bytes 524320 | tf_op jit(solution)/shard_map/ppermute | solution.py:22
  192.2 4.1 %collective-permute-start.30 = (bf16[128,2048]{1,0:T(8,128)(2,1)S(1)}, bf16[128,2048]{1,0:T(8,128)(2,1)S(1)}, u32[]{:S(2)}, u32[]{:S(2)}) collective-permute-start(bf16[128,2048]{1,0:T(8,128)(2,1)S(1)} %add_convert_fusion.3), channel_id=1, source_target_pairs={{0,24},{2,26},{4,28},{6,30},{8,0},{10,2},{12,4},{14,6},{16,8},{18,... | collective-permute-start | bytes 1572872 | tf_op jit(solution)/shard_map/ppermute | solution.py:22
  196.3 8.4 %collective-permute-done.26 = bf16[128,2048]{1,0:T(8,128)(2,1)S(1)} collective-permute-done((bf16[128,2048]{1,0:T(8,128)(2,1)S(1)}, bf16[128,2048]{1,0:T(8,128)(2,1)S(1)}, u32[]{:S(2)}, u32[]{:S(2)}) %collective-permute-start.26) | collective-permute-done | bytes 524320 | tf_op jit(solution)/shard_map/ppermute | solution.py:17
  204.9 3.3 %out.4 = (bf16[128,2048]{1,0:T(8,128)(2,1)S(1)}, bf16[128,2048]{1,0:T(8,128)(2,1)S(1)}, bf16[128,2048]{1,0:T(8,128)(2,1)S(1)}, bf16[128,2048]{1,0:T(8,128)(2,1)S(1)}) custom-call(s32[2]{0:T(128)S(1)} %pad_add_fusion.place, bf16[1536,768]{1,0:T(8,128)(2,1)S(1)} %copy-done.1, f32[1536,128]{1,0:T(8,128)S(1)} %copy-done.2, bf16[768,1024]{1,0:T(8,128)(2,1)} %bitcast.3.own, ...), custom_call_target="tpu_custom_call" | custom-call | flops 1610612736 | bytes 6500000 | tf_op jit(solution)/shard_map/out/pallas_call | solution.py:186
  208.3 2.1 collective-permute-start.19
  210.3 4.2 %collective-permute-done.25 = bf16[128,2048]{1,0:T(8,128)(2,1)S(1)} collective-permute-done((bf16[128,2048]{1,0:T(8,128)(2,1)S(1)}, bf16[128,2048]{1,0:T(8,128)(2,1)S(1)}, u32[]{:S(2)}, u32[]{:S(2)}) %collective-permute-start.25) | collective-permute-done | bytes 524320 | tf_op jit(solution)/shard_map/ppermute | solution.py:17
  214.8 4.9 %collective-permute-done.27 = bf16[128,2048]{1,0:T(8,128)(2,1)S(1)} collective-permute-done((bf16[128,2048]{1,0:T(8,128)(2,1)S(1)}, bf16[128,2048]{1,0:T(8,128)(2,1)S(1)}, u32[]{:S(2)}, u32[]{:S(2)}) %collective-permute-start.27) | collective-permute-done | bytes 524320 | tf_op jit(solution)/shard_map/ppermute | solution.py:17
  220.9 10.0 %collective-permute-done.19 = bf16[128,2048]{1,0:T(8,128)(2,1)S(1)} collective-permute-done((bf16[128,2048]{1,0:T(8,128)(2,1)S(1)}, bf16[128,2048]{1,0:T(8,128)(2,1)S(1)}, u32[]{:S(2)}, u32[]{:S(2)}) %collective-permute-start.19) | collective-permute-done | bytes 524320 | tf_op jit(solution)/shard_map/ppermute | solution.py:17
  232.1 1.9 collective-permute-start.32
  233.9 4.6 %collective-permute-done.22 = bf16[128,2048]{1,0:T(8,128)(2,1)S(1)} collective-permute-done((bf16[128,2048]{1,0:T(8,128)(2,1)S(1)}, bf16[128,2048]{1,0:T(8,128)(2,1)S(1)}, u32[]{:S(2)}, u32[]{:S(2)}) %collective-permute-start.22) | collective-permute-done | bytes 524320 | tf_op jit(solution)/shard_map/ppermute | solution.py:17
  238.5 1.8 collective-permute-done.20
  (104 shorter events, 45.9 us)
Async XLA Ops:
  2.9 14.7 %collective-permute-start = (bf16[128,2176]{1,0:T(8,128)(2,1)}, bf16[128,2176]{1,0:T(8,128)(2,1)}, u32[]{:S(2)}, u32[]{:S(2)}) collective-permute-start(bf16[128,2176]{1,0:T(8,128)(2,1)} %fusion.1.refs_0_), channel_id=1, source_target_pairs={{0,8},{2,10},{4,12},{6,14},{8,16},{10,18},{12,20},{14,22},{16,24},... | collective-permute-start | bytes 1671176 | tf_op jit(solution)/shard_map/ppermute | solution.py:22
  4.5 14.4 %collective-permute-start.1 = (bf16[128,2176]{1,0:T(8,128)(2,1)}, bf16[128,2176]{1,0:T(8,128)(2,1)}, u32[]{:S(2)}, u32[]{:S(2)}) collective-permute-start(bf16[128,2176]{1,0:T(8,128)(2,1)} %fusion.1.refs_0_), channel_id=1, source_target_pairs={{0,2},{2,0},{4,6},{6,4},{8,10},{10,8},{12,14},{14,12},{16,18},{18,... | collective-permute-start | bytes 1671176 | tf_op jit(solution)/shard_map/ppermute | solution.py:17
  6.0 14.1 %collective-permute-start.2 = (bf16[128,2176]{1,0:T(8,128)(2,1)}, bf16[128,2176]{1,0:T(8,128)(2,1)}, u32[]{:S(2)}, u32[]{:S(2)}) collective-permute-start(bf16[128,2176]{1,0:T(8,128)(2,1)} %fusion.1.refs_0_), channel_id=1, source_target_pairs={{0,4},{2,6},{4,0},{6,2},{8,12},{10,14},{12,8},{14,10},{16,20},{18,... | collective-permute-start | bytes 1671176 | tf_op jit(solution)/shard_map/ppermute | solution.py:17
  20.1 13.1 %collective-permute-start.3 = (bf16[128,2176]{1,0:T(8,128)(2,1)}, bf16[128,2176]{1,0:T(8,128)(2,1)S(1)}, u32[]{:S(2)}, u32[]{:S(2)}) collective-permute-start(bf16[128,2176]{1,0:T(8,128)(2,1)} %collective-permute-done.refs_4_), channel_id=1, source_target_pairs={{0,8},{2,10},{4,12},{6,14},{8,16},{10,18},{12,20},{14,22},{16,24},... | collective-permute-start | bytes 1671176 | tf_op jit(solution)/shard_map/ppermute | solution.py:22
  21.7 12.8 %collective-permute-start.4 = (bf16[128,2176]{1,0:T(8,128)(2,1)}, bf16[128,2176]{1,0:T(8,128)(2,1)S(1)}, u32[]{:S(2)}, u32[]{:S(2)}) collective-permute-start(bf16[128,2176]{1,0:T(8,128)(2,1)} %collective-permute-done.refs_4_), channel_id=1, source_target_pairs={{0,2},{2,0},{4,6},{6,4},{8,10},{10,8},{12,14},{14,12},{16,18},{18,... | collective-permute-start | bytes 1671176 | tf_op jit(solution)/shard_map/ppermute | solution.py:17
  22.2 13.1 %collective-permute-start.5 = (bf16[128,2176]{1,0:T(8,128)(2,1)}, bf16[128,2176]{1,0:T(8,128)(2,1)S(1)}, u32[]{:S(2)}, u32[]{:S(2)}) collective-permute-start(bf16[128,2176]{1,0:T(8,128)(2,1)} %collective-permute-done.refs_4_), channel_id=1, source_target_pairs={{0,4},{2,6},{4,0},{6,2},{8,12},{10,14},{12,8},{14,10},{16,20},{18,... | collective-permute-start | bytes 1671176 | tf_op jit(solution)/shard_map/ppermute | solution.py:17
  35.3 11.7 %collective-permute-start.6 = (bf16[128,2176]{1,0:T(8,128)(2,1)S(1)}, bf16[128,2176]{1,0:T(8,128)(2,1)S(1)}, u32[]{:S(2)}, u32[]{:S(2)}) collective-permute-start(bf16[128,2176]{1,0:T(8,128)(2,1)S(1)} %collective-permute-done.3.refs_8_), channel_id=1, source_target_pairs={{0,8},{2,10},{4,12},{6,14},{8,16},{10,18},{12,20},{14,22},{16,24},... | collective-permute-start | bytes 1671176 | tf_op jit(solution)/shard_map/ppermute | solution.py:22
  35.7 11.7 %collective-permute-start.7 = (bf16[128,2176]{1,0:T(8,128)(2,1)S(1)}, bf16[128,2176]{1,0:T(8,128)(2,1)}, u32[]{:S(2)}, u32[]{:S(2)}) collective-permute-start(bf16[128,2176]{1,0:T(8,128)(2,1)S(1)} %collective-permute-done.3.refs_8_), channel_id=1, source_target_pairs={{0,2},{2,0},{4,6},{6,4},{8,10},{10,8},{12,14},{14,12},{16,18},{18,... | collective-permute-start | bytes 1671176 | tf_op jit(solution)/shard_map/ppermute | solution.py:17
  36.6 11.5 %collective-permute-start.8 = (bf16[128,2176]{1,0:T(8,128)(2,1)S(1)}, bf16[128,2176]{1,0:T(8,128)(2,1)}, u32[]{:S(2)}, u32[]{:S(2)}) collective-permute-start(bf16[128,2176]{1,0:T(8,128)(2,1)S(1)} %collective-permute-done.3.refs_8_), channel_id=1, source_target_pairs={{0,4},{2,6},{4,0},{6,2},{8,12},{10,14},{12,8},{14,10},{16,20},{18,... | collective-permute-start | bytes 1671176 | tf_op jit(solution)/shard_map/ppermute | solution.py:17
  48.1 75.4 %all-to-all-start = ((bf16[16,128,768]{2,1,0:T(8,128)(2,1)}), bf16[16,128,768]{2,1,0:T(8,128)(2,1)}, u32[]{:S(2)}, u32[]{:S(2)}) async-start(bf16[16,128,768]{2,1,0:T(8,128)(2,1)} %pad_maximum_fusion), calls=%async_computation | async-start | bytes 6291456 | tf_op jit(solution)/shard_map/all_to_all | solution.py:26
  57.0 20.6 %collective-permute-start.13 = (bf16[64,2176]{1,0:T(8,128)(2,1)S(1)}, bf16[64,2176]{1,0:T(8,128)(2,1)S(1)}, u32[]{:S(2)}, u32[]{:S(2)}) collective-permute-start(bf16[64,2176]{1,0:T(8,128)(2,1)S(1)} %slice.6), channel_id=1, source_target_pairs={{0,4},{2,6},{4,0},{6,2},{8,12},{10,14},{12,8},{14,10},{16,20},{18,... | collective-permute-start | bytes 835592 | tf_op jit(solution)/shard_map/ppermute | solution.py:17
  58.6 21.7 %collective-permute-start.14 = (bf16[64,2176]{1,0:T(8,128)(2,1)S(1)}, bf16[64,2176]{1,0:T(8,128)(2,1)S(1)}, u32[]{:S(2)}, u32[]{:S(2)}) collective-permute-start(bf16[64,2176]{1,0:T(8,128)(2,1)S(1)} %slice.7), channel_id=1, source_target_pairs={{0,2},{2,0},{4,6},{6,4},{8,10},{10,8},{12,14},{14,12},{16,18},{18,... | collective-permute-start | bytes 835592 | tf_op jit(solution)/shard_map/ppermute | solution.py:17
  60.1 40.5 %collective-permute-start.10 = (bf16[128,2176]{1,0:T(8,128)(2,1)}, bf16[128,2176]{1,0:T(8,128)(2,1)}, u32[]{:S(2)}, u32[]{:S(2)}) collective-permute-start(bf16[128,2176]{1,0:T(8,128)(2,1)} %copy-done.9), channel_id=1, source_target_pairs={{0,4},{2,6},{4,0},{6,2},{8,12},{10,14},{12,8},{14,10},{16,20},{18,... | collective-permute-start | bytes 1671176 | tf_op jit(solution)/shard_map/ppermute | solution.py:17
  61.6 51.5 %collective-permute-start.11 = (bf16[128,2176]{1,0:T(8,128)(2,1)}, bf16[128,2176]{1,0:T(8,128)(2,1)S(1)}, u32[]{:S(2)}, u32[]{:S(2)}) collective-permute-start(bf16[128,2176]{1,0:T(8,128)(2,1)} %collective-permute-done.1.refs_1_), channel_id=1, source_target_pairs={{0,4},{2,6},{4,0},{6,2},{8,12},{10,14},{12,8},{14,10},{16,20},{18,... | collective-permute-start | bytes 1671176 | tf_op jit(solution)/shard_map/ppermute | solution.py:17
  62.2 51.8 %collective-permute-start.12 = (bf16[128,2176]{1,0:T(8,128)(2,1)}, bf16[128,2176]{1,0:T(8,128)(2,1)S(1)}, u32[]{:S(2)}, u32[]{:S(2)}) collective-permute-start(bf16[128,2176]{1,0:T(8,128)(2,1)} %copy-done.7), channel_id=1, source_target_pairs={{0,2},{2,0},{4,6},{6,4},{8,10},{10,8},{12,14},{14,12},{16,18},{18,... | collective-permute-start | bytes 1671176 | tf_op jit(solution)/shard_map/ppermute | solution.py:17
  77.7 37.2 %collective-permute-start.9 = (bf16[128,2176]{1,0:T(8,128)(2,1)}, bf16[128,2176]{1,0:T(8,128)(2,1)S(1)}, u32[]{:S(2)}, u32[]{:S(2)}) collective-permute-start(bf16[128,2176]{1,0:T(8,128)(2,1)} %copy-done.9), channel_id=1, source_target_pairs={{0,2},{2,0},{4,6},{6,4},{8,10},{10,8},{12,14},{14,12},{16,18},{18,... | collective-permute-start | bytes 1671176 | tf_op jit(solution)/shard_map/ppermute | solution.py:17
  123.5 43.3 %all-to-all-start.1 = ((bf16[16,48,1024]{2,1,0:T(8,128)(2,1)}), bf16[16,48,1024]{2,1,0:T(8,128)(2,1)}, u32[]{:S(2)}, u32[]{:S(2)}) async-start(bf16[16,48,1024]{2,1,0:T(8,128)(2,1)} %constant_dynamic-slice_fusion), calls=%async_computation.1 | async-start | bytes 3145728 | tf_op jit(solution)/shard_map/all_to_all | solution.py:26
  129.2 27.0 %collective-permute-start.16 = (bf16[128,2176]{1,0:T(8,128)(2,1)}, bf16[128,2176]{1,0:T(8,128)(2,1)S(1)}, u32[]{:S(2)}, u32[]{:S(2)}) collective-permute-start(bf16[128,2176]{1,0:T(8,128)(2,1)} %collective-permute-done.10.refs_2_), channel_id=1, source_target_pairs={{0,2},{2,0},{4,6},{6,4},{8,10},{10,8},{12,14},{14,12},{16,18},{18,... | collective-permute-start | bytes 1671176 | tf_op jit(solution)/shard_map/ppermute | solution.py:17
  174.9 14.7 %collective-permute-start.21 = (bf16[128,2048]{1,0:T(8,128)(2,1)S(1)}, bf16[128,2048]{1,0:T(8,128)(2,1)S(1)}, u32[]{:S(2)}, u32[]{:S(2)}) collective-permute-start(bf16[128,2048]{1,0:T(8,128)(2,1)S(1)} %get-tuple-element.132), channel_id=1, source_target_pairs={{0,24},{2,26},{4,28},{6,30},{8,0},{10,2},{12,4},{14,6},{16,8},{18,... | collective-permute-start | bytes 1572872 | tf_op jit(solution)/shard_map/ppermute | solution.py:22
  175.0 15.7 %collective-permute-start.28 = (bf16[128,2048]{1,0:T(8,128)(2,1)S(1)}, bf16[128,2048]{1,0:T(8,128)(2,1)S(1)}, u32[]{:S(2)}, u32[]{:S(2)}) collective-permute-start(bf16[128,2048]{1,0:T(8,128)(2,1)S(1)} %get-tuple-element.145), channel_id=1, source_target_pairs={{0,2},{2,0},{4,6},{6,4},{8,10},{10,8},{12,14},{14,12},{16,18},{18,... | collective-permute-start | bytes 1572872 | tf_op jit(solution)/shard_map/ppermute | solution.py:17
  176.3 15.6 %collective-permute-start.29 = (bf16[128,2048]{1,0:T(8,128)(2,1)S(1)}, bf16[128,2048]{1,0:T(8,128)(2,1)S(1)}, u32[]{:S(2)}, u32[]{:S(2)}) collective-permute-start(bf16[128,2048]{1,0:T(8,128)(2,1)S(1)} %get-tuple-element.146), channel_id=1, source_target_pairs={{0,4},{2,6},{4,0},{6,2},{8,12},{10,14},{12,8},{14,10},{16,20},{18,... | collective-permute-start | bytes 1572872 | tf_op jit(solution)/shard_map/ppermute | solution.py:17
  189.7 14.9 %collective-permute-start.26 = (bf16[128,2048]{1,0:T(8,128)(2,1)S(1)}, bf16[128,2048]{1,0:T(8,128)(2,1)S(1)}, u32[]{:S(2)}, u32[]{:S(2)}) collective-permute-start(bf16[128,2048]{1,0:T(8,128)(2,1)S(1)} %add_convert_fusion.5), channel_id=1, source_target_pairs={{0,2},{2,0},{4,6},{6,4},{8,10},{10,8},{12,14},{14,12},{16,18},{18,... | collective-permute-start | bytes 1572872 | tf_op jit(solution)/shard_map/ppermute | solution.py:17
  190.4 17.8 %collective-permute-start.18 = (bf16[128,2048]{1,0:T(8,128)(2,1)S(1)}, bf16[128,2048]{1,0:T(8,128)(2,1)S(1)}, u32[]{:S(2)}, u32[]{:S(2)}) collective-permute-start(bf16[128,2048]{1,0:T(8,128)(2,1)S(1)} %get-tuple-element.129), channel_id=1, source_target_pairs={{0,24},{2,26},{4,28},{6,30},{8,0},{10,2},{12,4},{14,6},{16,8},{18,... | collective-permute-start | bytes 1572872 | tf_op jit(solution)/shard_map/ppermute | solution.py:22
  190.6 41.1 %collective-permute-start.24 = (bf16[128,2048]{1,0:T(8,128)(2,1)S(1)}, bf16[128,2048]{1,0:T(8,128)(2,1)S(1)}, u32[]{:S(2)}, u32[]{:S(2)}) collective-permute-start(bf16[128,2048]{1,0:T(8,128)(2,1)S(1)} %get-tuple-element.139), channel_id=1, source_target_pairs={{0,4},{2,6},{4,0},{6,2},{8,12},{10,14},{12,8},{14,10},{16,20},{18,... | collective-permute-start | bytes 1572872 | tf_op jit(solution)/shard_map/ppermute | solution.py:17
  190.7 23.8 %collective-permute-start.25 = (bf16[128,2048]{1,0:T(8,128)(2,1)S(1)}, bf16[128,2048]{1,0:T(8,128)(2,1)S(1)}, u32[]{:S(2)}, u32[]{:S(2)}) collective-permute-start(bf16[128,2048]{1,0:T(8,128)(2,1)S(1)} %get-tuple-element.142), channel_id=1, source_target_pairs={{0,2},{2,0},{4,6},{6,4},{8,10},{10,8},{12,14},{14,12},{16,18},{18,... | collective-permute-start | bytes 1572872 | tf_op jit(solution)/shard_map/ppermute | solution.py:17
  192.2 22.6 %collective-permute-start.30 = (bf16[128,2048]{1,0:T(8,128)(2,1)S(1)}, bf16[128,2048]{1,0:T(8,128)(2,1)S(1)}, u32[]{:S(2)}, u32[]{:S(2)}) collective-permute-start(bf16[128,2048]{1,0:T(8,128)(2,1)S(1)} %add_convert_fusion.3), channel_id=1, source_target_pairs={{0,24},{2,26},{4,28},{6,30},{8,0},{10,2},{12,4},{14,6},{16,8},{18,... | collective-permute-start | bytes 1572872 | tf_op jit(solution)/shard_map/ppermute | solution.py:22
  204.8 14.9 %collective-permute-start.27 = (bf16[128,2048]{1,0:T(8,128)(2,1)S(1)}, bf16[128,2048]{1,0:T(8,128)(2,1)S(1)}, u32[]{:S(2)}, u32[]{:S(2)}) collective-permute-start(bf16[128,2048]{1,0:T(8,128)(2,1)S(1)} %add_convert_fusion.4), channel_id=1, source_target_pairs={{0,4},{2,6},{4,0},{6,2},{8,12},{10,14},{12,8},{14,10},{16,20},{18,... | collective-permute-start | bytes 1572872 | tf_op jit(solution)/shard_map/ppermute | solution.py:17
  208.3 22.7 %collective-permute-start.19 = (bf16[128,2048]{1,0:T(8,128)(2,1)S(1)}, bf16[128,2048]{1,0:T(8,128)(2,1)S(1)}, u32[]{:S(2)}, u32[]{:S(2)}) collective-permute-start(bf16[128,2048]{1,0:T(8,128)(2,1)S(1)} %add_convert_fusion.7), channel_id=1, source_target_pairs={{0,4},{2,6},{4,0},{6,2},{8,12},{10,14},{12,8},{14,10},{16,20},{18,... | collective-permute-start | bytes 1572872 | tf_op jit(solution)/shard_map/ppermute | solution.py:17
  214.5 17.2 %collective-permute-start.23 = (bf16[128,2048]{1,0:T(8,128)(2,1)S(1)}, bf16[128,2048]{1,0:T(8,128)(2,1)S(1)}, u32[]{:S(2)}, u32[]{:S(2)}) collective-permute-start(bf16[128,2048]{1,0:T(8,128)(2,1)S(1)} %get-tuple-element.138), channel_id=1, source_target_pairs={{0,2},{2,0},{4,6},{6,4},{8,10},{10,8},{12,14},{14,12},{16,18},{18,... | collective-permute-start | bytes 1572872 | tf_op jit(solution)/shard_map/ppermute | solution.py:17
  220.0 11.7 %collective-permute-start.31 = (bf16[128,2048]{1,0:T(8,128)(2,1)S(1)}, bf16[128,2048]{1,0:T(8,128)(2,1)S(1)}, u32[]{:S(2)}, u32[]{:S(2)}) collective-permute-start(bf16[128,2048]{1,0:T(8,128)(2,1)S(1)} %add_convert_fusion.2), channel_id=1, source_target_pairs={{0,24},{2,26},{4,28},{6,30},{8,0},{10,2},{12,4},{14,6},{16,8},{18,... | collective-permute-start | bytes 1572872 | tf_op jit(solution)/shard_map/ppermute | solution.py:22
  220.9 17.6 %collective-permute-start.22 = (bf16[128,2048]{1,0:T(8,128)(2,1)S(1)}, bf16[128,2048]{1,0:T(8,128)(2,1)S(1)}, u32[]{:S(2)}, u32[]{:S(2)}) collective-permute-start(bf16[128,2048]{1,0:T(8,128)(2,1)S(1)} %get-tuple-element.136), channel_id=1, source_target_pairs={{0,4},{2,6},{4,0},{6,2},{8,12},{10,14},{12,8},{14,10},{16,20},{18,... | collective-permute-start | bytes 1572872 | tf_op jit(solution)/shard_map/ppermute | solution.py:17
  231.1 9.2 %collective-permute-start.20 = (bf16[128,2048]{1,0:T(8,128)(2,1)S(1)}, bf16[128,2048]{1,0:T(8,128)(2,1)S(1)}, u32[]{:S(2)}, u32[]{:S(2)}) collective-permute-start(bf16[128,2048]{1,0:T(8,128)(2,1)S(1)} %add_convert_fusion.6), channel_id=1, source_target_pairs={{0,2},{2,0},{4,6},{6,4},{8,10},{10,8},{12,14},{14,12},{16,18},{18,... | collective-permute-start | bytes 1572872 | tf_op jit(solution)/shard_map/ppermute | solution.py:17
  (23 other events, 103.6 us)

commit v7 on v6

--- a/solution.py
+++ b/solution.py
@@ -67,16 +67,21 @@
                 hidden[at, pl.ds(start, piece)] = value.astype(jnp.bfloat16)
 
 
-def out_kernel(rows, place, hidden, scale, own, other, *outs):
+def out_kernel(rows, count, place, *refs):
+    hidden, scale = refs[:count], refs[count : 2 * count]
+    own, other = refs[2 * count : 2 * count + 2]
+    outs = refs[2 * count + 2 :]
     core = place[1]
     part = own.shape[1]
-    for side, w in ((0, own), (1, other)):
-        start = pl.multiple_of(jnp.where(side == 0, core, 1 - core) * part, part)
-        for c in range(0, part, 256):
-            value = jnp.dot(hidden[...], w[:, c : c + 256], preferred_element_type=jnp.float32)
-            value = (value * scale[:, :1]).astype(jnp.bfloat16)
-            for q in range(4):
-                outs[q][:, pl.ds(pl.multiple_of(start + c, 256), 256)] = value[q * rows : (q + 1) * rows]
+    for g in range(count):
+        for side, w in ((0, own), (1, other)):
+            start = pl.multiple_of(jnp.where(side == 0, core, 1 - core) * part, part)
+            for c in range(0, part, 256):
+                value = jnp.dot(hidden[g][...], w[:, c : c + 256], preferred_element_type=jnp.float32)
+                value = (value * scale[g][:, :1]).astype(jnp.bfloat16)
+                for q in range(4):
+                    out = outs[4 * g + q]
+                    out[:, pl.ds(pl.multiple_of(start + c, 256), 256)] = value[q * rows : (q + 1) * rows]
 
 
 def local(tokens, route_ids, route_weights, w_gate, w_up, w_down):
@@ -182,25 +187,28 @@
     second = work(range(line - 1, line))
     down_other = swap_cores(after(down, second))
     outs = [None] * line
-    for s in [*range(line - 1, 0, -2), *range(line - 2, -1, -2)]:
-        outs[s] = pl.pallas_call(
-            functools.partial(out_kernel, rows),
-            out_shape=[jax.ShapeDtypeStruct((rows, model), bf16)] * 4,
+    for places in [[line - 1], *[[s, s - 1] for s in range(line - 2, 0, -2)], [0]]:
+        count = len(places)
+        made = pl.pallas_call(
+            functools.partial(out_kernel, rows, count),
+            out_shape=[jax.ShapeDtypeStruct((rows, model), bf16)] * (4 * count),
             grid=(1,),
-            in_specs=[
-                smem_spec,
-                pl.BlockSpec((group, width), lambda i, s=hidden[s][1]: (s, 0)),
-                pl.BlockSpec((group, 128), lambda i, s=scale[s][1]: (s, 0)),
-                pl.BlockSpec((width, part), lambda i: (0, 0)),
-                pl.BlockSpec((width, part), lambda i: (0, 0)),
-            ],
-            out_specs=[pl.BlockSpec((rows, model), lambda i: (0, 0))] * 4,
+            in_specs=[smem_spec]
+            + [pl.BlockSpec((group, width), lambda i, s=hidden[s][1]: (s, 0)) for s in places]
+            + [pl.BlockSpec((group, 128), lambda i, s=scale[s][1]: (s, 0)) for s in places]
+            + [pl.BlockSpec((width, part), lambda i: (0, 0))] * 2,
+            out_specs=[pl.BlockSpec((rows, model), lambda i: (0, 0))] * (4 * count),
             compiler_params=pltpu.CompilerParams(vmem_limit_bytes=32 * 1024 * 1024),
             cost_estimate=pl.CostEstimate(
-                flops=2 * group * model * width, bytes_accessed=6_500_000, transcendentals=0
+                flops=2 * count * group * model * width,
+                bytes_accessed=3_200_000 + 3_200_000 * count,
+                transcendentals=0,
             ),
             name="out",
-        )(place, hidden[s][0], scale[s][0], down, down_other)
+        )(place, *[hidden[s][0] for s in places], *[scale[s][0] for s in places], down, down_other)
+        for i, s in enumerate(places):
+            outs[s] = made[4 * i : 4 * i + 4]
+
     def add(*terms):
         return sum(term.astype(f32) for term in terms).astype(bf16)
 

time: 246 us -> 246 us (level)
    pallas_call x4 -> x3, Pallas kernels: 13.2 us -> 11.6 us  [local(): pl.pallas_call(functools.partial(out_kernel, rows, count), out_shape=[jax...]
  transfers between devices with their start and end apart: 35 -> 35, of which waited for: 23 -> 23; matrix products, arithmetic and copies ran while one was open for 4% -> 4% of each run, Pallas kernels for 13% -> 12%
where the time goes in v7:
time: 246 us; the launch traced here: 242 us
  waiting for transfers between devices  139 us (57%)
  starting transfers between devices  43.8 us (18%)
  Pallas kernels  33.3 us (14%)
  local copies, waits for them, and re-layouts  18.4 us (7%)
  other arithmetic  8.29 us (3%)
    ppermute x23, waiting for transfers between devices, flip(): return lax.ppermute(x, 'expert', [(i, i ^ bit) for i in range(size)])  90.3 us
    ppermute x8, waiting for transfers between devices, turn(): lax.ppermute(x, 'expert', [(i, (i + 4 * by) % size) for i in range(size)])  33.6 us
    pallas_call x2, Pallas kernels, hidden_of(): pl.pallas_call(functools.partial(hidden_kernel, len(gathered), rows, mode...  21.7 us
    ppermute x23, starting transfers between devices, flip(): return lax.ppermute(x, 'expert', [(i, i ^ bit) for i in range(size)])  19.6 us
    all_to_all x2, starting transfers between devices, spread(): return lax.all_to_all(w, 'expert', split_axis=0, concat_axis=0, tiled=True)  13.5 us
    unnamed x40, local copies, waits for them, and re-layouts  13.1 us
    pallas_call x3, Pallas kernels, local(): pl.pallas_call(functools.partial(out_kernel, rows, count), out_shape=[jax...  11.6 us
    all_to_all x2, waiting for transfers between devices, spread(): return lax.all_to_all(w, 'expert', split_axis=0, concat_axis=0, tiled=True)  10.9 us
  transfers between devices with their start and end apart: 35, of which 23 were waited for; matrix products, arithmetic and copies ran while one was open for 4% of the time, Pallas kernels for 12%

profile of v7, /device:TPU:12, one launch (start us, length us, event | category | flops | bytes accessed | tf_op | source)
XLA Modules:
  0.0 242.4 jit_solution(7443429080080626002)
XLA Ops:
  1.0 1.9 fusion.1.refs_0_
  2.9 1.6 collective-permute-start
  8.9 1.9 constant_dynamic-slice_fusion.1
  10.8 2.0 pad_maximum_fusion
  12.9 4.7 %collective-permute-done.refs_4_ = bf16[128,2176]{1,0:T(8,128)(2,1)} collective-permute-done((bf16[128,2176]{1,0:T(8,128)(2,1)}, bf16[128,2176]{1,0:T(8,128)(2,1)}, u32[]{:S(2)}, u32[]{:S(2)}) %collective-permute-start) | collective-permute-done | bytes 557088 | tf_op jit(solution)/shard_map/ppermute | solution.py:22
  22.7 10.5 %collective-permute-done.3.refs_8_ = bf16[128,2176]{1,0:T(8,128)(2,1)S(1)} collective-permute-done((bf16[128,2176]{1,0:T(8,128)(2,1)}, bf16[128,2176]{1,0:T(8,128)(2,1)S(1)}, u32[]{:S(2)}, u32[]{:S(2)}) %collective-permute-start.3) | collective-permute-done | bytes 557088 | tf_op jit(solution)/shard_map/ppermute | solution.py:22
  37.9 9.1 %collective-permute-done.6.refs_0_ = bf16[128,2176]{1,0:T(8,128)(2,1)S(1)} collective-permute-done((bf16[128,2176]{1,0:T(8,128)(2,1)S(1)}, bf16[128,2176]{1,0:T(8,128)(2,1)S(1)}, u32[]{:S(2)}, u32[]{:S(2)}) %collective-permute-start.6) | collective-permute-done | bytes 557088 | tf_op jit(solution)/shard_map/ppermute | solution.py:22
  48.1 7.9 %all-to-all-start = ((bf16[16,128,768]{2,1,0:T(8,128)(2,1)}), bf16[16,128,768]{2,1,0:T(8,128)(2,1)}, u32[]{:S(2)}, u32[]{:S(2)}) async-start(bf16[16,128,768]{2,1,0:T(8,128)(2,1)} %pad_maximum_fusion), calls=%async_computation | async-start | bytes 6291456 | tf_op jit(solution)/shard_map/all_to_all | solution.py:26
  62.7 14.9 %collective-permute-done.13 = bf16[64,2176]{1,0:T(8,128)(2,1)S(1)} collective-permute-done((bf16[64,2176]{1,0:T(8,128)(2,1)S(1)}, bf16[64,2176]{1,0:T(8,128)(2,1)S(1)}, u32[]{:S(2)}, u32[]{:S(2)}) %collective-permute-start.13) | collective-permute-done | bytes 278560 | tf_op jit(solution)/shard_map/ppermute | solution.py:17
  77.6 2.7 %collective-permute-start.9 = (bf16[128,2176]{1,0:T(8,128)(2,1)}, bf16[128,2176]{1,0:T(8,128)(2,1)S(1)}, u32[]{:S(2)}, u32[]{:S(2)}) collective-permute-start(bf16[128,2176]{1,0:T(8,128)(2,1)} %copy-done.9), channel_id=1, source_target_pairs={{0,2},{2,0},{4,6},{6,4},{8,10},{10,8},{12,14},{14,12},{16,18},{18,... | collective-permute-start | bytes 1671176 | tf_op jit(solution)/shard_map/ppermute | solution.py:17
  81.2 19.5 %collective-permute-done.10.refs_2_ = bf16[128,2176]{1,0:T(8,128)(2,1)} collective-permute-done((bf16[128,2176]{1,0:T(8,128)(2,1)}, bf16[128,2176]{1,0:T(8,128)(2,1)}, u32[]{:S(2)}, u32[]{:S(2)}) %collective-permute-start.10) | collective-permute-done | bytes 557088 | tf_op jit(solution)/shard_map/ppermute | solution.py:17
  100.7 12.4 %collective-permute-done.11.refs_3_ = bf16[128,2176]{1,0:T(8,128)(2,1)S(1)} collective-permute-done((bf16[128,2176]{1,0:T(8,128)(2,1)}, bf16[128,2176]{1,0:T(8,128)(2,1)S(1)}, u32[]{:S(2)}, u32[]{:S(2)}) %collective-permute-start.11) | collective-permute-done | bytes 557088 | tf_op jit(solution)/shard_map/ppermute | solution.py:17
  115.6 7.9 %all-to-all-done = bf16[16,128,768]{2,1,0:T(8,128)(2,1)} async-done(((bf16[16,128,768]{2,1,0:T(8,128)(2,1)}), bf16[16,128,768]{2,1,0:T(8,128)(2,1)}, u32[]{:S(2)}, u32[]{:S(2)}) %all-to-all-start) | async-done | bytes 3145760 | tf_op jit(solution)/shard_map/all_to_all | solution.py:26
  123.5 5.6 %all-to-all-start.1 = ((bf16[16,48,1024]{2,1,0:T(8,128)(2,1)}), bf16[16,48,1024]{2,1,0:T(8,128)(2,1)}, u32[]{:S(2)}, u32[]{:S(2)}) async-start(bf16[16,48,1024]{2,1,0:T(8,128)(2,1)} %constant_dynamic-slice_fusion), calls=%async_computation.1 | async-start | bytes 3145728 | tf_op jit(solution)/shard_map/all_to_all | solution.py:26
  135.9 15.1 %hidden.2 = (bf16[1536,768]{1,0:T(8,128)(2,1)}, f32[1536,128]{1,0:T(8,128)}) custom-call(s32[2]{0:T(128)S(1)} %pad_add_fusion.place, bf16[128,2176]{1,0:T(8,128)(2,1)} %fusion.1.refs_0_, bf16[128,2176]{1,0:T(8,128)(2,1)} %collective-permute-done.1.refs_1_, bf16[128,2176]{1,0:T(8,128)(2,1)} %collective-permute-done.2.refs_2_, ...), custom_call_target="tpu_custom_call" | custom-call | flops 9663676416 | bytes 10000000 | tf_op jit(solution)/shard_map/hidden/pallas_call | solution.py:156
  151.0 5.2 %collective-permute-done.16.refs_3_ = bf16[128,2176]{1,0:T(8,128)(2,1)S(1)} collective-permute-done((bf16[128,2176]{1,0:T(8,128)(2,1)}, bf16[128,2176]{1,0:T(8,128)(2,1)S(1)}, u32[]{:S(2)}, u32[]{:S(2)}) %collective-permute-start.16) | collective-permute-done | bytes 557088 | tf_op jit(solution)/shard_map/ppermute | solution.py:17
  156.2 6.6 %hidden.3 = (bf16[512,768]{1,0:T(8,128)(2,1)S(1)}, f32[512,128]{1,0:T(8,128)S(1)}) custom-call(s32[2]{0:T(128)S(1)} %pad_add_fusion.place, bf16[128,2176]{1,0:T(8,128)(2,1)S(1)} %copy-done.10, bf16[128,2176]{1,0:T(8,128)(2,1)S(1)} %copy-done.14, bf16[128,2176]{1,0:T(8,128)(2,1)} %collective-permute-done.10.refs_2_, ...), custom_call_target="tpu_custom_call" | custom-call | flops 3221225472 | bytes 10000000 | tf_op jit(solution)/shard_map/hidden/pallas_call | solution.py:156
  163.7 3.1 %all-to-all-done.1 = bf16[16,48,1024]{2,1,0:T(8,128)(2,1)} async-done(((bf16[16,48,1024]{2,1,0:T(8,128)(2,1)}), bf16[16,48,1024]{2,1,0:T(8,128)(2,1)}, u32[]{:S(2)}, u32[]{:S(2)}) %all-to-all-start.1) | async-done | bytes 1572896 | tf_op jit(solution)/shard_map/all_to_all | solution.py:26
  166.7 3.6 %collective-permute-done.17.refs_3_.refs_5_ = bf16[768,1024]{1,0:T(8,128)(2,1)S(1)} collective-permute-done((bf16[768,1024]{1,0:T(8,128)(2,1)}, bf16[768,1024]{1,0:T(8,128)(2,1)S(1)}, u32[]{:S(2)}, u32[]{:S(2)}) %collective-permute-start.17) | collective-permute-done | bytes 1572896 | tf_op jit(solution)/shard_map/ppermute | solution.py:12
  171.5 3.4 %out.5 = (bf16[128,2048]{1,0:T(8,128)(2,1)S(1)}, bf16[128,2048]{1,0:T(8,128)(2,1)S(1)}, bf16[128,2048]{1,0:T(8,128)(2,1)S(1)}, bf16[128,2048]{1,0:T(8,128)(2,1)S(1)}) custom-call(s32[2]{0:T(128)S(1)} %pad_add_fusion.place, bf16[512,768]{1,0:T(8,128)(2,1)S(1)} %copy-done.18, f32[512,128]{1,0:T(8,128)S(1)} %get-tuple-element.131.refs_1_, ...), custom_call_target="tpu_custom_call" | custom-call | flops 1610612736 | bytes 6400000 | tf_op jit(solution)/shard_map/out/pallas_call | solution.py:192
  176.3 4.9 %out.4 = (bf16[128,2048]{1,0:T(8,128)(2,1)S(1)}, bf16[128,2048]{1,0:T(8,128)(2,1)S(1)}, bf16[128,2048]{1,0:T(8,128)(2,1)S(1)}, bf16[128,2048]{1,0:T(8,128)(2,1)S...) custom-call(s32[2]{0:T(128)S(1)} %pad_add_fusion.place, ...), custom_call_target="tpu_custom_call" | custom-call | flops 3221225472 | bytes 9600000 | tf_op jit(solution)/shard_map/out/pallas_call | solution.py:192
  181.3 8.3 %collective-permute-done.21 = bf16[128,2048]{1,0:T(8,128)(2,1)S(1)} collective-permute-done((bf16[128,2048]{1,0:T(8,128)(2,1)S(1)}, bf16[128,2048]{1,0:T(8,128)(2,1)S(1)}, u32[]{:S(2)}, u32[]{:S(2)}) %collective-permute-start.21) | collective-permute-done | bytes 524320 | tf_op jit(solution)/shard_map/ppermute | solution.py:22
  192.1 4.1 %collective-permute-start.30 = (bf16[128,2048]{1,0:T(8,128)(2,1)S(1)}, bf16[128,2048]{1,0:T(8,128)(2,1)S(1)}, u32[]{:S(2)}, u32[]{:S(2)}) collective-permute-start(bf16[128,2048]{1,0:T(8,128)(2,1)S(1)} %add_convert_fusion.3), channel_id=1, source_target_pairs={{0,24},{2,26},{4,28},{6,30},{8,0},{10,2},{12,4},{14,6},{16,8},{18,... | collective-permute-start | bytes 1572872 | tf_op jit(solution)/shard_map/ppermute | solution.py:22
  196.3 8.3 %collective-permute-done.26 = bf16[128,2048]{1,0:T(8,128)(2,1)S(1)} collective-permute-done((bf16[128,2048]{1,0:T(8,128)(2,1)S(1)}, bf16[128,2048]{1,0:T(8,128)(2,1)S(1)}, u32[]{:S(2)}, u32[]{:S(2)}) %collective-permute-start.26) | collective-permute-done | bytes 524320 | tf_op jit(solution)/shard_map/ppermute | solution.py:17
  204.8 3.3 %out.3 = (bf16[128,2048]{1,0:T(8,128)(2,1)S(1)}, bf16[128,2048]{1,0:T(8,128)(2,1)S(1)}, bf16[128,2048]{1,0:T(8,128)(2,1)S(1)}, bf16[128,2048]{1,0:T(8,128)(2,1)S(1)}) custom-call(s32[2]{0:T(128)S(1)} %pad_add_fusion.place, bf16[1536,768]{1,0:T(8,128)(2,1)S(1)} %copy-done.1, f32[1536,128]{1,0:T(8,128)S(1)} %copy-done.2, ...), custom_call_target="tpu_custom_call" | custom-call | flops 1610612736 | bytes 6400000 | tf_op jit(solution)/shard_map/out/pallas_call | solution.py:192
  208.3 2.1 collective-permute-start.19
  210.3 4.2 %collective-permute-done.25 = bf16[128,2048]{1,0:T(8,128)(2,1)S(1)} collective-permute-done((bf16[128,2048]{1,0:T(8,128)(2,1)S(1)}, bf16[128,2048]{1,0:T(8,128)(2,1)S(1)}, u32[]{:S(2)}, u32[]{:S(2)}) %collective-permute-start.25) | collective-permute-done | bytes 524320 | tf_op jit(solution)/shard_map/ppermute | solution.py:17
  214.8 4.9 %collective-permute-done.27 = bf16[128,2048]{1,0:T(8,128)(2,1)S(1)} collective-permute-done((bf16[128,2048]{1,0:T(8,128)(2,1)S(1)}, bf16[128,2048]{1,0:T(8,128)(2,1)S(1)}, u32[]{:S(2)}, u32[]{:S(2)}) %collective-permute-start.27) | collective-permute-done | bytes 524320 | tf_op jit(solution)/shard_map/ppermute | solution.py:17
  220.9 10.0 %collective-permute-done.19 = bf16[128,2048]{1,0:T(8,128)(2,1)S(1)} collective-permute-done((bf16[128,2048]{1,0:T(8,128)(2,1)S(1)}, bf16[128,2048]{1,0:T(8,128)(2,1)S(1)}, u32[]{:S(2)}, u32[]{:S(2)}) %collective-permute-start.19) | collective-permute-done | bytes 524320 | tf_op jit(solution)/shard_map/ppermute | solution.py:17
  232.1 1.9 collective-permute-start.32
  233.9 4.6 %collective-permute-done.22 = bf16[128,2048]{1,0:T(8,128)(2,1)S(1)} collective-permute-done((bf16[128,2048]{1,0:T(8,128)(2,1)S(1)}, bf16[128,2048]{1,0:T(8,128)(2,1)S(1)}, u32[]{:S(2)}, u32[]{:S(2)}) %collective-permute-start.22) | collective-permute-done | bytes 524320 | tf_op jit(solution)/shard_map/ppermute | solution.py:17
  238.5 1.8 collective-permute-done.20
  (103 shorter events, 44.3 us)
Async XLA Ops:
  2.9 14.7 %collective-permute-start = (bf16[128,2176]{1,0:T(8,128)(2,1)}, bf16[128,2176]{1,0:T(8,128)(2,1)}, u32[]{:S(2)}, u32[]{:S(2)}) collective-permute-start(bf16[128,2176]{1,0:T(8,128)(2,1)} %fusion.1.refs_0_), channel_id=1, source_target_pairs={{0,8},{2,10},{4,12},{6,14},{8,16},{10,18},{12,20},{14,22},{16,24},... | collective-permute-start | bytes 1671176 | tf_op jit(solution)/shard_map/ppermute | solution.py:22
  4.5 14.4 %collective-permute-start.1 = (bf16[128,2176]{1,0:T(8,128)(2,1)}, bf16[128,2176]{1,0:T(8,128)(2,1)}, u32[]{:S(2)}, u32[]{:S(2)}) collective-permute-start(bf16[128,2176]{1,0:T(8,128)(2,1)} %fusion.1.refs_0_), channel_id=1, source_target_pairs={{0,2},{2,0},{4,6},{6,4},{8,10},{10,8},{12,14},{14,12},{16,18},{18,... | collective-permute-start | bytes 1671176 | tf_op jit(solution)/shard_map/ppermute | solution.py:17
  6.0 14.1 %collective-permute-start.2 = (bf16[128,2176]{1,0:T(8,128)(2,1)}, bf16[128,2176]{1,0:T(8,128)(2,1)}, u32[]{:S(2)}, u32[]{:S(2)}) collective-permute-start(bf16[128,2176]{1,0:T(8,128)(2,1)} %fusion.1.refs_0_), channel_id=1, source_target_pairs={{0,4},{2,6},{4,0},{6,2},{8,12},{10,14},{12,8},{14,10},{16,20},{18,... | collective-permute-start | bytes 1671176 | tf_op jit(solution)/shard_map/ppermute | solution.py:17
  20.1 13.1 %collective-permute-start.3 = (bf16[128,2176]{1,0:T(8,128)(2,1)}, bf16[128,2176]{1,0:T(8,128)(2,1)S(1)}, u32[]{:S(2)}, u32[]{:S(2)}) collective-permute-start(bf16[128,2176]{1,0:T(8,128)(2,1)} %collective-permute-done.refs_4_), channel_id=1, source_target_pairs={{0,8},{2,10},{4,12},{6,14},{8,16},{10,18},{12,20},{14,22},{16,24},... | collective-permute-start | bytes 1671176 | tf_op jit(solution)/shard_map/ppermute | solution.py:22
  21.7 12.8 %collective-permute-start.4 = (bf16[128,2176]{1,0:T(8,128)(2,1)}, bf16[128,2176]{1,0:T(8,128)(2,1)S(1)}, u32[]{:S(2)}, u32[]{:S(2)}) collective-permute-start(bf16[128,2176]{1,0:T(8,128)(2,1)} %collective-permute-done.refs_4_), channel_id=1, source_target_pairs={{0,2},{2,0},{4,6},{6,4},{8,10},{10,8},{12,14},{14,12},{16,18},{18,... | collective-permute-start | bytes 1671176 | tf_op jit(solution)/shard_map/ppermute | solution.py:17
  22.2 13.1 %collective-permute-start.5 = (bf16[128,2176]{1,0:T(8,128)(2,1)}, bf16[128,2176]{1,0:T(8,128)(2,1)S(1)}, u32[]{:S(2)}, u32[]{:S(2)}) collective-permute-start(bf16[128,2176]{1,0:T(8,128)(2,1)} %collective-permute-done.refs_4_), channel_id=1, source_target_pairs={{0,4},{2,6},{4,0},{6,2},{8,12},{10,14},{12,8},{14,10},{16,20},{18,... | collective-permute-start | bytes 1671176 | tf_op jit(solution)/shard_map/ppermute | solution.py:17
  35.3 11.7 %collective-permute-start.6 = (bf16[128,2176]{1,0:T(8,128)(2,1)S(1)}, bf16[128,2176]{1,0:T(8,128)(2,1)S(1)}, u32[]{:S(2)}, u32[]{:S(2)}) collective-permute-start(bf16[128,2176]{1,0:T(8,128)(2,1)S(1)} %collective-permute-done.3.refs_8_), channel_id=1, source_target_pairs={{0,8},{2,10},{4,12},{6,14},{8,16},{10,18},{12,20},{14,22},{16,24},... | collective-permute-start | bytes 1671176 | tf_op jit(solution)/shard_map/ppermute | solution.py:22
  35.7 11.7 %collective-permute-start.7 = (bf16[128,2176]{1,0:T(8,128)(2,1)S(1)}, bf16[128,2176]{1,0:T(8,128)(2,1)}, u32[]{:S(2)}, u32[]{:S(2)}) collective-permute-start(bf16[128,2176]{1,0:T(8,128)(2,1)S(1)} %collective-permute-done.3.refs_8_), channel_id=1, source_target_pairs={{0,2},{2,0},{4,6},{6,4},{8,10},{10,8},{12,14},{14,12},{16,18},{18,... | collective-permute-start | bytes 1671176 | tf_op jit(solution)/shard_map/ppermute | solution.py:17
  36.6 11.5 %collective-permute-start.8 = (bf16[128,2176]{1,0:T(8,128)(2,1)S(1)}, bf16[128,2176]{1,0:T(8,128)(2,1)}, u32[]{:S(2)}, u32[]{:S(2)}) collective-permute-start(bf16[128,2176]{1,0:T(8,128)(2,1)S(1)} %collective-permute-done.3.refs_8_), channel_id=1, source_target_pairs={{0,4},{2,6},{4,0},{6,2},{8,12},{10,14},{12,8},{14,10},{16,20},{18,... | collective-permute-start | bytes 1671176 | tf_op jit(solution)/shard_map/ppermute | solution.py:17
  48.1 75.4 %all-to-all-start = ((bf16[16,128,768]{2,1,0:T(8,128)(2,1)}), bf16[16,128,768]{2,1,0:T(8,128)(2,1)}, u32[]{:S(2)}, u32[]{:S(2)}) async-start(bf16[16,128,768]{2,1,0:T(8,128)(2,1)} %pad_maximum_fusion), calls=%async_computation | async-start | bytes 6291456 | tf_op jit(solution)/shard_map/all_to_all | solution.py:26
  57.0 20.6 %collective-permute-start.13 = (bf16[64,2176]{1,0:T(8,128)(2,1)S(1)}, bf16[64,2176]{1,0:T(8,128)(2,1)S(1)}, u32[]{:S(2)}, u32[]{:S(2)}) collective-permute-start(bf16[64,2176]{1,0:T(8,128)(2,1)S(1)} %slice.6), channel_id=1, source_target_pairs={{0,4},{2,6},{4,0},{6,2},{8,12},{10,14},{12,8},{14,10},{16,20},{18,... | collective-permute-start | bytes 835592 | tf_op jit(solution)/shard_map/ppermute | solution.py:17
  58.6 21.7 %collective-permute-start.14 = (bf16[64,2176]{1,0:T(8,128)(2,1)S(1)}, bf16[64,2176]{1,0:T(8,128)(2,1)S(1)}, u32[]{:S(2)}, u32[]{:S(2)}) collective-permute-start(bf16[64,2176]{1,0:T(8,128)(2,1)S(1)} %slice.7), channel_id=1, source_target_pairs={{0,2},{2,0},{4,6},{6,4},{8,10},{10,8},{12,14},{14,12},{16,18},{18,... | collective-permute-start | bytes 835592 | tf_op jit(solution)/shard_map/ppermute | solution.py:17
  60.1 40.5 %collective-permute-start.10 = (bf16[128,2176]{1,0:T(8,128)(2,1)}, bf16[128,2176]{1,0:T(8,128)(2,1)}, u32[]{:S(2)}, u32[]{:S(2)}) collective-permute-start(bf16[128,2176]{1,0:T(8,128)(2,1)} %copy-done.9), channel_id=1, source_target_pairs={{0,4},{2,6},{4,0},{6,2},{8,12},{10,14},{12,8},{14,10},{16,20},{18,... | collective-permute-start | bytes 1671176 | tf_op jit(solution)/shard_map/ppermute | solution.py:17
  61.6 51.5 %collective-permute-start.11 = (bf16[128,2176]{1,0:T(8,128)(2,1)}, bf16[128,2176]{1,0:T(8,128)(2,1)S(1)}, u32[]{:S(2)}, u32[]{:S(2)}) collective-permute-start(bf16[128,2176]{1,0:T(8,128)(2,1)} %collective-permute-done.1.refs_1_), channel_id=1, source_target_pairs={{0,4},{2,6},{4,0},{6,2},{8,12},{10,14},{12,8},{14,10},{16,20},{18,... | collective-permute-start | bytes 1671176 | tf_op jit(solution)/shard_map/ppermute | solution.py:17
  62.2 51.8 %collective-permute-start.12 = (bf16[128,2176]{1,0:T(8,128)(2,1)}, bf16[128,2176]{1,0:T(8,128)(2,1)S(1)}, u32[]{:S(2)}, u32[]{:S(2)}) collective-permute-start(bf16[128,2176]{1,0:T(8,128)(2,1)} %copy-done.7), channel_id=1, source_target_pairs={{0,2},{2,0},{4,6},{6,4},{8,10},{10,8},{12,14},{14,12},{16,18},{18,... | collective-permute-start | bytes 1671176 | tf_op jit(solution)/shard_map/ppermute | solution.py:17
  77.6 37.2 %collective-permute-start.9 = (bf16[128,2176]{1,0:T(8,128)(2,1)}, bf16[128,2176]{1,0:T(8,128)(2,1)S(1)}, u32[]{:S(2)}, u32[]{:S(2)}) collective-permute-start(bf16[128,2176]{1,0:T(8,128)(2,1)} %copy-done.9), channel_id=1, source_target_pairs={{0,2},{2,0},{4,6},{6,4},{8,10},{10,8},{12,14},{14,12},{16,18},{18,... | collective-permute-start | bytes 1671176 | tf_op jit(solution)/shard_map/ppermute | solution.py:17
  123.5 43.2 %all-to-all-start.1 = ((bf16[16,48,1024]{2,1,0:T(8,128)(2,1)}), bf16[16,48,1024]{2,1,0:T(8,128)(2,1)}, u32[]{:S(2)}, u32[]{:S(2)}) async-start(bf16[16,48,1024]{2,1,0:T(8,128)(2,1)} %constant_dynamic-slice_fusion), calls=%async_computation.1 | async-start | bytes 3145728 | tf_op jit(solution)/shard_map/all_to_all | solution.py:26
  129.2 27.0 %collective-permute-start.16 = (bf16[128,2176]{1,0:T(8,128)(2,1)}, bf16[128,2176]{1,0:T(8,128)(2,1)S(1)}, u32[]{:S(2)}, u32[]{:S(2)}) collective-permute-start(bf16[128,2176]{1,0:T(8,128)(2,1)} %collective-permute-done.10.refs_2_), channel_id=1, source_target_pairs={{0,2},{2,0},{4,6},{6,4},{8,10},{10,8},{12,14},{14,12},{16,18},{18,... | collective-permute-start | bytes 1671176 | tf_op jit(solution)/shard_map/ppermute | solution.py:17
  174.9 14.7 %collective-permute-start.21 = (bf16[128,2048]{1,0:T(8,128)(2,1)S(1)}, bf16[128,2048]{1,0:T(8,128)(2,1)S(1)}, u32[]{:S(2)}, u32[]{:S(2)}) collective-permute-start(bf16[128,2048]{1,0:T(8,128)(2,1)S(1)} %get-tuple-element.132), channel_id=1, source_target_pairs={{0,24},{2,26},{4,28},{6,30},{8,0},{10,2},{12,4},{14,6},{16,8},{18,... | collective-permute-start | bytes 1572872 | tf_op jit(solution)/shard_map/ppermute | solution.py:22
  175.0 15.7 %collective-permute-start.28 = (bf16[128,2048]{1,0:T(8,128)(2,1)S(1)}, bf16[128,2048]{1,0:T(8,128)(2,1)S(1)}, u32[]{:S(2)}, u32[]{:S(2)}) collective-permute-start(bf16[128,2048]{1,0:T(8,128)(2,1)S(1)} %get-tuple-element.145), channel_id=1, source_target_pairs={{0,2},{2,0},{4,6},{6,4},{8,10},{10,8},{12,14},{14,12},{16,18},{18,... | collective-permute-start | bytes 1572872 | tf_op jit(solution)/shard_map/ppermute | solution.py:17
  176.3 15.6 %collective-permute-start.29 = (bf16[128,2048]{1,0:T(8,128)(2,1)S(1)}, bf16[128,2048]{1,0:T(8,128)(2,1)S(1)}, u32[]{:S(2)}, u32[]{:S(2)}) collective-permute-start(bf16[128,2048]{1,0:T(8,128)(2,1)S(1)} %get-tuple-element.146), channel_id=1, source_target_pairs={{0,4},{2,6},{4,0},{6,2},{8,12},{10,14},{12,8},{14,10},{16,20},{18,... | collective-permute-start | bytes 1572872 | tf_op jit(solution)/shard_map/ppermute | solution.py:17
  189.7 14.9 %collective-permute-start.26 = (bf16[128,2048]{1,0:T(8,128)(2,1)S(1)}, bf16[128,2048]{1,0:T(8,128)(2,1)S(1)}, u32[]{:S(2)}, u32[]{:S(2)}) collective-permute-start(bf16[128,2048]{1,0:T(8,128)(2,1)S(1)} %add_convert_fusion.5), channel_id=1, source_target_pairs={{0,2},{2,0},{4,6},{6,4},{8,10},{10,8},{12,14},{14,12},{16,18},{18,... | collective-permute-start | bytes 1572872 | tf_op jit(solution)/shard_map/ppermute | solution.py:17
  190.4 17.7 %collective-permute-start.18 = (bf16[128,2048]{1,0:T(8,128)(2,1)S(1)}, bf16[128,2048]{1,0:T(8,128)(2,1)S(1)}, u32[]{:S(2)}, u32[]{:S(2)}) collective-permute-start(bf16[128,2048]{1,0:T(8,128)(2,1)S(1)} %get-tuple-element.129), channel_id=1, source_target_pairs={{0,24},{2,26},{4,28},{6,30},{8,0},{10,2},{12,4},{14,6},{16,8},{18,... | collective-permute-start | bytes 1572872 | tf_op jit(solution)/shard_map/ppermute | solution.py:22
  190.6 41.1 %collective-permute-start.24 = (bf16[128,2048]{1,0:T(8,128)(2,1)S(1)}, bf16[128,2048]{1,0:T(8,128)(2,1)S(1)}, u32[]{:S(2)}, u32[]{:S(2)}) collective-permute-start(bf16[128,2048]{1,0:T(8,128)(2,1)S(1)} %get-tuple-element.139), channel_id=1, source_target_pairs={{0,4},{2,6},{4,0},{6,2},{8,12},{10,14},{12,8},{14,10},{16,20},{18,... | collective-permute-start | bytes 1572872 | tf_op jit(solution)/shard_map/ppermute | solution.py:17
  190.7 23.8 %collective-permute-start.25 = (bf16[128,2048]{1,0:T(8,128)(2,1)S(1)}, bf16[128,2048]{1,0:T(8,128)(2,1)S(1)}, u32[]{:S(2)}, u32[]{:S(2)}) collective-permute-start(bf16[128,2048]{1,0:T(8,128)(2,1)S(1)} %get-tuple-element.142), channel_id=1, source_target_pairs={{0,2},{2,0},{4,6},{6,4},{8,10},{10,8},{12,14},{14,12},{16,18},{18,... | collective-permute-start | bytes 1572872 | tf_op jit(solution)/shard_map/ppermute | solution.py:17
  192.1 22.6 %collective-permute-start.30 = (bf16[128,2048]{1,0:T(8,128)(2,1)S(1)}, bf16[128,2048]{1,0:T(8,128)(2,1)S(1)}, u32[]{:S(2)}, u32[]{:S(2)}) collective-permute-start(bf16[128,2048]{1,0:T(8,128)(2,1)S(1)} %add_convert_fusion.3), channel_id=1, source_target_pairs={{0,24},{2,26},{4,28},{6,30},{8,0},{10,2},{12,4},{14,6},{16,8},{18,... | collective-permute-start | bytes 1572872 | tf_op jit(solution)/shard_map/ppermute | solution.py:22
  204.8 14.9 %collective-permute-start.27 = (bf16[128,2048]{1,0:T(8,128)(2,1)S(1)}, bf16[128,2048]{1,0:T(8,128)(2,1)S(1)}, u32[]{:S(2)}, u32[]{:S(2)}) collective-permute-start(bf16[128,2048]{1,0:T(8,128)(2,1)S(1)} %add_convert_fusion.4), channel_id=1, source_target_pairs={{0,4},{2,6},{4,0},{6,2},{8,12},{10,14},{12,8},{14,10},{16,20},{18,... | collective-permute-start | bytes 1572872 | tf_op jit(solution)/shard_map/ppermute | solution.py:17
  208.3 22.7 %collective-permute-start.19 = (bf16[128,2048]{1,0:T(8,128)(2,1)S(1)}, bf16[128,2048]{1,0:T(8,128)(2,1)S(1)}, u32[]{:S(2)}, u32[]{:S(2)}) collective-permute-start(bf16[128,2048]{1,0:T(8,128)(2,1)S(1)} %add_convert_fusion.7), channel_id=1, source_target_pairs={{0,4},{2,6},{4,0},{6,2},{8,12},{10,14},{12,8},{14,10},{16,20},{18,... | collective-permute-start | bytes 1572872 | tf_op jit(solution)/shard_map/ppermute | solution.py:17
  214.5 17.2 %collective-permute-start.23 = (bf16[128,2048]{1,0:T(8,128)(2,1)S(1)}, bf16[128,2048]{1,0:T(8,128)(2,1)S(1)}, u32[]{:S(2)}, u32[]{:S(2)}) collective-permute-start(bf16[128,2048]{1,0:T(8,128)(2,1)S(1)} %get-tuple-element.138), channel_id=1, source_target_pairs={{0,2},{2,0},{4,6},{6,4},{8,10},{10,8},{12,14},{14,12},{16,18},{18,... | collective-permute-start | bytes 1572872 | tf_op jit(solution)/shard_map/ppermute | solution.py:17
  220.0 11.7 %collective-permute-start.31 = (bf16[128,2048]{1,0:T(8,128)(2,1)S(1)}, bf16[128,2048]{1,0:T(8,128)(2,1)S(1)}, u32[]{:S(2)}, u32[]{:S(2)}) collective-permute-start(bf16[128,2048]{1,0:T(8,128)(2,1)S(1)} %add_convert_fusion.2), channel_id=1, source_target_pairs={{0,24},{2,26},{4,28},{6,30},{8,0},{10,2},{12,4},{14,6},{16,8},{18,... | collective-permute-start | bytes 1572872 | tf_op jit(solution)/shard_map/ppermute | solution.py:22
  220.9 17.6 %collective-permute-start.22 = (bf16[128,2048]{1,0:T(8,128)(2,1)S(1)}, bf16[128,2048]{1,0:T(8,128)(2,1)S(1)}, u32[]{:S(2)}, u32[]{:S(2)}) collective-permute-start(bf16[128,2048]{1,0:T(8,128)(2,1)S(1)} %get-tuple-element.136), channel_id=1, source_target_pairs={{0,4},{2,6},{4,0},{6,2},{8,12},{10,14},{12,8},{14,10},{16,20},{18,... | collective-permute-start | bytes 1572872 | tf_op jit(solution)/shard_map/ppermute | solution.py:17
  231.1 9.2 %collective-permute-start.20 = (bf16[128,2048]{1,0:T(8,128)(2,1)S(1)}, bf16[128,2048]{1,0:T(8,128)(2,1)S(1)}, u32[]{:S(2)}, u32[]{:S(2)}) collective-permute-start(bf16[128,2048]{1,0:T(8,128)(2,1)S(1)} %add_convert_fusion.6), channel_id=1, source_target_pairs={{0,2},{2,0},{4,6},{6,4},{8,10},{10,8},{12,14},{14,12},{16,18},{18,... | collective-permute-start | bytes 1572872 | tf_op jit(solution)/shard_map/ppermute | solution.py:17
  (23 other events, 103.5 us)
